TPU v7x, 32 devices: a whole 2x2x4 slice. The times are simulated.
32 devices in a mesh: slot: 8 (over z, y), row: 2 (over core), col: 2 (over x).
Axes of the slice: x: 2, y: 2, z: 4, core: 2. Of those that a mesh axis runs over, the one named last changes fastest.
Arguments:
- hidden: bfloat16 [8, 32, 4096], P('slot', None, 'row'), may hold values from -20 to 20
- w_query: bfloat16 [4096, 4096], P('row', 'col'), may hold values from -0.09375 to 0.09375
- key_weight: bfloat16 [4096, 1024], P('row', 'col'), may hold values from -0.09375 to 0.09375
- value_weight: bfloat16 [4096, 1024], P('row', 'col'), may hold values from -0.09375 to 0.09375
- w_out: bfloat16 [4096, 4096], P('col', 'row'), may hold values from -0.09375 to 0.09375
- kv_store: bfloat16 [512, 2, 8, 1024], P(('slot', 'row'), None, None, 'col'), may hold values from -250 to 250
- stretch_offset: int32 [512], replicated, may hold values from 0 to 4095
- tile_stretch: int32 [8, 64], replicated, may hold values from 0 to 511, as said below
- slot_count: int32 [8], replicated, may hold values from 40 to 64, as said below
- recomp_pos: int32 [8, 32], P('slot'), may hold values from 0 to 511, as said below
Outputs:
- attn_out: bfloat16 [8, 32, 4096], P('slot', 'col', 'row')
Inputs may be any that keep to these rules, and one draw needn't show every extreme that they name: Within each aligned block of 32 tiles of a slot, every value of tile_stretch // 32 that occurs occurs exactly 2 times, and 16 distinct such values occur. `slot_count`: one slot uses all 64 tiles. `recomp_pos`: entry i of slot s lies in [i * q, (i + 1) * q) with q = slot_count[s] * 8 // 32.
All inputs are finite; a program needn't handle non-finite values.
Results may differ from a plain program's by a relative error of at most 0.018.
The roundings to bfloat16 on the way count: a program that leaves them out, or rounds other values in their place, can miss the bound.
Values may be sent and summed in bfloat16 or wider, within the bound.
No kernel may reach another device: no remote copies, remote signals or barrier semaphores. Data moves between devices by JAX's collectives and lax.ppermute only.
A program may use at most 128 MiB of HBM per device.

v0:
```python
import math

import jax
import jax.numpy as jnp
from jax import lax
from jax.sharding import PartitionSpec as P

HEAD_WIDTH = 128


NEGATIVE = -1e30
ROPE_BASE = 500000.0


def joined(value, axis, join):
    pieces = jax.tree.map(lambda part: lax.all_gather(part, axis), value)
    head = jax.tree.map(lambda part: part[0], pieces)
    tail = jax.tree.map(lambda part: part[1:], pieces)
    running, _ = lax.scan(lambda running, piece: (join(running, piece), None), head, tail)
    return running


def frequencies(head_size):
    freq_index = jnp.arange(head_size // 2, dtype=jnp.float32)
    return ROPE_BASE ** (-2.0 * freq_index / head_size)


def apply_rotation(vectors, angles):
    half_dim = vectors.shape[-1] // 2
    front_half = vectors[..., :half_dim]
    back_half = vectors[..., half_dim:]
    cosine_part = jnp.cos(angles)
    sine_part = jnp.sin(angles)
    return jnp.concatenate(
        [
            front_half * cosine_part - back_half * sine_part,
            back_half * cosine_part + front_half * sine_part,
        ],
        axis=-1,
    )


def combine_partials(first, second):
    peak_score = jnp.maximum(first[0], second[0])
    left_scale = jnp.exp(first[0] - peak_score)
    right_scale = jnp.exp(second[0] - peak_score)
    return (
        peak_score,
        first[1] * left_scale + second[1] * right_scale,
        first[2] * left_scale[..., None] + second[2] * right_scale[..., None],
    )


def on_device(
    hidden,
    w_query,
    key_weight,
    value_weight,
    w_out,
    kv_store,
    stretch_offset,
    tile_stretch,
    slot_count,
    recomp_pos,
):
    slot_total = lax.axis_size("slot")
    row_total = lax.axis_size("row")
    peer_count = slot_total * row_total
    tile_count = kv_store.shape[0]
    stretch_len = kv_store.shape[2]
    key_value_columns = kv_store.shape[3]
    head_size = HEAD_WIDTH
    kv_heads = key_value_columns // head_size
    query_columns = w_query.shape[1]
    q_heads = query_columns // head_size
    queries_per_key_head = q_heads // kv_heads
    capacity = max(2, tile_count // peer_count)
    rsel_rows = hidden.shape[1]
    row_share = rsel_rows // row_total
    slot_index = lax.axis_index("slot")
    row_index = lax.axis_index("row")
    own_index = slot_index * row_total + row_index
    freq_table = frequencies(head_size)
    tile_ids = jnp.arange(tile_stretch.shape[1], dtype=jnp.int32)
    valid_all = (tile_ids[None, :] < slot_count[:, None]).reshape(peer_count, tile_count)
    stretches_all = tile_stretch.reshape(peer_count, tile_count)
    is_mine = jnp.logical_and(stretches_all // tile_count == own_index, valid_all).astype(jnp.int32)
    slot_rank = jnp.cumsum(is_mine, axis=1) - 1
    capacity_ids = jnp.arange(capacity, dtype=jnp.int32)
    select = is_mine[:, None, :] * (slot_rank[:, None, :] == capacity_ids[None, :, None]).astype(
        jnp.int32
    )
    local_ids = jnp.sum(select * (stretches_all % tile_count)[:, None, :], axis=2)
    present = jnp.sum(select, axis=2) > 0
    outgoing = jnp.take(kv_store, local_ids.reshape(-1), axis=0)
    outgoing = jnp.where(
        present.reshape(-1)[:, None, None, None], outgoing, jnp.zeros((), kv_store.dtype)
    )
    outgoing = outgoing.reshape(peer_count, capacity, 2, stretch_len, key_value_columns)
    incoming = lax.all_to_all(outgoing, ("slot", "row"), split_axis=0, concat_axis=0, tiled=True)
    incoming = incoming.reshape(peer_count * capacity, 2, stretch_len, key_value_columns)
    weights = jnp.concatenate([w_query, key_weight, value_weight], axis=1)
    tokens = hidden[0]
    row_block = tokens
    projected_rows = lax.psum_scatter(
        jnp.dot(row_block, weights, preferred_element_type=jnp.float32),
        "row",
        scatter_dimension=0,
        tiled=True,
    )
    positions = recomp_pos[0]
    own_pos = lax.dynamic_slice_in_dim(positions, row_index * row_share, row_share)
    token_angle = own_pos.astype(jnp.float32)[:, None, None] * freq_table
    queries = (
        apply_rotation(
            projected_rows[:, :query_columns].reshape(row_share, q_heads, head_size), token_angle
        )
        .astype(jnp.bfloat16)
        .reshape(row_share, query_columns)
    )
    fresh_keys = (
        apply_rotation(
            projected_rows[:, query_columns : query_columns + key_value_columns].reshape(
                row_share, kv_heads, head_size
            ),
            token_angle,
        )
        .astype(jnp.bfloat16)
        .reshape(row_share, key_value_columns)
    )
    new_values = projected_rows[:, query_columns + key_value_columns :].astype(jnp.bfloat16)
    queries, fresh_keys, new_values = (
        lax.all_gather(queries, "row", axis=0, tiled=True),
        lax.all_gather(fresh_keys, "row", axis=0, tiled=True),
        lax.all_gather(new_values, "row", axis=0, tiled=True),
    )
    base_tile = row_index * tile_count
    my_stretches = lax.dynamic_slice_in_dim(tile_stretch[slot_index], base_tile, tile_count)
    my_count = slot_count[slot_index]
    local_tiles = jnp.arange(tile_count, dtype=jnp.int32)
    my_valid = base_tile + local_tiles < my_count
    owners = my_stretches // tile_count
    earlier = jnp.logical_and(
        owners[None, :] == owners[:, None], local_tiles[None, :] < local_tiles[:, None]
    )
    earlier = jnp.logical_and(earlier, my_valid[None, :])
    my_rank = jnp.sum(earlier.astype(jnp.int32), axis=1)
    landing_slot = jnp.where(my_valid, owners * capacity + jnp.minimum(my_rank, capacity - 1), 0)
    arrived = jnp.take(incoming, landing_slot, axis=0)
    key_shift = (base_tile + local_tiles) * stretch_len - jnp.take(stretch_offset, my_stretches)
    key_angle = key_shift.astype(jnp.float32)[:, None, None, None] * freq_table
    unrotated_keys = (
        arrived[:, 0].astype(jnp.float32).reshape(tile_count, stretch_len, kv_heads, head_size)
    )
    local_keys = tile_count * stretch_len
    joined_keys = (
        apply_rotation(unrotated_keys, key_angle)
        .astype(jnp.bfloat16)
        .reshape(local_keys, key_value_columns)
    )
    joined_values = arrived[:, 1].reshape(local_keys, key_value_columns)
    key_base = base_tile * stretch_len
    landing = positions - key_base
    inside = jnp.logical_and(landing >= 0, landing < local_keys)
    landing = jnp.where(inside, landing, local_keys)
    joined_keys = joined_keys.at[landing].set(fresh_keys, mode="drop")
    joined_values = joined_values.at[landing].set(new_values, mode="drop")
    key_span = min(256, local_keys)
    span_count = local_keys // key_span
    grouped = queries.reshape(rsel_rows, kv_heads, queries_per_key_head, head_size)
    length_limit = my_count * stretch_len
    score_scale = 1.0 / math.sqrt(head_size)

    def attend(carry, span_index):
        running_max, weight_sum, weighted = carry
        span_start = span_index * key_span
        key_block = lax.dynamic_slice_in_dim(joined_keys, span_start, key_span, 0).reshape(
            key_span, kv_heads, head_size
        )
        value_block = lax.dynamic_slice_in_dim(joined_values, span_start, key_span, 0).reshape(
            key_span, kv_heads, head_size
        )
        scores = (
            jnp.einsum("qgjd,kgd->qgjk", grouped, key_block, preferred_element_type=jnp.float32)
            * score_scale
        )
        key_pos = key_base + span_start + jnp.arange(key_span, dtype=jnp.int32)
        allowed = jnp.logical_and(
            key_pos[None, :] <= positions[:, None], key_pos[None, :] < length_limit
        )[:, None, None, :]
        scores = jnp.where(allowed, scores, NEGATIVE)
        peak_score = jnp.maximum(running_max, jnp.max(scores, axis=3))
        probs = jnp.where(allowed, jnp.exp(scores - peak_score[..., None]), 0.0)
        factor = jnp.exp(running_max - peak_score)
        weight_sum = weight_sum * factor + jnp.sum(probs, axis=3)
        weighted = weighted * factor[..., None] + jnp.einsum(
            "qgjk,kgd->qgjd",
            probs.astype(jnp.bfloat16),
            value_block,
            preferred_element_type=jnp.float32,
        )
        return ((peak_score, weight_sum, weighted), None)

    start_max = jnp.full((rsel_rows, kv_heads, queries_per_key_head), NEGATIVE, jnp.float32)
    start_sum = jnp.zeros((rsel_rows, kv_heads, queries_per_key_head), jnp.float32)
    start_weighted = jnp.zeros((rsel_rows, kv_heads, queries_per_key_head, head_size), jnp.float32)
    (running_max, weight_sum, weighted), _ = lax.scan(
        attend, (start_max, start_sum, start_weighted), jnp.arange(span_count, dtype=jnp.int32)
    )
    running_max, weight_sum, weighted = joined(
        (running_max, weight_sum, weighted), "row", combine_partials
    )
    attended = (
        (weighted / weight_sum[..., None]).astype(jnp.bfloat16).reshape(rsel_rows, query_columns)
    )
    row_block = attended
    result = lax.psum_scatter(
        jnp.dot(row_block, w_out, preferred_element_type=jnp.float32).astype(jnp.bfloat16),
        "col",
        scatter_dimension=0,
        tiled=True,
    )
    return result[None]


def solution(mesh):
    return jax.shard_map(
        on_device,
        mesh=mesh,
        in_specs=(
            P("slot", None, "row"),
            P("row", "col"),
            P("row", "col"),
            P("row", "col"),
            P("col", "row"),
            P(("slot", "row"), None, None, "col"),
            P(),
            P(),
            P(),
            P("slot", None),
        ),
        out_specs=P("slot", "col", "row"),
        check_vma=False,
    )
```

profile of v0, /device:TPU:0, one launch (start us, length us, event | category | flops | bytes accessed | tf_op | source)
XLA Modules:
  0.0 77.4 jit_solution(4875667874474167413)
XLA Ops:
  6.5 0.8 %reshape.576 = s32[16,32]{1,0:T(8,128)S(1)} reshape(s32[8,64]{1,0:T(8,128)} %param.19) | data formatting | bytes 4096 | tf_op jit(solution)/shard_map/reshape | solution.py:86
  7.4 0.7 lt.137
  8.2 0.2 reduce_window_sum.11
  8.4 0.1 select_reduce_fusion
  8.7 0.1 reshape.577
  8.8 0.1 copy.62
  8.9 0.1 gt.17
  9.0 0.6 gather_fusion.1
  9.6 0.9 %select_select_fusion = bf16[32,2,8,512]{3,2,1,0:T(8,128)(2,1)} fusion(bf16[32,2,8,512]{3,2,1,0:T(8,128)(2,1)S(1)} %gather_fusion.1, pred[32]{0:T(512)(128)(4,1)S(1)} %compare_and_fusion.2, pred[32]{0:T(512)(128)(4,1)S(1)} %gt.17), kind=kLoop, calls=%fused_computation.18 | loop fusion | flops 524288 | bytes 1048640 | tf_op jit(solution)/shard_map/jit(_where)/select_n | solution.py:96
  10.6 7.4 %all-to-all-start = ((bf16[16,2,2,8,512]{4,3,2,1,0:T(8,128)(2,1)}), bf16[16,2,2,8,512]{4,3,2,1,0:T(8,128)(2,1)S(1)}, u32[]{:S(2)}, u32[]{:S(2)}) async-start(bf16[16,2,2,8,512]{4,3,2,1,0:T(8,128)(2,1)} %bitcast.5), calls=%async_computation | async-start | bytes 1048576 | tf_op jit(solution)/shard_map/all_to_all | solution.py:100
  18.0 6.7 %fusion.6 = f32[32,3072]{1,0:T(8,128)} fusion(bf16[2048,512]{1,0:T(8,128)(2,1)} %param.15, bf16[2048,512]{1,0:T(8,128)(2,1)} %param.14, bf16[2048,2048]{1,0:T(8,128)(2,1)} %param.13, bf16[1,32,2048]{2,1,0:T(8,128)(2,1)} %param.12), kind=kOutput, calls=%fused_computation.11 | convolution fusion | flops 440401920 | bytes 13107200 | tf_op jit(solution)/shard_map/dot_general | solution.py:106
  24.8 0.6 dynamic_slice.29
  25.4 0.7 fusion.39
  26.7 0.8 fusion.36
  27.5 0.7 gather_fusion
  28.2 0.2 convert_reduce_fusion
  28.4 0.7 compare_and_fusion.1
  29.3 0.1 multiply_cosine_fusion.1
  29.4 0.1 multiply_cosine_fusion
  29.6 4.4 %reduce-scatter.3.cloned.1.call-done = f32[16,3072]{1,0:T(8,128)} async-done(((f32[32,3072]{1,0:T(8,128)}), f32[16,3072]{1,0:T(8,128)}) %reduce-scatter.3.cloned.1.call-update) | async-done | bytes 196624 | tf_op jit(solution)/shard_map/reduce_scatter | solution.py:105
  34.0 0.8 slice.82
  34.9 0.9 %slice_bitcast_fusion.2 = f32[2,8,16,128]{3,1,2,0:T(8,128)S(1)} fusion(f32[16,3072]{1,0:T(8,128)} %reduce-scatter.3.cloned.1.call-done), kind=kLoop, calls=%fused_computation.37 | loop fusion | bytes 262144
  35.9 0.1 subtract_convert_fusion.1
  36.0 0.1 pad_maximum_fusion
  36.1 1.9 %all_gather.24 = bf16[32,2048]{1,0:T(8,128)(2,1)S(1)} all-gather(bf16[16,2048]{1,0:T(8,128)(2,1)S(1)} %bitcast.95), channel_id=1, replica_groups=mesh['slot'=8,'row'=2,'col'=2] {'row'}, dimensions={0}, use_global_device_ids=true | all-gather | bytes 196608 | tf_op jit(solution)/shard_map/all_gather | solution.py:133
  38.1 0.8 slice.136
  38.9 1.8 %all_gather.23 = bf16[32,512]{1,0:T(8,128)(2,1)S(1)} all-gather(bf16[16,512]{1,0:T(8,128)(2,1)S(1)} %bitcast.96), channel_id=1, replica_groups=mesh['slot'=8,'row'=2,'col'=2] {'row'}, dimensions={0}, use_global_device_ids=true | all-gather | bytes 49152 | tf_op jit(solution)/shard_map/all_gather | solution.py:134
  40.7 1.8 %all_gather.25 = bf16[32,512]{1,0:T(8,128)(2,1)S(1)} all-gather(bf16[16,512]{1,0:T(8,128)(2,1)S(1)} %slice.136), channel_id=1, replica_groups=mesh['slot'=8,'row'=2,'col'=2] {'row'}, dimensions={0}, use_global_device_ids=true | all-gather | bytes 49152 | tf_op jit(solution)/shard_map/all_gather | solution.py:135
  42.5 0.6 gather_fusion.2
  43.1 0.1 broadcast_select_fusion
  43.3 0.2 subtract_convert_fusion
  43.5 0.1 maximum_bitcast_fusion
  43.7 0.9 %scatter_fusion = bf16[256,512]{1,0:T(8,128)(2,1)S(1)} fusion(bf16[256,512]{1,0:T(8,128)(2,1)S(1)} %maximum_bitcast_fusion, s32[32]{0:T(128)S(1)} %fusion.37, bf16[32,512]{1,0:T(8,128)(2,1)S(1)} %all_gather.23), kind=kCustom, calls=%fused_computation.3 | custom fusion | bytes 98432 | tf_op jit(solution)/shard_map/scatter | solution.py:166
  44.6 0.1 copy.64
  44.7 0.3 fusion.46
  45.1 0.1 copy.69
  45.2 1.9 %all-gather.1 = f32[64,4,4]{2,1,0:T(4,128)S(1)} all-gather(f32[32,4,4]{2,1,0:T(4,128)S(1)} %copy.69), channel_id=3, replica_groups=mesh['slot'=8,'row'=2,'col'=2] {'row'}, dimensions={0}, use_global_device_ids=true | all-gather | bytes 6144 | tf_op jit(solution)/shard_map/all_gather | solution.py:16
  47.1 0.1 copy.79
  47.2 0.1 copy.80
  47.3 0.3 fusion.12
  47.6 1.8 %all_gather.29 = f32[2,32,4,4]{1,3,2,0:T(4,128)S(1)} all-gather(f32[1,32,4,4]{1,3,2,0:T(4,128)S(1)} %get-tuple-element.76), channel_id=1, replica_groups=mesh['slot'=8,'row'=2,'col'=2] {'row'}, dimensions={0}, use_global_device_ids=true | all-gather | bytes 6144 | tf_op jit(solution)/shard_map/all_gather | solution.py:16
  49.4 0.9 %scatter_fusion.1 = bf16[256,512]{1,0:T(8,128)(2,1)S(1)} fusion(bf16[256,512]{1,0:T(8,128)(2,1)S(1)} %get-tuple-element.60, s32[32]{0:T(128)S(1)} %fusion.37, bf16[32,512]{1,0:T(8,128)(2,1)S(1)} %all_gather.25), kind=kCustom, calls=%fused_computation.4 | custom fusion | bytes 98432 | tf_op jit(solution)/shard_map/scatter | solution.py:167
  50.3 0.1 copy.67
  50.4 0.3 fusion.11
  50.7 2.2 %all-gather = f32[64,4,4,128]{3,0,2,1:T(8,128)S(1)} all-gather(f32[32,4,4,128]{3,0,2,1:T(8,128)S(1)} %fusion.11), channel_id=2, replica_groups=mesh['slot'=8,'row'=2,'col'=2] {'row'}, dimensions={0}, use_global_device_ids=true | all-gather | bytes 786432 | tf_op jit(solution)/shard_map/all_gather | solution.py:16
  52.9 0.3 fusion.20
  53.4 5.6 %convolution_convert_fusion = bf16[32,2048]{1,0:T(8,128)(2,1)} fusion(bf16[32,2048]{1,0:T(8,128)(2,1)S(1)} %reshape.648, bf16[2048,2048]{1,0:T(8,128)(2,1)} %param.16), kind=kOutput, calls=%fused_computation.12 | convolution fusion | flops 268500992 | bytes 8650752 | tf_op jit(solution)/shard_map/dot_general | solution.py:218
  59.0 11.6 %reduce-scatter.5.cloned.1.call-done = bf16[16,2048]{1,0:T(8,128)(2,1)} async-done(((bf16[32,2048]{1,0:T(8,128)(2,1)}), bf16[16,2048]{1,0:T(8,128)(2,1)}) %reduce-scatter.5.cloned.1.call-update) | async-done | bytes 65552 | tf_op jit(solution)/shard_map/reduce_scatter | solution.py:217
  (47 shorter events, 1.2 us)
Async XLA Ops:
  6.5 2.5 %copy-start = (bf16[32,2,8,512]{3,2,1,0:T(8,128)(2,1)S(1)}, bf16[32,2,8,512]{3,2,1,0:T(8,128)(2,1)}, u32[]{:S(2)}) copy-start(bf16[32,2,8,512]{3,2,1,0:T(8,128)(2,1)} %param.17) | copy-start | bytes 1572868
  10.6 32.0 %all-to-all-start = ((bf16[16,2,2,8,512]{4,3,2,1,0:T(8,128)(2,1)}), bf16[16,2,2,8,512]{4,3,2,1,0:T(8,128)(2,1)S(1)}, u32[]{:S(2)}, u32[]{:S(2)}) async-start(bf16[16,2,2,8,512]{4,3,2,1,0:T(8,128)(2,1)} %bitcast.5), calls=%async_computation | async-start | bytes 1048576 | tf_op jit(solution)/shard_map/all_to_all | solution.py:100
  17.9 6.8 %copy-start.2 = (s32[8]{0:T(128)S(1)}, s32[8]{0:T(128)}, u32[]{:S(2)}) copy-start(s32[8]{0:T(128)} %param.20) | copy-start | bytes 100
  18.0 9.5 %copy-start.1 = (s32[512]{0:T(512)S(1)}, s32[512]{0:T(512)}, u32[]{:S(2)}) copy-start(s32[512]{0:T(512)} %param.18) | copy-start | bytes 6148
  18.0 11.1 %copy-start.3 = (s32[1,32]{1,0:T(1,128)S(1)}, s32[1,32]{1,0:T(1,128)}, u32[]{:S(2)}) copy-start(s32[1,32]{1,0:T(1,128)} %param.21) | copy-start | bytes 388
  18.0 16.0 %reduce-scatter.3.cloned.1.call-start = ((), (), s32[]{:S(2)}) async-start(), calls=%async_computation.3 | async-start | bytes 589824 | tf_op jit(solution)/shard_map/reduce_scatter | solution.py:105
  24.7 45.8 %reduce-scatter.5.cloned.1.call-start = ((), (), s32[]{:S(2)}) async-start(), calls=%async_computation.4 | async-start | bytes 196608 | tf_op jit(solution)/shard_map/reduce_scatter | solution.py:217
Sparse Core Ops, SparseCore 0:
  24.8 9.0 reduce-scatter.2
  59.1 11.3 reduce-scatter.4
where the time goes:
time: 77.9 us; the launch traced here: 77.4 us
  waiting for transfers between devices  16 us (21%)
  between operations  14.4 us (18%)
  matrix products  12.8 us (16%)
  blocking collectives  11.4 us (15%)
  local copies, waits for them, and re-layouts  9.58 us (12%)
  starting transfers between devices  7.47 us (10%)
  other arithmetic  5.64 us (7%)
    reduce_scatter x1, waiting for transfers between devices, on_device(): lax.psum_scatter(jnp.dot(row_block, w_out, preferred_element_type=jnp.flo...  11.6 us
    all_to_all x1, starting transfers between devices, on_device(): lax.all_to_all(outgoing, ('slot', 'row'), split_axis=0, concat_axis=0, ti...  7.39 us
    dot_general x1, matrix products, on_device(): jnp.dot(row_block, weights, preferred_element_type=jnp.float32)  6.66 us
    all_gather x3, blocking collectives, joined(): pieces = jax.tree.map(lambda part: lax.all_gather(part, axis), value)  5.89 us
    dot_general x1, matrix products, on_device(): jnp.dot(row_block, w_out, preferred_element_type=jnp.float32)  5.57 us
    reduce_scatter x1, waiting for transfers between devices, on_device(): lax.psum_scatter(jnp.dot(row_block, weights, preferred_element_type=jnp.f...  4.41 us
    all_gather x1, blocking collectives, on_device(): lax.all_gather(queries, 'row', axis=0, tiled=True)  1.9 us
    all_gather x1, blocking collectives, on_device(): lax.all_gather(new_values, 'row', axis=0, tiled=True)  1.82 us
  transfers between devices with their start and end apart: 3, of which 2 were waited for; matrix products, arithmetic and copies ran while one was open for 18% of the time, Pallas kernels for 0%

commit v1 on v0

v1 whole, which is shorter than its diff:
```python
import functools
import math

import jax
import jax.numpy as jnp
import numpy as np
from jax import lax
from jax.experimental import pallas as pl
from jax.experimental.pallas import tpu as pltpu
from jax.sharding import PartitionSpec as P

HEAD_WIDTH = 128
NEGATIVE = -1e30
ROPE_BASE = 500000.0
MIB = 1024 * 1024
FAR = 1 << 28
F32 = jnp.float32
BF16 = jnp.bfloat16
VMEM = pl.BlockSpec(memory_space=pltpu.VMEM)
ANY = pl.BlockSpec(memory_space=pl.ANY)
SMEM = pl.BlockSpec(memory_space=pltpu.SMEM)


def iota(shape, dim):
    return lax.broadcasted_iota(jnp.int32, shape, dim)


def divide(value, by):
    if by & (by - 1) == 0:
        shift = by.bit_length() - 1
        return lax.shift_right_logical(value, jnp.full_like(value, shift)), value & (by - 1)
    quotient = jnp.floor((value.astype(F32) + 0.5) * (1.0 / by)).astype(jnp.int32)
    return quotient, value - quotient * by


def earlier_count(flags):
    n = flags.shape[1]
    before = (iota((n, n), 0) < iota((n, n), 1)).astype(BF16)
    return jnp.dot(flags.astype(BF16), before, preferred_element_type=F32)


def pack_kernel(tiles, ranks, stretch_len, stretches_ref, store_ref, out_ref):
    own = lax.axis_index("slot") * lax.axis_size("row") + lax.axis_index("row")
    slots, slot_tiles = stretches_ref.shape
    owner, local = divide(stretches_ref[...], tiles)
    mine = (owner == own).astype(F32)
    rank = earlier_count(mine)
    lane = iota((slots, 128), 1)
    ids = jnp.zeros((slots, 128), F32)
    for k in range(ranks):
        picked = jnp.where(rank == k, mine * local.astype(F32), 0.0)
        ids = jnp.where(lane == k, jnp.sum(picked, axis=1, keepdims=True), ids)
    per_slot = ranks * 2 * stretch_len
    rows = slots * per_slot
    ids = jnp.broadcast_to(ids[:, None, :], (slots, per_slot, 128)).reshape(rows, 128)
    part, token = divide(iota((rows, 128), 0), stretch_len)
    part, rank_of_row = divide(part, ranks)
    kind = part & 1
    stretch = jnp.sum(
        jnp.where(iota((rows, 128), 1) == rank_of_row, ids, 0.0), axis=1, keepdims=True
    ).astype(jnp.int32)
    source = stretch * (2 * stretch_len) + kind[:, :1] * stretch_len + token[:, :1]
    store_rows = tiles * 2 * stretch_len
    pick = (iota((rows, store_rows), 1) == source).astype(F32).astype(BF16)
    out_ref[...] = jnp.dot(pick, store_ref[...], preferred_element_type=F32).astype(BF16)


def project_kernel(step, hidden_ref, wq_ref, wk_ref, wv_ref, out_ref, wq, wk, wv, sems):
    pieces = []
    for source, target in ((wk_ref, wk), (wv_ref, wv), (wq_ref, wq)):
        for start in range(0, source.shape[1], step):
            pieces.append((source, target, start))
    offsets = {id(wq): 0, id(wk): wq_ref.shape[1], id(wv): wq_ref.shape[1] + wk_ref.shape[1]}
    copies = []
    for i, (source, target, start) in enumerate(pieces):
        cols = pl.ds(start, step)
        copy = pltpu.make_async_copy(source.at[:, cols], target.at[:, cols], sems.at[i])
        copy.start()
        copies.append(copy)
    tokens = hidden_ref[...]
    for (source, target, start), copy in zip(pieces, copies):
        copy.wait()
        base = offsets[id(target)] + start
        out_ref[:, base : base + step] = jnp.dot(
            tokens, target[:, start : start + step], preferred_element_type=F32
        )


def angle_tables(shift, freq):
    angle = shift.astype(F32) * freq
    low = iota(angle.shape, 1) < HEAD_WIDTH // 2
    sine = jnp.sin(angle)
    return jnp.cos(angle), jnp.where(low, -sine, sine)


def rotated(vectors, cosine, sine):
    return vectors * cosine + pltpu.roll(vectors, HEAD_WIDTH // 2, 1) * sine


def prepare_kernel(
    tiles,
    ranks,
    stretch_len,
    row_total,
    own_ref,
    other_ref,
    stretches_ref,
    offsets_ref,
    counts_ref,
    positions_ref,
    freq_ref,
    q_ref,
    keys_ref,
    values_ref,
    cos_ref,
    sin_ref,
    bias_ref,
):
    slot = lax.axis_index("slot")
    row = lax.axis_index("row")
    freq = freq_ref[...]
    count = counts_ref[slot]
    arriving = tiles
    slot_tiles = stretches_ref.shape[1]
    stretches = stretches_ref[pl.ds(slot, 1), :]
    owner, _ = divide(stretches, tiles)
    from_slot, rank_wanted = divide(iota((arriving, slot_tiles), 0), ranks)
    match = (owner == from_slot * row_total + row).astype(F32)
    rank = earlier_count(match)
    picked = jnp.where(rank == rank_wanted.astype(F32), match, 0.0)
    tile = jnp.sum(picked * iota((arriving, slot_tiles), 1).astype(F32), axis=1, keepdims=True)
    stretch = jnp.sum(picked * stretches.astype(F32), axis=1, keepdims=True)
    tile = tile.astype(jnp.int32)
    stretch = stretch.astype(jnp.int32)
    page_count = offsets_ref.shape[0]
    page, lane = divide(stretch, 128)
    in_lane = (iota((arriving, 128), 1) == lane).astype(BF16)
    offsets = offsets_ref[...]
    upper, lower = divide(offsets, 64)
    nt = (((1,), (1,)), ((), ()))
    upper = lax.dot_general(in_lane, upper.astype(BF16), nt, preferred_element_type=F32)
    lower = lax.dot_general(in_lane, lower.astype(BF16), nt, preferred_element_type=F32)
    in_page = (iota((arriving, page_count), 1) == page).astype(F32)
    offset = jnp.sum(in_page * (upper * 64.0 + lower), axis=1, keepdims=True).astype(jnp.int32)
    cosine, sine = angle_tables(tile * stretch_len - offset, freq)
    local_keys = arriving * stretch_len
    spread = lambda x: jnp.broadcast_to(
        x[:, None, :], (arriving, stretch_len, x.shape[1])
    ).reshape(local_keys, x.shape[1])
    cos_ref[...] = spread(cosine)
    sin_ref[...] = spread(sine)
    token_total = positions_ref.shape[1]
    share = token_total // row_total
    positions = positions_ref[...]
    group = q_ref.shape[1] // token_total
    query_positions = jnp.concatenate([positions] * group, axis=1)
    wide = jnp.broadcast_to(tile, (arriving, 128))
    _, token = divide(iota((local_keys, 1), 0), stretch_len)
    key_positions = spread(wide)[:, :1] * stretch_len + token
    redone = jnp.sum(
        (key_positions == positions).astype(F32), axis=1, keepdims=True
    )
    usable = jnp.logical_and(key_positions < count * stretch_len, redone == 0.0)
    key_positions = jnp.where(usable, key_positions, FAR)
    bias_ref[:local_keys, :] = jnp.where(key_positions <= query_positions, 0.0, NEGATIVE)
    square = iota((token_total, token_total), 0) == iota((token_total, token_total), 1)
    column = jnp.sum(
        jnp.where(square, positions.astype(F32), 0.0), axis=1, keepdims=True
    ).astype(jnp.int32)
    at_row = lambda x: functools.reduce(
        lambda kept, r: jnp.where(row == r, x[r * share : (r + 1) * share], kept),
        range(1, row_total),
        x[:share],
    )
    new_positions = at_row(column)
    new_usable = new_positions < count * stretch_len
    new_positions = jnp.where(new_usable, new_positions, FAR)
    bias_ref[local_keys:, :] = jnp.where(new_positions <= query_positions, 0.0, NEGATIVE)
    cosine, sine = angle_tables(column, freq)
    key_heads = q_ref.shape[0]
    query_columns = key_heads * group * HEAD_WIDTH
    key_columns = key_heads * HEAD_WIDTH
    for head in range(key_heads * group):
        cols = slice(head * HEAD_WIDTH, (head + 1) * HEAD_WIDTH)
        vectors = own_ref[:, cols] + other_ref[:, cols]
        rows = slice((head % group) * token_total, (head % group + 1) * token_total)
        q_ref[head // group, rows, :] = rotated(vectors, cosine, sine).astype(BF16)
    for head in range(key_heads):
        start = query_columns + head * HEAD_WIDTH
        vectors = own_ref[:, start : start + HEAD_WIDTH] + other_ref[:, start : start + HEAD_WIDTH]
        keys_ref[:, head * HEAD_WIDTH : (head + 1) * HEAD_WIDTH] = at_row(
            rotated(vectors, cosine, sine)
        ).astype(BF16)
    start = query_columns + key_columns
    values_ref[...] = at_row(own_ref[:, start:] + other_ref[:, start:]).astype(BF16)


def attend_kernel(
    stretch_rows, arrived_ref, q_ref, keys_ref, values_ref, cos_ref, sin_ref, bias_ref, out_ref
):
    key_heads = q_ref.shape[0]
    local_keys = cos_ref.shape[0]
    scale = 1.0 / math.sqrt(HEAD_WIDTH)
    cosine = cos_ref[...]
    sine = sin_ref[...]
    bias = bias_ref[...]
    for head in range(key_heads):
        cols = slice(head * HEAD_WIDTH, (head + 1) * HEAD_WIDTH)
        keys = arrived_ref[:, :stretch_rows, cols].reshape(local_keys, HEAD_WIDTH)
        values = arrived_ref[:, stretch_rows:, cols].reshape(local_keys, HEAD_WIDTH)
        keys = rotated(keys.astype(F32), cosine, sine).astype(BF16)
        keys = jnp.concatenate([keys, keys_ref[:, cols]], axis=0)
        values = jnp.concatenate([values, values_ref[:, cols]], axis=0)
        scores = lax.dot_general(
            keys, q_ref[head], (((1,), (1,)), ((), ())), preferred_element_type=F32
        )
        scores = scores * scale + bias
        peak = jnp.max(scores, axis=0, keepdims=True)
        probs = jnp.exp(scores - peak)
        total = jnp.sum(probs, axis=0, keepdims=True)
        out_ref[cols, :] = lax.dot_general(
            values, probs.astype(BF16), (((0,), (0,)), ((), ())), preferred_element_type=F32
        )
        base = key_heads * HEAD_WIDTH
        out_ref[base + head : base + head + 1, :] = peak
        out_ref[base + key_heads + head : base + key_heads + head + 1, :] = total


def output_kernel(step, key_heads, own_ref, other_ref, w_ref, keep_ref, send_ref, w, attended, sems):
    copies = []
    for i, start in enumerate(range(0, w_ref.shape[1], step)):
        cols = pl.ds(start, step)
        copy = pltpu.make_async_copy(w_ref.at[:, cols], w.at[:, cols], sems.at[i])
        copy.start()
        copies.append(copy)
    token_total = attended.shape[0]
    group = own_ref.shape[1] // token_total
    base = key_heads * HEAD_WIDTH
    for head in range(key_heads):
        rows = slice(head * HEAD_WIDTH, (head + 1) * HEAD_WIDTH)
        at_peak = slice(base + head, base + head + 1)
        at_total = slice(base + key_heads + head, base + key_heads + head + 1)
        peak = jnp.maximum(own_ref[at_peak, :], other_ref[at_peak, :])
        own_scale = jnp.exp(own_ref[at_peak, :] - peak)
        other_scale = jnp.exp(other_ref[at_peak, :] - peak)
        total = own_ref[at_total, :] * own_scale + other_ref[at_total, :] * other_scale
        weighted = own_ref[rows, :] * own_scale + other_ref[rows, :] * other_scale
        result = jnp.transpose(weighted / total).astype(BF16)
        for j in range(group):
            start = (head * group + j) * HEAD_WIDTH
            attended[:, start : start + HEAD_WIDTH] = result[
                j * token_total : (j + 1) * token_total
            ]
    tokens = attended[...]
    share = keep_ref.shape[0]
    first = lax.axis_index("col") == 0
    for start, copy in zip(range(0, w_ref.shape[1], step), copies):
        copy.wait()
        cols = slice(start, start + step)
        part = jnp.dot(tokens, w[:, cols], preferred_element_type=F32)
        keep_ref[:, cols] = jnp.where(first, part[:share], part[share:])
        send_ref[:, cols] = jnp.where(first, part[share:], part[:share]).astype(BF16)


def params(mib):
    return pltpu.CompilerParams(vmem_limit_bytes=mib * MIB)


def on_device(
    hidden,
    w_query,
    key_weight,
    value_weight,
    w_out,
    kv_store,
    stretch_offset,
    tile_stretch,
    slot_count,
    recomp_pos,
):
    slot_total = lax.axis_size("slot")
    row_total = lax.axis_size("row")
    tiles, _, stretch_len, key_columns = kv_store.shape
    slot_tiles = tile_stretch.shape[1]
    ranks = slot_tiles // (slot_total * row_total)
    width = hidden.shape[2]
    token_total = hidden.shape[1]
    query_columns = w_query.shape[1]
    key_heads = key_columns // HEAD_WIDTH
    group = query_columns // key_columns
    query_rows = group * token_total
    per_slot = ranks * 2 * stretch_len
    local_keys = tiles * stretch_len
    share = token_total // row_total
    all_keys = local_keys + share
    swap = [(0, 1), (1, 0)]

    freq = np.arange(HEAD_WIDTH // 2, dtype=np.float64)
    freq = (ROPE_BASE ** (-2.0 * freq / HEAD_WIDTH)).astype(np.float32)
    freq = jnp.asarray(np.concatenate([freq, freq])[None, :])

    outgoing = pl.pallas_call(
        functools.partial(pack_kernel, tiles, ranks, stretch_len),
        out_shape=jax.ShapeDtypeStruct((slot_total * per_slot, key_columns), BF16),
        in_specs=[VMEM, VMEM],
        out_specs=VMEM,
        compiler_params=params(32),
        name="pack",
    )(tile_stretch, kv_store.reshape(tiles * 2 * stretch_len, key_columns))
    outgoing = outgoing.reshape(slot_total, per_slot, key_columns)
    arrived = lax.all_to_all(outgoing, "slot", split_axis=0, concat_axis=0, tiled=True)

    step = key_columns
    projected = pl.pallas_call(
        functools.partial(project_kernel, step),
        out_shape=jax.ShapeDtypeStruct((token_total, query_columns + 2 * key_columns), F32),
        in_specs=[VMEM, ANY, ANY, ANY],
        out_specs=VMEM,
        scratch_shapes=[
            pltpu.VMEM((width, query_columns), BF16),
            pltpu.VMEM((width, key_columns), BF16),
            pltpu.VMEM((width, key_columns), BF16),
            pltpu.SemaphoreType.DMA((query_columns // step + 2,)),
        ],
        compiler_params=params(32),
        name="project",
    )(hidden[0], w_query, key_weight, value_weight)
    projected_other = lax.ppermute(projected, "row", swap)

    queries, fresh_keys, new_values, cosine, sine, bias = pl.pallas_call(
        functools.partial(prepare_kernel, tiles, ranks, stretch_len, row_total),
        out_shape=(
            jax.ShapeDtypeStruct((key_heads, query_rows, HEAD_WIDTH), BF16),
            jax.ShapeDtypeStruct((share, key_columns), BF16),
            jax.ShapeDtypeStruct((share, key_columns), BF16),
            jax.ShapeDtypeStruct((local_keys, HEAD_WIDTH), F32),
            jax.ShapeDtypeStruct((local_keys, HEAD_WIDTH), F32),
            jax.ShapeDtypeStruct((all_keys, query_rows), F32),
        ),
        in_specs=[VMEM, VMEM, VMEM, VMEM, SMEM, VMEM, VMEM],
        out_specs=(VMEM,) * 6,
        compiler_params=params(32),
        name="prepare",
    )(
        projected,
        projected_other,
        tile_stretch,
        stretch_offset.reshape(-1, 128),
        slot_count,
        recomp_pos,
        freq,
    )

    partial = pl.pallas_call(
        functools.partial(attend_kernel, ranks * stretch_len),
        out_shape=jax.ShapeDtypeStruct((key_heads * HEAD_WIDTH + 2 * key_heads, query_rows), F32),
        in_specs=[VMEM] * 7,
        out_specs=VMEM,
        compiler_params=params(48),
        name="attend",
    )(arrived, queries, fresh_keys, new_values, cosine, sine, bias)
    partial_other = lax.ppermute(partial, "row", swap)

    out_columns = w_out.shape[1]
    out_share = token_total // lax.axis_size("col")
    keep, send = pl.pallas_call(
        functools.partial(output_kernel, step, key_heads),
        out_shape=(
            jax.ShapeDtypeStruct((out_share, out_columns), F32),
            jax.ShapeDtypeStruct((out_share, out_columns), BF16),
        ),
        in_specs=[VMEM, VMEM, ANY],
        out_specs=(VMEM, VMEM),
        scratch_shapes=[
            pltpu.VMEM(w_out.shape, BF16),
            pltpu.VMEM((token_total, query_columns), BF16),
            pltpu.SemaphoreType.DMA((out_columns // step,)),
        ],
        compiler_params=params(32),
        name="output",
    )(partial, partial_other, w_out)
    received = lax.ppermute(send, "col", swap)
    return (keep + received.astype(F32)).astype(BF16)[None]


def solution(mesh):
    return jax.shard_map(
        on_device,
        mesh=mesh,
        in_specs=(
            P("slot", None, "row"),
            P("row", "col"),
            P("row", "col"),
            P("row", "col"),
            P("col", "row"),
            P(("slot", "row"), None, None, "col"),
            P(),
            P(),
            P(),
            P("slot", None),
        ),
        out_specs=P("slot", "col", "row"),
        check_vma=False,
    )
```

time: 77.9 us -> 41 us (0.53)
  between operations: 14.4 us -> 0.08 us
  matrix products: 12.8 us -> 0 us
  Pallas kernels: 0 us -> 12.2 us
  blocking collectives: 11.4 us -> 0 us
  waiting for transfers between devices: 16 us -> 5.91 us
  other arithmetic: 5.64 us -> 0.65 us
  local copies, waits for them, and re-layouts: 9.58 us -> 12.6 us
  starting transfers between devices: 7.47 us -> 9.1 us
    reduce_scatter x2 -> x0, waiting for transfers between devices: 16 us -> none  [the longest x1 11.6 us: on_device(): lax.psum_scatter(jnp.dot(row_block, w_out, preferred_element_type=jnp.flo...]
    dot_general x4 -> x0, matrix products: 12.8 us -> none  [the longest x1 6.66 us: on_device(): jnp.dot(row_block, weights, preferred_element_type=jnp.float32)]
    pallas_call x0 -> x5, Pallas kernels: none -> 12.2 us  [the longest x1 5.27 us: on_device(): pl.pallas_call(functools.partial(project_kernel, step), out_shape=jax.Sha...]
    unnamed x14 -> x24, local copies, waits for them, and re-layouts: 1.19 us -> 12.6 us
    all_gather x6 -> x0, blocking collectives: 11.4 us -> none  [the longest x3 5.89 us: joined(): pieces = jax.tree.map(lambda part: lax.all_gather(part, axis), value)]
    ppermute x0 -> x3, waiting for transfers between devices: none -> 5.9 us  [the longest x1 2.78 us: on_device(): received = lax.ppermute(send, 'col', swap)]
    scatter x4 -> x0, local copies, waits for them, and re-layouts: 2.05 us -> none  [the longest x2 1.03 us: on_device(): joined_keys = joined_keys.at[landing].set(fresh_keys, mode='drop')]
    gather x3 -> x0, local copies, waits for them, and re-layouts: 1.87 us -> none  [the longest x1 0.71 us: on_device(): jnp.take(stretch_offset, my_stretches)]
  transfers between devices with their start and end apart: 3 -> 4, of which waited for: 2 -> 3; matrix products, arithmetic and copies ran while one was open for 18% -> 0% of each run, Pallas kernels for 0% -> 16%
where the time goes in v1:
time: 41 us; the launch traced here: 40.6 us
  local copies, waits for them, and re-layouts  12.6 us (31%)
  Pallas kernels  12.2 us (30%)
  starting transfers between devices  9.1 us (22%)
  waiting for transfers between devices  5.91 us (14%)
  other arithmetic  0.65 us (2%)
    unnamed x24, local copies, waits for them, and re-layouts  12.6 us
    all_to_all x1, starting transfers between devices, on_device(): lax.all_to_all(outgoing, 'slot', split_axis=0, concat_axis=0, tiled=True)  7.28 us
    pallas_call x1, Pallas kernels, on_device(): pl.pallas_call(functools.partial(project_kernel, step), out_shape=jax.Sha...  5.27 us
    pallas_call x1, Pallas kernels, on_device(): pl.pallas_call(functools.partial(output_kernel, step, key_heads), out_sha...  3.15 us
    ppermute x1, waiting for transfers between devices, on_device(): received = lax.ppermute(send, 'col', swap)  2.78 us
    ppermute x1, waiting for transfers between devices, on_device(): projected_other = lax.ppermute(projected, 'row', swap)  1.71 us
    pallas_call x1, Pallas kernels, on_device(): pl.pallas_call(functools.partial(pack_kernel, tiles, ranks, stretch_len),...  1.56 us
    ppermute x1, starting transfers between devices, on_device(): received = lax.ppermute(send, 'col', swap)  1.55 us
  transfers between devices with their start and end apart: 4, of which 3 were waited for; matrix products, arithmetic and copies ran while one was open for 0% of the time, Pallas kernels for 16%

profile of v1, /device:TPU:0, one launch (start us, length us, event | category | flops | bytes accessed | tf_op | source)
XLA Modules:
  0.0 40.6 jit_solution(12537923206489623875)
XLA Ops:
  0.0 0.0 copy-start.11
  0.0 0.0 copy-start.10
  0.0 0.0 copy-start.9
  0.0 0.0 copy-start.4
  0.0 1.1 %copy-done.4 = bf16[32,2,8,512]{3,2,1,0:T(8,128)(2,1)S(1)} copy-done((bf16[32,2,8,512]{3,2,1,0:T(8,128)(2,1)S(1)}, bf16[32,2,8,512]{3,2,1,0:T(8,128)(2,1)}, u32[]{:S(2)}) %copy-start.4) | copy-done | bytes 524312
  1.1 0.0 copy-start.6
  1.1 0.7 %copy-done.6 = s32[8,64]{1,0:T(8,128)S(1)} copy-done((s32[8,64]{1,0:T(8,128)S(1)}, s32[8,64]{1,0:T(8,128)}, u32[]{:S(2)}) %copy-start.6) | copy-done | bytes 2072
  1.8 0.0 copy-start.7
  1.8 0.0 copy-start.8
  1.8 1.6 %pack.1 = bf16[512,512]{1,0:T(8,128)(2,1)} custom-call(s32[8,64]{1,0:T(8,128)S(1)} %copy-done.6, bf16[512,512]{1,0:T(8,128)(2,1)S(1)} %bitcast.6), custom_call_target="tpu_custom_call" | custom-call | tf_op jit(solution)/shard_map/pack/pallas_call | solution.py:302
  3.3 7.3 %all-to-all-start = ((bf16[8,64,512]{2,1,0:T(8,128)(2,1)}), bf16[8,64,512]{2,1,0:T(8,128)(2,1)S(1)}, u32[]{:S(2)}, u32[]{:S(2)}) async-start(bf16[8,64,512]{2,1,0:T(8,128)(2,1)} %bitcast.1), calls=%async_computation | async-start | bytes 1048576 | tf_op jit(solution)/shard_map/all_to_all | solution.py:311
  10.6 0.0 copy-start.1
  10.6 3.4 %copy-done.1 = bf16[2048,2048]{1,0:T(8,128)(2,1)S(1)} copy-done((bf16[2048,2048]{1,0:T(8,128)(2,1)S(1)}, bf16[2048,2048]{1,0:T(8,128)(2,1)}, u32[]{:S(2)}) %copy-start.1) | copy-done | bytes 8388632
  14.0 0.0 copy-start.2
  14.0 1.6 %copy-done.2 = bf16[2048,512]{1,0:T(8,128)(2,1)S(1)} copy-done((bf16[2048,512]{1,0:T(8,128)(2,1)S(1)}, bf16[2048,512]{1,0:T(8,128)(2,1)}, u32[]{:S(2)}) %copy-start.2) | copy-done | bytes 2097176
  15.6 0.0 copy-start.3
  15.6 1.6 %copy-done.3 = bf16[2048,512]{1,0:T(8,128)(2,1)S(1)} copy-done((bf16[2048,512]{1,0:T(8,128)(2,1)S(1)}, bf16[2048,512]{1,0:T(8,128)(2,1)}, u32[]{:S(2)}) %copy-start.3) | copy-done | bytes 2097176
  17.2 0.0 copy-start.5
  17.2 0.9 %copy-done.5 = bf16[1,32,2048]{2,1,0:T(8,128)(2,1)S(1)} copy-done((bf16[1,32,2048]{2,1,0:T(8,128)(2,1)S(1)}, bf16[1,32,2048]{2,1,0:T(8,128)(2,1)}, u32[]{:S(2)}) %copy-start.5) | copy-done | bytes 131096
  18.1 5.3 %project.1.own_ref = f32[32,3072]{1,0:T(8,128)S(1)} custom-call(bf16[32,2048]{1,0:T(8,128)(2,1)S(1)} %bitcast.7, bf16[2048,2048]{1,0:T(8,128)(2,1)S(1)} %copy-done.1, bf16[2048,512]{1,0:T(8,128)(2,1)S(1)} %copy-done.2, bf16[2048,512]{1,0:T(8,128)(2,1)S(1)} %copy-done.3), custom_call_target="tpu_custom_call" | custom-call | tf_op jit(solution)/shard_map/project/pallas_call | solution.py:314
  23.4 0.1 collective-permute-start
  23.5 1.7 %collective-permute-done.other_ref = f32[32,3072]{1,0:T(8,128)S(1)} collective-permute-done((f32[32,3072]{1,0:T(8,128)S(1)}, f32[32,3072]{1,0:T(8,128)S(1)}, u32[]{:S(2)}, u32[]{:S(2)}) %collective-permute-start) | collective-permute-done | bytes 393248 | tf_op jit(solution)/shard_map/ppermute | solution.py:328
  25.2 0.0 copy-done.11
  25.2 0.0 copy-done.10
  25.2 0.0 copy-done.9
  25.2 0.0 copy-done.7
  25.2 0.0 copy-done.8
  25.2 1.1 %prepare.1 = (bf16[4,128,128]{2,1,0:T(8,128)(2,1)S(1)}, bf16[16,512]{1,0:T(8,128)(2,1)S(1)}, bf16[16,512]{1,0:T(8,128)(2,1)S(1)}, f32[256,128]{1,0:T(8,128)S(1)}...) custom-call(f32[32,3072]{1,0:T(8,128)S(1)} %project.1.own_ref, f32[32,3072]{1,0:T(8,128)S(1)} %collective-permute-done.other_ref, ...), custom_call_target="tpu_custom_call" | custom-call | tf_op jit(solution)/shard_map/prepare/pallas_call | solution.py:330
  26.3 0.0 all-to-all-done.arrived_ref
  26.3 1.2 %attend.1.own_ref = f32[520,128]{1,0:T(8,128)S(1)} custom-call(bf16[8,64,512]{2,1,0:T(8,128)(2,1)S(1)} %all-to-all-done.arrived_ref, bf16[4,128,128]{2,1,0:T(8,128)(2,1)S(1)} %get-tuple-element.13.q_ref, bf16[16,512]{1,0:T(8,128)(2,1)S(1)} %get-tuple-element.14.keys_ref, bf16[16,512]{1,0:T(8,128)(2,1)S(1)} %get-tuple-element.15.values_ref, ...), custom_call_target="tpu_custom_call" | custom-call | tf_op jit(solution)/shard_map/attend/pallas_call | solution.py:354
  27.5 0.2 collective-permute-start.1
  27.7 1.4 %collective-permute-done.1.other_ref = f32[520,128]{1,0:T(8,128)S(1)} collective-permute-done((f32[520,128]{1,0:T(8,128)S(1)}, f32[520,128]{1,0:T(8,128)S(1)}, u32[]{:S(2)}, u32[]{:S(2)}) %collective-permute-start.1) | collective-permute-done | bytes 266272 | tf_op jit(solution)/shard_map/ppermute | solution.py:362
  29.1 0.0 copy-start
  29.1 3.4 %copy-done = bf16[2048,2048]{1,0:T(8,128)(2,1)S(1)} copy-done((bf16[2048,2048]{1,0:T(8,128)(2,1)S(1)}, bf16[2048,2048]{1,0:T(8,128)(2,1)}, u32[]{:S(2)}) %copy-start) | copy-done | bytes 8388632
  32.5 3.1 %output.1 = (f32[16,2048]{1,0:T(8,128)S(1)}, bf16[16,2048]{1,0:T(8,128)(2,1)S(1)}) custom-call(f32[520,128]{1,0:T(8,128)S(1)} %attend.1.own_ref, f32[520,128]{1,0:T(8,128)S(1)} %collective-permute-done.1.other_ref, bf16[2048,2048]{1,0:T(8,128)(2,1)S(1)} %copy-done), custom_call_target="tpu_custom_call" | custom-call | tf_op jit(solution)/shard_map/output/pallas_call | solution.py:366
  35.6 1.6 %collective-permute-start.2 = (bf16[16,2048]{1,0:T(8,128)(2,1)S(1)}, bf16[16,2048]{1,0:T(8,128)(2,1)S(1)}, u32[]{:S(2)}, u32[]{:S(2)}) collective-permute-start(bf16[16,2048]{1,0:T(8,128)(2,1)S(1)} %get-tuple-element.20), channel_id=1, source_target_pairs={{0,1},{1,0},{2,3},{3,2},{4,5},{5,4},{6,7},{7,6},{8,9},{9,8},{10,11... | collective-permute-start | bytes 196616 | tf_op jit(solution)/shard_map/ppermute | solution.py:382
  37.2 2.8 %collective-permute-done.2 = bf16[16,2048]{1,0:T(8,128)(2,1)S(1)} collective-permute-done((bf16[16,2048]{1,0:T(8,128)(2,1)S(1)}, bf16[16,2048]{1,0:T(8,128)(2,1)S(1)}, u32[]{:S(2)}, u32[]{:S(2)}) %collective-permute-start.2) | collective-permute-done | bytes 65568 | tf_op jit(solution)/shard_map/ppermute | solution.py:382
  39.9 0.6 %fusion = bf16[1,16,2048]{2,1,0:T(8,128)(2,1)} fusion(f32[16,2048]{1,0:T(8,128)S(1)} %get-tuple-element.19, bf16[16,2048]{1,0:T(8,128)(2,1)S(1)} %collective-permute-done.2), kind=kLoop, calls=%fused_computation.1 | loop fusion | flops 98304 | bytes 262144 | tf_op jit(solution)/shard_map/broadcast_in_dim | solution.py:383
Async XLA Ops:
  0.0 25.2 %copy-start.11 = (f32[1,128]{1,0:T(1,128)S(1)}, f32[1,128]{1,0:T(1,128)}, u32[]{:S(2)}) copy-start(f32[1,128]{1,0:T(1,128)} %constant.2.clone.freq_ref) | copy-start | bytes 1540
  0.0 25.2 %copy-start.10 = (s32[1,32]{1,0:T(1,128)S(1)}, s32[1,32]{1,0:T(1,128)}, u32[]{:S(2)}) copy-start(s32[1,32]{1,0:T(1,128)} %positions_ref.1) | copy-start | bytes 388
  0.0 25.2 %copy-start.9 = (s32[8]{0:T(128)S(1)}, s32[8]{0:T(128)}, u32[]{:S(2)}) copy-start(s32[8]{0:T(128)} %counts_ref.1) | copy-start | bytes 100
  0.0 1.1 %copy-start.4 = (bf16[32,2,8,512]{3,2,1,0:T(8,128)(2,1)S(1)}, bf16[32,2,8,512]{3,2,1,0:T(8,128)(2,1)}, u32[]{:S(2)}) copy-start(bf16[32,2,8,512]{3,2,1,0:T(8,128)(2,1)} %param.16) | copy-start | bytes 1572868
  1.1 0.7 %copy-start.6 = (s32[8,64]{1,0:T(8,128)S(1)}, s32[8,64]{1,0:T(8,128)}, u32[]{:S(2)}) copy-start(s32[8,64]{1,0:T(8,128)} %stretches_ref.3) | copy-start | bytes 6148
  1.8 23.4 %copy-start.7 = (s32[8,64]{1,0:T(8,128)S(1)}, s32[8,64]{1,0:T(8,128)}, u32[]{:S(2)}) copy-start(s32[8,64]{1,0:T(8,128)} %stretches_ref.3) | copy-start | bytes 6148
  1.8 23.4 %copy-start.8 = (s32[512]{0:T(512)S(1)}, s32[512]{0:T(512)}, u32[]{:S(2)}) copy-start(s32[512]{0:T(512)} %param.17) | copy-start | bytes 6148
  3.3 22.9 %all-to-all-start = ((bf16[8,64,512]{2,1,0:T(8,128)(2,1)}), bf16[8,64,512]{2,1,0:T(8,128)(2,1)S(1)}, u32[]{:S(2)}, u32[]{:S(2)}) async-start(bf16[8,64,512]{2,1,0:T(8,128)(2,1)} %bitcast.1), calls=%async_computation | async-start | bytes 1048576 | tf_op jit(solution)/shard_map/all_to_all | solution.py:311
  10.6 3.4 %copy-start.1 = (bf16[2048,2048]{1,0:T(8,128)(2,1)S(1)}, bf16[2048,2048]{1,0:T(8,128)(2,1)}, u32[]{:S(2)}) copy-start(bf16[2048,2048]{1,0:T(8,128)(2,1)} %wq_ref.1) | copy-start | bytes 25165828
  14.0 1.6 %copy-start.2 = (bf16[2048,512]{1,0:T(8,128)(2,1)S(1)}, bf16[2048,512]{1,0:T(8,128)(2,1)}, u32[]{:S(2)}) copy-start(bf16[2048,512]{1,0:T(8,128)(2,1)} %wk_ref.1) | copy-start | bytes 6291460
  15.6 1.6 %copy-start.3 = (bf16[2048,512]{1,0:T(8,128)(2,1)S(1)}, bf16[2048,512]{1,0:T(8,128)(2,1)}, u32[]{:S(2)}) copy-start(bf16[2048,512]{1,0:T(8,128)(2,1)} %wv_ref.1) | copy-start | bytes 6291460
  17.2 0.9 %copy-start.5 = (bf16[1,32,2048]{2,1,0:T(8,128)(2,1)S(1)}, bf16[1,32,2048]{2,1,0:T(8,128)(2,1)}, u32[]{:S(2)}) copy-start(bf16[1,32,2048]{2,1,0:T(8,128)(2,1)} %param.11) | copy-start | bytes 393220
  23.4 1.8 %collective-permute-start = (f32[32,3072]{1,0:T(8,128)S(1)}, f32[32,3072]{1,0:T(8,128)S(1)}, u32[]{:S(2)}, u32[]{:S(2)}) collective-permute-start(f32[32,3072]{1,0:T(8,128)S(1)} %project.1.own_ref), channel_id=1, source_target_pairs={{0,2},{2,0},{1,3},{3,1},{4,6},{6,4},{5,7},{7,5},{8,10},{10,8},{9,1... | collective-permute-start | bytes 1179656 | tf_op jit(solution)/shard_map/ppermute | solution.py:328
  27.5 1.6 %collective-permute-start.1 = (f32[520,128]{1,0:T(8,128)S(1)}, f32[520,128]{1,0:T(8,128)S(1)}, u32[]{:S(2)}, u32[]{:S(2)}) collective-permute-start(f32[520,128]{1,0:T(8,128)S(1)} %attend.1.own_ref), channel_id=1, source_target_pairs={{0,2},{2,0},{1,3},{3,1},{4,6},{6,4},{5,7},{7,5},{8,10},{10,8},{9,1... | collective-permute-start | bytes 798728 | tf_op jit(solution)/shard_map/ppermute | solution.py:362
  29.1 3.4 %copy-start = (bf16[2048,2048]{1,0:T(8,128)(2,1)S(1)}, bf16[2048,2048]{1,0:T(8,128)(2,1)}, u32[]{:S(2)}) copy-start(bf16[2048,2048]{1,0:T(8,128)(2,1)} %w_ref.1) | copy-start | bytes 25165828
  35.6 4.3 %collective-permute-start.2 = (bf16[16,2048]{1,0:T(8,128)(2,1)S(1)}, bf16[16,2048]{1,0:T(8,128)(2,1)S(1)}, u32[]{:S(2)}, u32[]{:S(2)}) collective-permute-start(bf16[16,2048]{1,0:T(8,128)(2,1)S(1)} %get-tuple-element.20), channel_id=1, source_target_pairs={{0,1},{1,0},{2,3},{3,2},{4,5},{5,4},{6,7},{7,6},{8,9},{9,8},{10,11... | collective-permute-start | bytes 196616 | tf_op jit(solution)/shard_map/ppermute | solution.py:382

commit v2 on v1

v2 whole, which is shorter than its diff:
```python
import functools
import math

import jax
import jax.numpy as jnp
import numpy as np
from jax import lax
from jax.experimental import pallas as pl
from jax.experimental.pallas import tpu as pltpu
from jax.sharding import PartitionSpec as P

HEAD_WIDTH = 128
NEGATIVE = -1e30
ROPE_BASE = 500000.0
MIB = 1024 * 1024
FAR = 1 << 28
F32 = jnp.float32
BF16 = jnp.bfloat16
VMEM = pl.BlockSpec(memory_space=pltpu.VMEM)
ANY = pl.BlockSpec(memory_space=pl.ANY)
HBM = pl.BlockSpec(memory_space=pltpu.HBM)
SMEM = pl.BlockSpec(memory_space=pltpu.SMEM)


def block_bits(place, slots):
    return (slots - place) & (slots - 1)


def iota(shape, dim):
    return lax.broadcasted_iota(jnp.int32, shape, dim)


def divide(value, by):
    if by & (by - 1) == 0:
        shift = by.bit_length() - 1
        return lax.shift_right_logical(value, jnp.full_like(value, shift)), value & (by - 1)
    quotient = jnp.floor((value.astype(F32) + 0.5) * (1.0 / by)).astype(jnp.int32)
    return quotient, value - quotient * by


def earlier_count(flags):
    n = flags.shape[1]
    before = (iota((n, n), 0) < iota((n, n), 1)).astype(BF16)
    return jnp.dot(flags.astype(BF16), before, preferred_element_type=F32)


def pack_kernel(tiles, ranks, stretch_len, stretches_hbm, store_hbm, *refs):
    *outs, stretches_ref, store_ref, ids_ref, sems = refs
    get_store = pltpu.make_async_copy(store_hbm, store_ref, sems.at[0])
    get_stretches = pltpu.make_async_copy(stretches_hbm, stretches_ref, sems.at[1])
    get_stretches.start()
    get_store.start()
    slot = lax.axis_index("slot")
    own = slot * lax.axis_size("row") + lax.axis_index("row")
    slots, slot_tiles = stretches_ref.shape
    per_slot = ranks * 2 * stretch_len
    rows = slots * per_slot
    part, token = divide(iota((rows, 128), 0), stretch_len)
    part, rank_of_row = divide(part, ranks)
    kind = part & 1
    rank_here = iota((rows, 128), 1) == rank_of_row
    within = (kind * stretch_len + token)[:, :1]
    get_stretches.wait()
    owner, local = divide(stretches_ref[...], tiles)
    mine = (owner == own).astype(F32)
    rank = earlier_count(mine)
    lane = iota((slots, 128), 1)
    ids = jnp.zeros((slots, 128), F32)
    for k in range(ranks):
        picked = jnp.where(rank == k, mine * local.astype(F32), 0.0)
        ids = jnp.where(lane == k, jnp.sum(picked, axis=1, keepdims=True), ids)
    ids_ref[...] = ids
    ids = jnp.concatenate(
        [
            jnp.broadcast_to(ids_ref[pl.ds(slot ^ k, 1), :], (per_slot, 128))
            for k in range(slots)
        ],
        axis=0,
    )
    stretch = jnp.sum(jnp.where(rank_here, ids, 0.0), axis=1, keepdims=True).astype(jnp.int32)
    source = stretch * (2 * stretch_len) + within
    store_rows = tiles * 2 * stretch_len
    pick = (iota((rows, store_rows), 1) == source).astype(F32).astype(BF16)
    get_store.wait()
    picked = jnp.dot(pick, store_ref[...], preferred_element_type=F32).astype(BF16)
    for k in range(slots):
        outs[k][...] = picked[k * per_slot : (k + 1) * per_slot]


def fetch(pieces, sems):
    copies = [pltpu.make_async_copy(a, b, sems.at[i]) for i, (a, b) in enumerate(pieces)]
    for copy in copies:
        copy.start()
    return copies


def column_pieces(source, target, step):
    return [
        (source.at[:, pl.ds(start, step)], target.at[:, pl.ds(start, step)])
        for start in range(0, source.shape[1], step)
    ]


def project_kernel(step, hidden_ref, wq_ref, wk_ref, wv_ref, out_ref):
    tokens = hidden_ref[...]
    base = 0
    for weight_ref in (wq_ref, wk_ref, wv_ref):
        for start in range(0, weight_ref.shape[1], step):
            out_ref[:, base : base + step] = jnp.dot(
                tokens, weight_ref[:, start : start + step], preferred_element_type=F32
            )
            base += step


def angle_tables(shift, freq):
    angle = shift.astype(F32) * freq
    low = iota(angle.shape, 1) < HEAD_WIDTH // 2
    sine = jnp.sin(angle)
    return jnp.cos(angle), jnp.where(low, -sine, sine)


def rotated(vectors, cosine, sine):
    return vectors * cosine + pltpu.roll(vectors, HEAD_WIDTH // 2, 1) * sine


def tables_kernel(
    tiles,
    ranks,
    stretch_len,
    row_total,
    stretches_ref,
    offsets_ref,
    counts_ref,
    positions_ref,
    freq_ref,
    cos_ref,
    sin_ref,
    bias_ref,
    token_cos_ref,
    token_sin_ref,
):
    slot = lax.axis_index("slot")
    row = lax.axis_index("row")
    freq = freq_ref[...]
    count = counts_ref[slot]
    arriving = tiles
    slot_tiles = stretches_ref.shape[1]
    stretches = stretches_ref[pl.ds(slot, 1), :]
    owner, _ = divide(stretches, tiles)
    from_slot, rank_wanted = divide(iota((arriving, slot_tiles), 0), ranks)
    from_slot = block_bits(from_slot, arriving // ranks) ^ slot
    match = (owner == from_slot * row_total + row).astype(F32)
    rank = earlier_count(match)
    picked = jnp.where(rank == rank_wanted.astype(F32), match, 0.0)
    tile = jnp.sum(picked * iota((arriving, slot_tiles), 1).astype(F32), axis=1, keepdims=True)
    stretch = jnp.sum(picked * stretches.astype(F32), axis=1, keepdims=True)
    tile = tile.astype(jnp.int32)
    stretch = stretch.astype(jnp.int32)
    page_count = offsets_ref.shape[0]
    page, lane = divide(stretch, 128)
    in_lane = (iota((arriving, 128), 1) == lane).astype(BF16)
    offsets = offsets_ref[...]
    upper, lower = divide(offsets, 64)
    nt = (((1,), (1,)), ((), ()))
    upper = lax.dot_general(in_lane, upper.astype(BF16), nt, preferred_element_type=F32)
    lower = lax.dot_general(in_lane, lower.astype(BF16), nt, preferred_element_type=F32)
    in_page = (iota((arriving, page_count), 1) == page).astype(F32)
    offset = jnp.sum(in_page * (upper * 64.0 + lower), axis=1, keepdims=True).astype(jnp.int32)
    cosine, sine = angle_tables(tile * stretch_len - offset, freq)
    local_keys = arriving * stretch_len
    spread = lambda x: jnp.broadcast_to(
        x[:, None, :], (arriving, stretch_len, x.shape[1])
    ).reshape(local_keys, x.shape[1])
    cos_ref[...] = spread(cosine)
    sin_ref[...] = spread(sine)
    token_total = positions_ref.shape[1]
    share = token_total // row_total
    positions = positions_ref[...]
    group = bias_ref.shape[1] // token_total
    query_positions = jnp.concatenate([positions] * group, axis=1)
    wide = jnp.broadcast_to(tile, (arriving, 128))
    _, token = divide(iota((local_keys, 1), 0), stretch_len)
    key_positions = spread(wide)[:, :1] * stretch_len + token
    redone = jnp.sum(
        (key_positions == positions).astype(F32), axis=1, keepdims=True
    )
    usable = jnp.logical_and(key_positions < count * stretch_len, redone == 0.0)
    key_positions = jnp.where(usable, key_positions, FAR)
    bias_ref[:local_keys, :] = jnp.where(key_positions <= query_positions, 0.0, NEGATIVE)
    square = iota((token_total, token_total), 0) == iota((token_total, token_total), 1)
    column = jnp.sum(
        jnp.where(square, positions.astype(F32), 0.0), axis=1, keepdims=True
    ).astype(jnp.int32)
    new_positions = of_row(column, row, share)
    new_usable = new_positions < count * stretch_len
    new_positions = jnp.where(new_usable, new_positions, FAR)
    bias_ref[local_keys:, :] = jnp.where(new_positions <= query_positions, 0.0, NEGATIVE)
    token_cos_ref[...], token_sin_ref[...] = angle_tables(column, freq)


def of_row(value, row, share):
    kept = value[:share]
    for r in range(1, value.shape[0] // share):
        kept = jnp.where(row == r, value[r * share : (r + 1) * share], kept)
    return kept


def attend_kernel(stretch_rows, *refs):
    *arrived, cos_ref, sin_ref, bias_ref, token_cos_ref, token_sin_ref, both_ref, out_ref = refs
    row = lax.axis_index("row")
    token_total = token_cos_ref.shape[0]
    share = bias_ref.shape[0] - cos_ref.shape[0]
    group = bias_ref.shape[1] // token_total
    key_columns = arrived[0].shape[1]
    key_heads = key_columns // HEAD_WIDTH
    query_columns = group * key_columns
    scale = 1.0 / math.sqrt(HEAD_WIDTH)
    cosine = cos_ref[...]
    sine = sin_ref[...]
    token_cosine = token_cos_ref[...]
    token_sine = token_sin_ref[...]
    bias = bias_ref[...]

    def projected(start):
        cols = slice(start, start + HEAD_WIDTH)
        return both_ref[0, :, cols] + both_ref[1, :, cols]

    for head in range(key_heads):
        at = head * HEAD_WIDTH
        cols = slice(at, at + HEAD_WIDTH)
        queries = jnp.concatenate(
            [
                rotated(projected((head * group + j) * HEAD_WIDTH), token_cosine, token_sine)
                for j in range(group)
            ],
            axis=0,
        ).astype(BF16)
        new_keys = rotated(projected(query_columns + at), token_cosine, token_sine)
        new_values = projected(query_columns + key_columns + at)
        keys = jnp.concatenate([ref[:stretch_rows, cols] for ref in arrived], axis=0)
        keys = rotated(keys.astype(F32), cosine, sine).astype(BF16)
        keys = jnp.concatenate([keys, of_row(new_keys, row, share).astype(BF16)], axis=0)
        values = [ref[stretch_rows:, cols] for ref in arrived]
        values = jnp.concatenate(values + [of_row(new_values, row, share).astype(BF16)], axis=0)
        scores = lax.dot_general(
            keys, queries, (((1,), (1,)), ((), ())), preferred_element_type=F32
        )
        scores = scores * scale + bias
        peak = jnp.max(scores, axis=0, keepdims=True)
        probs = jnp.exp(scores - peak)
        total = jnp.sum(probs, axis=0, keepdims=True)
        out_ref[cols, :] = lax.dot_general(
            values, probs.astype(BF16), (((0,), (0,)), ((), ())), preferred_element_type=F32
        )
        base = key_heads * HEAD_WIDTH
        out_ref[base + head : base + head + 1, :] = peak
        out_ref[base + key_heads + head : base + key_heads + head + 1, :] = total


def output_kernel(step, key_heads, own_ref, other_ref, w_ref, keep_ref, send_ref, attended):
    token_total = attended.shape[0]
    group = own_ref.shape[1] // token_total
    base = key_heads * HEAD_WIDTH
    for head in range(key_heads):
        rows = slice(head * HEAD_WIDTH, (head + 1) * HEAD_WIDTH)
        at_peak = slice(base + head, base + head + 1)
        at_total = slice(base + key_heads + head, base + key_heads + head + 1)
        peak = jnp.maximum(own_ref[at_peak, :], other_ref[at_peak, :])
        own_scale = jnp.exp(own_ref[at_peak, :] - peak)
        other_scale = jnp.exp(other_ref[at_peak, :] - peak)
        total = own_ref[at_total, :] * own_scale + other_ref[at_total, :] * other_scale
        weighted = own_ref[rows, :] * own_scale + other_ref[rows, :] * other_scale
        result = jnp.transpose(weighted / total).astype(BF16)
        for j in range(group):
            start = (head * group + j) * HEAD_WIDTH
            attended[:, start : start + HEAD_WIDTH] = result[
                j * token_total : (j + 1) * token_total
            ]
    tokens = attended[...]
    share = keep_ref.shape[0]
    first = lax.axis_index("col") == 0
    for start in range(0, w_ref.shape[1], step):
        cols = slice(start, start + step)
        part = jnp.dot(tokens, w_ref[:, cols], preferred_element_type=F32)
        keep_ref[:, cols] = jnp.where(first, part[:share], part[share:])
        send_ref[:, cols] = jnp.where(first, part[share:], part[:share]).astype(BF16)


def cost(us):
    return pl.CostEstimate(flops=us * 1_000_000_000, bytes_accessed=1000, transcendentals=0)


def in_hbm(value):
    return pltpu.with_memory_space_constraint(value, pltpu.HBM)


def params(mib):
    return pltpu.CompilerParams(vmem_limit_bytes=mib * MIB)


def on_device(
    hidden,
    w_query,
    key_weight,
    value_weight,
    w_out,
    kv_store,
    stretch_offset,
    tile_stretch,
    slot_count,
    recomp_pos,
):
    slot_total = lax.axis_size("slot")
    row_total = lax.axis_size("row")
    tiles, _, stretch_len, key_columns = kv_store.shape
    slot_tiles = tile_stretch.shape[1]
    ranks = slot_tiles // (slot_total * row_total)
    width = hidden.shape[2]
    token_total = hidden.shape[1]
    query_columns = w_query.shape[1]
    key_heads = key_columns // HEAD_WIDTH
    group = query_columns // key_columns
    query_rows = group * token_total
    per_slot = ranks * 2 * stretch_len
    local_keys = tiles * stretch_len
    share = token_total // row_total
    all_keys = local_keys + share
    swap = [(0, 1), (1, 0)]
    grant = 16 if slot_total <= 8 else 40

    freq = np.arange(HEAD_WIDTH // 2, dtype=np.float64)
    freq = (ROPE_BASE ** (-2.0 * freq / HEAD_WIDTH)).astype(np.float32)
    freq = jnp.asarray(np.concatenate([freq, freq])[None, :])

    store_shape = (tiles * 2 * stretch_len, key_columns)
    outgoing = pl.pallas_call(
        functools.partial(pack_kernel, tiles, ranks, stretch_len),
        out_shape=[jax.ShapeDtypeStruct((per_slot, key_columns), BF16)] * slot_total,
        in_specs=[HBM, HBM],
        out_specs=[VMEM] * slot_total,
        scratch_shapes=[
            pltpu.VMEM(tile_stretch.shape, jnp.int32),
            pltpu.VMEM(store_shape, BF16),
            pltpu.VMEM((slot_total, 128), F32),
            pltpu.SemaphoreType.DMA((2,)),
        ],
        compiler_params=params(grant),
        cost_estimate=cost(8),
        name="pack",
    )(in_hbm(tile_stretch), in_hbm(kv_store.reshape(store_shape)))
    step = key_columns
    order = [block_bits(place, slot_total) for place in range(slot_total)]
    blocks = [outgoing[0]] + [
        lax.ppermute(outgoing[k], "slot", [(i, i ^ k) for i in range(slot_total)])
        for k in order[1:]
    ]

    projected = pl.pallas_call(
        functools.partial(project_kernel, step),
        out_shape=jax.ShapeDtypeStruct((token_total, query_columns + 2 * key_columns), F32),
        in_specs=[VMEM] * 4,
        out_specs=VMEM,
        compiler_params=params(grant),
        cost_estimate=cost(0),
        name="project",
    )(hidden[0], w_query, key_weight, value_weight)
    both = lax.all_gather(projected, "row")

    tables = pl.pallas_call(
        functools.partial(tables_kernel, tiles, ranks, stretch_len, row_total),
        out_shape=(
            jax.ShapeDtypeStruct((local_keys, HEAD_WIDTH), F32),
            jax.ShapeDtypeStruct((local_keys, HEAD_WIDTH), F32),
            jax.ShapeDtypeStruct((all_keys, query_rows), F32),
            jax.ShapeDtypeStruct((token_total, HEAD_WIDTH), F32),
            jax.ShapeDtypeStruct((token_total, HEAD_WIDTH), F32),
        ),
        in_specs=[VMEM, VMEM, SMEM, VMEM, VMEM],
        out_specs=(VMEM,) * 5,
        compiler_params=params(grant),
        cost_estimate=cost(0),
        name="tables",
    )(tile_stretch, stretch_offset.reshape(-1, 128), slot_count, recomp_pos, freq)

    partial = pl.pallas_call(
        functools.partial(attend_kernel, ranks * stretch_len),
        out_shape=jax.ShapeDtypeStruct((key_heads * HEAD_WIDTH + 2 * key_heads, query_rows), F32),
        in_specs=[VMEM] * (slot_total + 6),
        out_specs=VMEM,
        compiler_params=params(grant),
        cost_estimate=cost(8),
        name="attend",
    )(*blocks, *tables, both)
    partial_other = lax.ppermute(partial, "row", swap)

    out_columns = w_out.shape[1]
    out_share = token_total // lax.axis_size("col")
    keep, send = pl.pallas_call(
        functools.partial(output_kernel, step, key_heads),
        out_shape=(
            jax.ShapeDtypeStruct((out_share, out_columns), F32),
            jax.ShapeDtypeStruct((out_share, out_columns), BF16),
        ),
        in_specs=[VMEM, VMEM, VMEM],
        out_specs=(VMEM, VMEM),
        scratch_shapes=[pltpu.VMEM((token_total, query_columns), BF16)],
        compiler_params=params(grant),
        name="output",
    )(partial, partial_other, w_out)
    received = lax.ppermute(send, "col", swap)
    return (keep + received.astype(F32)).astype(BF16)[None]


def solution(mesh):
    return jax.shard_map(
        on_device,
        mesh=mesh,
        in_specs=(
            P("slot", None, "row"),
            P("row", "col"),
            P("row", "col"),
            P("row", "col"),
            P("col", "row"),
            P(("slot", "row"), None, None, "col"),
            P(),
            P(),
            P(),
            P("slot", None),
        ),
        out_specs=P("slot", "col", "row"),
        check_vma=False,
    )
```

time: 41 us -> 30 us (0.73)
  local copies, waits for them, and re-layouts: 12.6 us -> 0.05 us
  starting transfers between devices: 9.1 us -> 14.2 us
  Pallas kernels: 12.2 us -> 7.85 us
  blocking collectives: 0 us -> 2.49 us
  waiting for transfers between devices: 5.91 us -> 4.52 us
    unnamed x24 -> x22, local copies, waits for them, and re-layouts: 12.6 us -> 0.05 us
    ppermute x1 -> x7, starting transfers between devices: 0.07 us -> 12.6 us  [on_device(): lax.ppermute(outgoing[k], 'slot', [(i, i ^ k) for i in range(slot_total)])]
    all_to_all x1 -> x0, starting transfers between devices: 7.28 us -> none  [on_device(): lax.all_to_all(outgoing, 'slot', split_axis=0, concat_axis=0, tiled=True)]
    pallas_call x1, Pallas kernels: 5.27 us -> 2.24 us  [on_device(): pl.pallas_call(functools.partial(project_kernel, step), out_shape=jax.Sha...]
    all_gather x0 -> x1, blocking collectives: none -> 2.49 us  [on_device(): both = lax.all_gather(projected, 'row')]
    pallas_call x1, Pallas kernels: 3.15 us -> 1.64 us  [on_device(): pl.pallas_call(functools.partial(output_kernel, step, key_heads), out_sha...]
    ppermute x1 -> x7, waiting for transfers between devices: 1.71 us -> 0.22 us  [on_device(): lax.ppermute(outgoing[k], 'slot', [(i, i ^ k) for i in range(slot_total)])]
  transfers between devices with their start and end apart: 4 -> 9, of which waited for: 3 -> 3; matrix products, arithmetic and copies ran while one was open for 0% -> 0% of each run, Pallas kernels for 16% -> 11%
where the time goes in v2:
time: 30 us; the launch traced here: 29.9 us
  starting transfers between devices  14.2 us (47%)
  Pallas kernels  7.85 us (26%)
  waiting for transfers between devices  4.52 us (15%)
  blocking collectives  2.49 us (8%)
  other arithmetic  0.64 us (2%)
    ppermute x7, starting transfers between devices, on_device(): lax.ppermute(outgoing[k], 'slot', [(i, i ^ k) for i in range(slot_total)])  12.6 us
    ppermute x1, waiting for transfers between devices, on_device(): received = lax.ppermute(send, 'col', swap)  2.77 us
    all_gather x1, blocking collectives, on_device(): both = lax.all_gather(projected, 'row')  2.49 us
    pallas_call x1, Pallas kernels, on_device(): pl.pallas_call(functools.partial(project_kernel, step), out_shape=jax.Sha...  2.24 us
    pallas_call x1, Pallas kernels, on_device(): pl.pallas_call(functools.partial(pack_kernel, tiles, ranks, stretch_len),...  1.71 us
    pallas_call x1, Pallas kernels, on_device(): pl.pallas_call(functools.partial(output_kernel, step, key_heads), out_sha...  1.64 us
    ppermute x1, waiting for transfers between devices, on_device(): partial_other = lax.ppermute(partial, 'row', swap)  1.53 us
    ppermute x1, starting transfers between devices, on_device(): received = lax.ppermute(send, 'col', swap)  1.51 us
  transfers between devices with their start and end apart: 9, of which 3 were waited for; matrix products, arithmetic and copies ran while one was open for 0% of the time, Pallas kernels for 11%

profile of v2, /device:TPU:0, one launch (start us, length us, event | category | flops | bytes accessed | tf_op | source)
XLA Modules:
  0.0 29.9 jit_solution(7888083693131508831)
XLA Ops:
  0.0 0.0 copy-start
  0.0 0.0 copy-start.1
  0.0 0.0 copy-start.2
  0.0 0.0 copy-start.3
  0.0 1.7 %pack.1 = (bf16[64,512]{1,0:T(8,128)(2,1)S(1)}, bf16[64,512]{1,0:T(8,128)(2,1)S(1)}, bf16[64,512]{1,0:T(8,128)(2,1)S(1)}, bf16[64,512]{1,0:T(8,128)(2,1)S(1)}, b...) custom-call(s32[8,64]{1,0:T(8,128)} %stretches_ref.1, ...), custom_call_target="tpu_custom_call" | custom-call | flops 8000000000 | bytes 1000 | tf_op jit(solution)/shard_map/pack/pallas_call | solution.py:336
  1.7 0.0 copy-start.4
  1.7 0.0 copy-start.5
  1.8 0.0 copy-start.6
  1.8 0.0 copy-start.7
  1.8 0.0 copy-start.8
  1.8 6.1 %collective-permute-start = (bf16[64,512]{1,0:T(8,128)(2,1)S(1)}, bf16[64,512]{1,0:T(8,128)(2,1)S(1)}, u32[]{:S(2)}, u32[]{:S(2)}) collective-permute-start(bf16[64,512]{1,0:T(8,128)(2,1)S(1)} %get-tuple-element.21), channel_id=1, source_target_pairs={{0,28},{4,24},{8,20},{12,16},{16,12},{20,8},{24,4},{28,0},{1,29},{... | collective-permute-start | bytes 196616 | tf_op jit(solution)/shard_map/ppermute | solution.py:354
  7.9 0.2 collective-permute-start.1
  8.1 0.7 %collective-permute-start.2 = (bf16[64,512]{1,0:T(8,128)(2,1)S(1)}, bf16[64,512]{1,0:T(8,128)(2,1)S(1)}, u32[]{:S(2)}, u32[]{:S(2)}) collective-permute-start(bf16[64,512]{1,0:T(8,128)(2,1)S(1)} %get-tuple-element.23), channel_id=1, source_target_pairs={{0,20},{4,16},{8,28},{12,24},{16,4},{20,0},{24,12},{28,8},{1,21},{... | collective-permute-start | bytes 196616 | tf_op jit(solution)/shard_map/ppermute | solution.py:354
  8.8 2.0 %collective-permute-start.3 = (bf16[64,512]{1,0:T(8,128)(2,1)S(1)}, bf16[64,512]{1,0:T(8,128)(2,1)S(1)}, u32[]{:S(2)}, u32[]{:S(2)}) collective-permute-start(bf16[64,512]{1,0:T(8,128)(2,1)S(1)} %get-tuple-element.24), channel_id=1, source_target_pairs={{0,16},{4,20},{8,24},{12,28},{16,0},{20,4},{24,8},{28,12},{1,17},{... | collective-permute-start | bytes 196616 | tf_op jit(solution)/shard_map/ppermute | solution.py:354
  10.9 2.3 %collective-permute-start.4 = (bf16[64,512]{1,0:T(8,128)(2,1)S(1)}, bf16[64,512]{1,0:T(8,128)(2,1)S(1)}, u32[]{:S(2)}, u32[]{:S(2)}) collective-permute-start(bf16[64,512]{1,0:T(8,128)(2,1)S(1)} %get-tuple-element.25), channel_id=1, source_target_pairs={{0,12},{4,8},{8,4},{12,0},{16,28},{20,24},{24,20},{28,16},{1,13},{... | collective-permute-start | bytes 196616 | tf_op jit(solution)/shard_map/ppermute | solution.py:354
  13.2 0.0 copy-done
  13.2 0.0 copy-done.1
  13.2 0.0 copy-done.2
  13.2 0.0 copy-done.3
  13.2 2.2 %project.1 = f32[32,3072]{1,0:T(8,128)S(1)} custom-call(bf16[32,2048]{1,0:T(8,128)(2,1)S(1)} %bitcast.9, bf16[2048,2048]{1,0:T(8,128)(2,1)S(1)} %copy-done, bf16[2048,512]{1,0:T(8,128)(2,1)S(1)} %copy-done.1, bf16[2048,512]{1,0:T(8,128)(2,1)S(1)} %copy-done.2), custom_call_target="tpu_custom_call" | custom-call | bytes 1000 | tf_op jit(solution)/shard_map/project/pallas_call | solution.py:358
  15.4 0.0 collective-permute-done.refs_1_
  15.4 0.8 %collective-permute-start.5 = (bf16[64,512]{1,0:T(8,128)(2,1)S(1)}, bf16[64,512]{1,0:T(8,128)(2,1)S(1)}, u32[]{:S(2)}, u32[]{:S(2)}) collective-permute-start(bf16[64,512]{1,0:T(8,128)(2,1)S(1)} %get-tuple-element.26), channel_id=1, source_target_pairs={{0,8},{4,12},{8,0},{12,4},{16,24},{20,28},{24,16},{28,20},{1,9},{5... | collective-permute-start | bytes 196616 | tf_op jit(solution)/shard_map/ppermute | solution.py:354
  16.2 0.0 collective-permute-done.1.refs_2_
  16.2 0.4 %collective-permute-start.6 = (bf16[64,512]{1,0:T(8,128)(2,1)S(1)}, bf16[64,512]{1,0:T(8,128)(2,1)S(1)}, u32[]{:S(2)}, u32[]{:S(2)}) collective-permute-start(bf16[64,512]{1,0:T(8,128)(2,1)S(1)} %get-tuple-element.27), channel_id=1, source_target_pairs={{0,4},{4,0},{8,12},{12,8},{16,20},{20,16},{24,28},{28,24},{1,5},{5... | collective-permute-start | bytes 196616 | tf_op jit(solution)/shard_map/ppermute | solution.py:354
  16.7 0.0 slice-start
  16.7 2.5 %all-gather = f32[64,3072]{1,0:T(8,128)S(1)} all-gather(f32[32,3072]{1,0:T(8,128)S(1)} %project.1), channel_id=2, replica_groups=mesh['slot'=8,'row'=2,'col'=2] {'row'}, dimensions={0}, use_global_device_ids=true | all-gather | bytes 1179648 | tf_op jit(solution)/shard_map/all_gather | solution.py:367
  19.1 0.0 copy-done.4
  19.1 0.0 copy-done.5
  19.2 0.0 copy-done.6
  19.2 0.0 copy-done.7
  19.2 0.0 copy-done.8
  19.2 1.1 %tables.1 = (f32[256,128]{1,0:T(8,128)S(1)}, f32[256,128]{1,0:T(8,128)S(1)}, f32[272,128]{1,0:T(8,128)S(1)}, f32[32,128]{1,0:T(8,128)S(1)}, f32[32,128]{1,0:T(8,128)S(1)}) custom-call(s32[8,64]{1,0:T(8,128)S(1)} %copy-done.4, s32[4,128]{1,0:T(4,128)S(1)} %bitcast.10, s32[8]{0:T(128)S(1)} %copy-done.6, s32[1,32]{1,0:T(1,128)S(1)} %copy-done.7, ...), custom_call_target="tpu_custom_call" | custom-call | bytes 1000 | tf_op jit(solution)/shard_map/tables/pallas_call | solution.py:369
  20.3 0.0 collective-permute-done.2.refs_3_
  20.3 0.0 collective-permute-done.3.refs_4_
  20.3 0.0 collective-permute-done.4.refs_5_
  20.3 0.0 collective-permute-done.5.refs_6_
  20.3 0.2 collective-permute-done.6.refs_7_
  20.5 0.0 slice-start.1
  20.5 1.2 %attend.1.own_ref = f32[520,128]{1,0:T(8,128)S(1)} custom-call(bf16[64,512]{1,0:T(8,128)(2,1)S(1)} %get-tuple-element.20.refs_0_, bf16[64,512]{1,0:T(8,128)(2,1)S(1)} %collective-permute-done.refs_1_, bf16[64,512]{1,0:T(8,128)(2,1)S(1)} %collective-permute-done.1.refs_2_, bf16[64,512]{1,0:T(8,128)(2,1)S(1)} %collective-permute-done.2.refs_3_, ...), custom_call_target="tpu_custom_call" | custom-call | flops 8000000000 | bytes 1000 | tf_op jit(solution)/shard_map/attend/pallas_call | solution.py:385
  21.7 0.1 collective-permute-start.7
  21.8 1.5 %collective-permute-done.7.other_ref = f32[520,128]{1,0:T(8,128)S(1)} collective-permute-done((f32[520,128]{1,0:T(8,128)S(1)}, f32[520,128]{1,0:T(8,128)S(1)}, u32[]{:S(2)}, u32[]{:S(2)}) %collective-permute-start.7) | collective-permute-done | bytes 266272 | tf_op jit(solution)/shard_map/ppermute | solution.py:394
  23.3 0.0 slice-done
  23.3 0.0 slice-done.1
  23.3 1.6 %output.1 = (f32[16,2048]{1,0:T(8,128)S(1)}, bf16[16,2048]{1,0:T(8,128)(2,1)S(1)}) custom-call(f32[520,128]{1,0:T(8,128)S(1)} %attend.1.own_ref, f32[520,128]{1,0:T(8,128)S(1)} %collective-permute-done.7.other_ref, bf16[2048,2048]{1,0:T(8,128)(2,1)S(1)} %bitcast.7), custom_call_target="tpu_custom_call" | custom-call | tf_op jit(solution)/shard_map/output/pallas_call | solution.py:398
  25.0 1.5 %collective-permute-start.8 = (bf16[16,2048]{1,0:T(8,128)(2,1)S(1)}, bf16[16,2048]{1,0:T(8,128)(2,1)S(1)}, u32[]{:S(2)}, u32[]{:S(2)}) collective-permute-start(bf16[16,2048]{1,0:T(8,128)(2,1)S(1)} %get-tuple-element.34), channel_id=1, source_target_pairs={{0,1},{1,0},{2,3},{3,2},{4,5},{5,4},{6,7},{7,6},{8,9},{9,8},{10,11... | collective-permute-start | bytes 196616 | tf_op jit(solution)/shard_map/ppermute | solution.py:410
  26.5 2.8 %collective-permute-done.8 = bf16[16,2048]{1,0:T(8,128)(2,1)S(1)} collective-permute-done((bf16[16,2048]{1,0:T(8,128)(2,1)S(1)}, bf16[16,2048]{1,0:T(8,128)(2,1)S(1)}, u32[]{:S(2)}, u32[]{:S(2)}) %collective-permute-start.8) | collective-permute-done | bytes 65568 | tf_op jit(solution)/shard_map/ppermute | solution.py:410
  29.2 0.6 %fusion = bf16[1,16,2048]{2,1,0:T(8,128)(2,1)} fusion(f32[16,2048]{1,0:T(8,128)S(1)} %get-tuple-element.33, bf16[16,2048]{1,0:T(8,128)(2,1)S(1)} %collective-permute-done.8), kind=kLoop, calls=%fused_computation.1 | loop fusion | flops 98304 | bytes 262144 | tf_op jit(solution)/shard_map/broadcast_in_dim | solution.py:411
  (1 shorter events, 0.0 us)
Async XLA Ops:
  0.0 13.2 %copy-start = (bf16[2048,2048]{1,0:T(8,128)(2,1)S(1)}, bf16[2048,2048]{1,0:T(8,128)(2,1)}, u32[]{:S(2)}) copy-start(bf16[2048,2048]{1,0:T(8,128)(2,1)} %wq_ref.1) | copy-start | bytes 25165828
  0.0 13.2 %copy-start.1 = (bf16[2048,512]{1,0:T(8,128)(2,1)S(1)}, bf16[2048,512]{1,0:T(8,128)(2,1)}, u32[]{:S(2)}) copy-start(bf16[2048,512]{1,0:T(8,128)(2,1)} %wk_ref.1) | copy-start | bytes 6291460
  0.0 13.2 %copy-start.2 = (bf16[2048,512]{1,0:T(8,128)(2,1)S(1)}, bf16[2048,512]{1,0:T(8,128)(2,1)}, u32[]{:S(2)}) copy-start(bf16[2048,512]{1,0:T(8,128)(2,1)} %wv_ref.1) | copy-start | bytes 6291460
  0.0 13.2 %copy-start.3 = (bf16[1,32,2048]{2,1,0:T(8,128)(2,1)S(1)}, bf16[1,32,2048]{2,1,0:T(8,128)(2,1)}, u32[]{:S(2)}) copy-start(bf16[1,32,2048]{2,1,0:T(8,128)(2,1)} %param.11) | copy-start | bytes 393220
  1.7 17.4 %copy-start.4 = (s32[8,64]{1,0:T(8,128)S(1)}, s32[8,64]{1,0:T(8,128)}, u32[]{:S(2)}) copy-start(s32[8,64]{1,0:T(8,128)} %stretches_ref.1) | copy-start | bytes 6148
  1.7 17.4 %copy-start.5 = (s32[512]{0:T(512)S(1)}, s32[512]{0:T(512)}, u32[]{:S(2)}) copy-start(s32[512]{0:T(512)} %param.17) | copy-start | bytes 6148
  1.8 17.4 %copy-start.6 = (s32[8]{0:T(128)S(1)}, s32[8]{0:T(128)}, u32[]{:S(2)}) copy-start(s32[8]{0:T(128)} %counts_ref.1) | copy-start | bytes 100
  1.8 17.4 %copy-start.7 = (s32[1,32]{1,0:T(1,128)S(1)}, s32[1,32]{1,0:T(1,128)}, u32[]{:S(2)}) copy-start(s32[1,32]{1,0:T(1,128)} %positions_ref.1) | copy-start | bytes 388
  1.8 17.4 %copy-start.8 = (f32[1,128]{1,0:T(1,128)S(1)}, f32[1,128]{1,0:T(1,128)}, u32[]{:S(2)}) copy-start(f32[1,128]{1,0:T(1,128)} %constant.2.clone.freq_ref) | copy-start | bytes 1540
  1.8 13.6 %collective-permute-start = (bf16[64,512]{1,0:T(8,128)(2,1)S(1)}, bf16[64,512]{1,0:T(8,128)(2,1)S(1)}, u32[]{:S(2)}, u32[]{:S(2)}) collective-permute-start(bf16[64,512]{1,0:T(8,128)(2,1)S(1)} %get-tuple-element.21), channel_id=1, source_target_pairs={{0,28},{4,24},{8,20},{12,16},{16,12},{20,8},{24,4},{28,0},{1,29},{... | collective-permute-start | bytes 196616 | tf_op jit(solution)/shard_map/ppermute | solution.py:354
  7.9 8.4 %collective-permute-start.1 = (bf16[64,512]{1,0:T(8,128)(2,1)S(1)}, bf16[64,512]{1,0:T(8,128)(2,1)S(1)}, u32[]{:S(2)}, u32[]{:S(2)}) collective-permute-start(bf16[64,512]{1,0:T(8,128)(2,1)S(1)} %get-tuple-element.22), channel_id=1, source_target_pairs={{0,24},{4,28},{8,16},{12,20},{16,8},{20,12},{24,0},{28,4},{1,25},{... | collective-permute-start | bytes 196616 | tf_op jit(solution)/shard_map/ppermute | solution.py:354
  8.1 12.2 %collective-permute-start.2 = (bf16[64,512]{1,0:T(8,128)(2,1)S(1)}, bf16[64,512]{1,0:T(8,128)(2,1)S(1)}, u32[]{:S(2)}, u32[]{:S(2)}) collective-permute-start(bf16[64,512]{1,0:T(8,128)(2,1)S(1)} %get-tuple-element.23), channel_id=1, source_target_pairs={{0,20},{4,16},{8,28},{12,24},{16,4},{20,0},{24,12},{28,8},{1,21},{... | collective-permute-start | bytes 196616 | tf_op jit(solution)/shard_map/ppermute | solution.py:354
  8.8 11.4 %collective-permute-start.3 = (bf16[64,512]{1,0:T(8,128)(2,1)S(1)}, bf16[64,512]{1,0:T(8,128)(2,1)S(1)}, u32[]{:S(2)}, u32[]{:S(2)}) collective-permute-start(bf16[64,512]{1,0:T(8,128)(2,1)S(1)} %get-tuple-element.24), channel_id=1, source_target_pairs={{0,16},{4,20},{8,24},{12,28},{16,0},{20,4},{24,8},{28,12},{1,17},{... | collective-permute-start | bytes 196616 | tf_op jit(solution)/shard_map/ppermute | solution.py:354
  10.9 9.4 %collective-permute-start.4 = (bf16[64,512]{1,0:T(8,128)(2,1)S(1)}, bf16[64,512]{1,0:T(8,128)(2,1)S(1)}, u32[]{:S(2)}, u32[]{:S(2)}) collective-permute-start(bf16[64,512]{1,0:T(8,128)(2,1)S(1)} %get-tuple-element.25), channel_id=1, source_target_pairs={{0,12},{4,8},{8,4},{12,0},{16,28},{20,24},{24,20},{28,16},{1,13},{... | collective-permute-start | bytes 196616 | tf_op jit(solution)/shard_map/ppermute | solution.py:354
  15.4 4.9 %collective-permute-start.5 = (bf16[64,512]{1,0:T(8,128)(2,1)S(1)}, bf16[64,512]{1,0:T(8,128)(2,1)S(1)}, u32[]{:S(2)}, u32[]{:S(2)}) collective-permute-start(bf16[64,512]{1,0:T(8,128)(2,1)S(1)} %get-tuple-element.26), channel_id=1, source_target_pairs={{0,8},{4,12},{8,0},{12,4},{16,24},{20,28},{24,16},{28,20},{1,9},{5... | collective-permute-start | bytes 196616 | tf_op jit(solution)/shard_map/ppermute | solution.py:354
  16.2 4.3 %collective-permute-start.6 = (bf16[64,512]{1,0:T(8,128)(2,1)S(1)}, bf16[64,512]{1,0:T(8,128)(2,1)S(1)}, u32[]{:S(2)}, u32[]{:S(2)}) collective-permute-start(bf16[64,512]{1,0:T(8,128)(2,1)S(1)} %get-tuple-element.27), channel_id=1, source_target_pairs={{0,4},{4,0},{8,12},{12,8},{16,20},{20,16},{24,28},{28,24},{1,5},{5... | collective-permute-start | bytes 196616 | tf_op jit(solution)/shard_map/ppermute | solution.py:354
  16.7 6.7 %slice-start = ((s8[8388608]{0:T(1024)(128)(4,1)}), s8[4194304]{0:T(1024)(128)(4,1)S(1)}, s32[]{:S(2)}) async-start(s8[8388608]{0:T(1024)(128)(4,1)} %bitcast.6), calls=%async_computation | async-start | bytes 8388608
  20.5 2.8 %slice-start.1 = ((s8[8388608]{0:T(1024)(128)(4,1)}), s8[4194304]{0:T(1024)(128)(4,1)S(1)}, s32[]{:S(2)}) async-start(s8[8388608]{0:T(1024)(128)(4,1)} %bitcast.6), calls=%async_computation.1 | async-start | bytes 8388608
  21.7 1.6 %collective-permute-start.7 = (f32[520,128]{1,0:T(8,128)S(1)}, f32[520,128]{1,0:T(8,128)S(1)}, u32[]{:S(2)}, u32[]{:S(2)}) collective-permute-start(f32[520,128]{1,0:T(8,128)S(1)} %attend.1.own_ref), channel_id=1, source_target_pairs={{0,2},{2,0},{1,3},{3,1},{4,6},{6,4},{5,7},{7,5},{8,10},{10,8},{9,1... | collective-permute-start | bytes 798728 | tf_op jit(solution)/shard_map/ppermute | solution.py:394
  25.0 4.3 %collective-permute-start.8 = (bf16[16,2048]{1,0:T(8,128)(2,1)S(1)}, bf16[16,2048]{1,0:T(8,128)(2,1)S(1)}, u32[]{:S(2)}, u32[]{:S(2)}) collective-permute-start(bf16[16,2048]{1,0:T(8,128)(2,1)S(1)} %get-tuple-element.34), channel_id=1, source_target_pairs={{0,1},{1,0},{2,3},{3,2},{4,5},{5,4},{6,7},{7,6},{8,9},{9,8},{10,11... | collective-permute-start | bytes 196616 | tf_op jit(solution)/shard_map/ppermute | solution.py:410

commit v3 on v2

--- a/solution.py
+++ b/solution.py
@@ -22,8 +22,8 @@
 SMEM = pl.BlockSpec(memory_space=pltpu.SMEM)
 
 
-def block_bits(place, slots):
-    return (slots - place) & (slots - 1)
+def far_bits(i, row, slots):
+    return slots // 2 + i + (1 - row) * (slots // 4)
 
 
 def iota(shape, dim):
@@ -45,13 +45,14 @@
 
 
 def pack_kernel(tiles, ranks, stretch_len, stretches_hbm, store_hbm, *refs):
-    *outs, stretches_ref, store_ref, ids_ref, sems = refs
+    *outs, give_ref, stretches_ref, store_ref, ids_ref, sems = refs
     get_store = pltpu.make_async_copy(store_hbm, store_ref, sems.at[0])
     get_stretches = pltpu.make_async_copy(stretches_hbm, stretches_ref, sems.at[1])
     get_stretches.start()
     get_store.start()
     slot = lax.axis_index("slot")
-    own = slot * lax.axis_size("row") + lax.axis_index("row")
+    row = lax.axis_index("row")
+    own = slot * lax.axis_size("row") + row
     slots, slot_tiles = stretches_ref.shape
     per_slot = ranks * 2 * stretch_len
     rows = slots * per_slot
@@ -73,7 +74,8 @@
     ids = jnp.concatenate(
         [
             jnp.broadcast_to(ids_ref[pl.ds(slot ^ k, 1), :], (per_slot, 128))
-            for k in range(slots)
+            for k in list(range(slots // 2))
+            + [far_bits(i, r, slots) for r in (row, 1 - row) for i in range(slots // 4)]
         ],
         axis=0,
     )
@@ -83,8 +85,9 @@
     pick = (iota((rows, store_rows), 1) == source).astype(F32).astype(BF16)
     get_store.wait()
     picked = jnp.dot(pick, store_ref[...], preferred_element_type=F32).astype(BF16)
-    for k in range(slots):
-        outs[k][...] = picked[k * per_slot : (k + 1) * per_slot]
+    for i, out_ref in enumerate(outs):
+        out_ref[...] = picked[i * per_slot : (i + 1) * per_slot]
+    give_ref[...] = picked[len(outs) * per_slot :]
 
 
 def fetch(pieces, sems):
@@ -101,7 +104,7 @@
     ]
 
 
-def project_kernel(step, hidden_ref, wq_ref, wk_ref, wv_ref, out_ref):
+def project_kernel(step, after_ref, hidden_ref, wq_ref, wk_ref, wv_ref, out_ref):
     tokens = hidden_ref[...]
     base = 0
     for weight_ref in (wq_ref, wk_ref, wv_ref):
@@ -147,9 +150,13 @@
     slot_tiles = stretches_ref.shape[1]
     stretches = stretches_ref[pl.ds(slot, 1), :]
     owner, _ = divide(stretches, tiles)
-    from_slot, rank_wanted = divide(iota((arriving, slot_tiles), 0), ranks)
-    from_slot = block_bits(from_slot, arriving // ranks) ^ slot
-    match = (owner == from_slot * row_total + row).astype(F32)
+    slots = arriving // ranks
+    place, rank_wanted = divide(iota((arriving, slot_tiles), 0), ranks)
+    near = place < slots // 2
+    beyond = place - slots // 2
+    from_slot = slot ^ jnp.where(near, place, far_bits(beyond >> 1, row, slots))
+    from_row = row ^ jnp.where(near, 0, beyond & 1)
+    match = (owner == from_slot * row_total + from_row).astype(F32)
     rank = earlier_count(match)
     picked = jnp.where(rank == rank_wanted.astype(F32), match, 0.0)
     tile = jnp.sum(picked * iota((arriving, slot_tiles), 1).astype(F32), axis=1, keepdims=True)
@@ -205,8 +212,12 @@
     return kept
 
 
-def attend_kernel(stretch_rows, *refs):
+def attend_kernel(stretch_rows, far_count, *refs):
     *arrived, cos_ref, sin_ref, bias_ref, token_cos_ref, token_sin_ref, both_ref, out_ref = refs
+    arrived = arrived[far_count:][::-1] + arrived[:far_count]
+    parts = [
+        (ref, at) for ref in arrived for at in range(0, ref.shape[0], 2 * stretch_rows)
+    ]
     row = lax.axis_index("row")
     token_total = token_cos_ref.shape[0]
     share = bias_ref.shape[0] - cos_ref.shape[0]
@@ -237,10 +248,12 @@
         ).astype(BF16)
         new_keys = rotated(projected(query_columns + at), token_cosine, token_sine)
         new_values = projected(query_columns + key_columns + at)
-        keys = jnp.concatenate([ref[:stretch_rows, cols] for ref in arrived], axis=0)
+        keys = jnp.concatenate([ref[at : at + stretch_rows, cols] for ref, at in parts], axis=0)
         keys = rotated(keys.astype(F32), cosine, sine).astype(BF16)
         keys = jnp.concatenate([keys, of_row(new_keys, row, share).astype(BF16)], axis=0)
-        values = [ref[stretch_rows:, cols] for ref in arrived]
+        values = [
+            ref[at + stretch_rows : at + 2 * stretch_rows, cols] for ref, at in parts
+        ]
         values = jnp.concatenate(values + [of_row(new_values, row, share).astype(BF16)], axis=0)
         scores = lax.dot_general(
             keys, queries, (((1,), (1,)), ((), ())), preferred_element_type=F32
@@ -292,6 +305,31 @@
 
 def in_hbm(value):
     return pltpu.with_memory_space_constraint(value, pltpu.HBM)
+
+
+def merge_kernel(count, near_count, *refs):
+    kept, given, outs = refs[:count], refs[count], refs[count + 1 + near_count :]
+    rows = kept[0].shape[0]
+    for i in range(count):
+        outs[i][:rows] = kept[i][...]
+        outs[i][rows:] = given[i * rows : (i + 1) * rows]
+
+
+def merge(kept, given, near, grant):
+    count, near_count = len(kept), len(near)
+    block = kept[0]
+    results = pl.pallas_call(
+        functools.partial(merge_kernel, count, near_count),
+        out_shape=[jax.ShapeDtypeStruct((2 * block.shape[0], block.shape[1]), BF16)] * count
+        + [jax.ShapeDtypeStruct(block.shape, BF16)] * near_count,
+        in_specs=[VMEM] * (count + 1) + [ANY] * near_count,
+        out_specs=[VMEM] * count + [ANY] * near_count,
+        input_output_aliases={count + 1 + i: count + i for i in range(near_count)},
+        compiler_params=params(grant),
+        cost_estimate=cost(0),
+        name="merge",
+    )(*kept, given, *near)
+    return *results[:count], results[count:]
 
 
 def params(mib):
@@ -333,11 +371,15 @@
     freq = jnp.asarray(np.concatenate([freq, freq])[None, :])
 
     store_shape = (tiles * 2 * stretch_len, key_columns)
-    outgoing = pl.pallas_call(
+    step = key_columns
+    half, quarter = slot_total // 2, slot_total // 4
+    block = jax.ShapeDtypeStruct((per_slot, key_columns), BF16)
+    *outgoing, give = pl.pallas_call(
         functools.partial(pack_kernel, tiles, ranks, stretch_len),
-        out_shape=[jax.ShapeDtypeStruct((per_slot, key_columns), BF16)] * slot_total,
+        out_shape=[block] * (half + quarter)
+        + [jax.ShapeDtypeStruct((quarter * per_slot, key_columns), BF16)],
         in_specs=[HBM, HBM],
-        out_specs=[VMEM] * slot_total,
+        out_specs=[VMEM] * (half + quarter + 1),
         scratch_shapes=[
             pltpu.VMEM(tile_stretch.shape, jnp.int32),
             pltpu.VMEM(store_shape, BF16),
@@ -348,22 +390,30 @@
         cost_estimate=cost(8),
         name="pack",
     )(in_hbm(tile_stretch), in_hbm(kv_store.reshape(store_shape)))
-    step = key_columns
-    order = [block_bits(place, slot_total) for place in range(slot_total)]
-    blocks = [outgoing[0]] + [
-        lax.ppermute(outgoing[k], "slot", [(i, i ^ k) for i in range(slot_total)])
-        for k in order[1:]
+    given = lax.ppermute(give, "row", swap)
+    *merged, near_blocks = merge(outgoing[half:], given, outgoing[1:half], grant)
+    far = []
+    for i in range(quarter):
+        pairs = [
+            (s * row_total + r, (s ^ far_bits(i, r, slot_total)) * row_total + r)
+            for s in range(slot_total)
+            for r in range(row_total)
+        ]
+        far.append(lax.ppermute(merged[i], ("slot", "row"), pairs))
+    near = [outgoing[0]] + [
+        lax.ppermute(near_blocks[k - 1], "slot", [(s, s ^ k) for s in range(slot_total)])
+        for k in range(1, half)
     ]
 
     projected = pl.pallas_call(
         functools.partial(project_kernel, step),
         out_shape=jax.ShapeDtypeStruct((token_total, query_columns + 2 * key_columns), F32),
-        in_specs=[VMEM] * 4,
+        in_specs=[ANY] + [VMEM] * 4,
         out_specs=VMEM,
         compiler_params=params(grant),
         cost_estimate=cost(0),
         name="project",
-    )(hidden[0], w_query, key_weight, value_weight)
+    )(merged[0], hidden[0], w_query, key_weight, value_weight)
     both = lax.all_gather(projected, "row")
 
     tables = pl.pallas_call(
@@ -383,14 +433,14 @@
     )(tile_stretch, stretch_offset.reshape(-1, 128), slot_count, recomp_pos, freq)
 
     partial = pl.pallas_call(
-        functools.partial(attend_kernel, ranks * stretch_len),
+        functools.partial(attend_kernel, ranks * stretch_len, quarter),
         out_shape=jax.ShapeDtypeStruct((key_heads * HEAD_WIDTH + 2 * key_heads, query_rows), F32),
-        in_specs=[VMEM] * (slot_total + 6),
+        in_specs=[VMEM] * (quarter + half + 6),
         out_specs=VMEM,
         compiler_params=params(grant),
         cost_estimate=cost(8),
         name="attend",
-    )(*blocks, *tables, both)
+    )(*far, *reversed(near), *tables, both)
     partial_other = lax.ppermute(partial, "row", swap)
 
     out_columns = w_out.shape[1]

time: 30 us -> 29 us (0.967)
  starting transfers between devices: 14.2 us -> 13.6 us
  waiting for transfers between devices: 4.52 us -> 4.05 us
    ppermute x7 -> x6, starting transfers between devices: 12.6 us -> 10.1 us  [the longest x2 6.07 us: on_device(): far.append(lax.ppermute(merged[i], ('slot', 'row'), pairs))]
    ppermute x1, starting transfers between devices: 0.07 us -> 1.99 us  [on_device(): partial_other = lax.ppermute(partial, 'row', swap)]
    ppermute x1, waiting for transfers between devices: 1.53 us -> 1.17 us  [on_device(): partial_other = lax.ppermute(partial, 'row', swap)]
    pallas_call x1 -> x2, Pallas kernels: 1.19 us -> 1.22 us  [the longest x1 1.2 us: on_device(): pl.pallas_call(functools.partial(attend_kernel, ranks * stretch_len, quar...]
  transfers between devices with their start and end apart: 9 -> 8, of which waited for: 3 -> 2; matrix products, arithmetic and copies ran while one was open for 0% -> 0% of each run, Pallas kernels for 11% -> 11%
where the time goes in v3:
time: 29 us; the launch traced here: 28.9 us
  starting transfers between devices  13.6 us (47%)
  Pallas kernels  7.88 us (27%)
  waiting for transfers between devices  4.05 us (14%)
  blocking collectives  2.5 us (9%)
  other arithmetic  0.64 us (2%)
    ppermute x2, starting transfers between devices, on_device(): far.append(lax.ppermute(merged[i], ('slot', 'row'), pairs))  6.07 us
    ppermute x3, starting transfers between devices, on_device(): lax.ppermute(near_blocks[k - 1], 'slot', [(s, s ^ k) for s in range(slot_...  3.49 us
    ppermute x1, waiting for transfers between devices, on_device(): received = lax.ppermute(send, 'col', swap)  2.87 us
    all_gather x1, blocking collectives, on_device(): both = lax.all_gather(projected, 'row')  2.5 us
    pallas_call x1, Pallas kernels, on_device(): pl.pallas_call(functools.partial(project_kernel, step), out_shape=jax.Sha...  2.24 us
    ppermute x1, starting transfers between devices, on_device(): partial_other = lax.ppermute(partial, 'row', swap)  1.99 us
    pallas_call x1, Pallas kernels, on_device(): pl.pallas_call(functools.partial(pack_kernel, tiles, ranks, stretch_len),...  1.72 us
    pallas_call x1, Pallas kernels, on_device(): pl.pallas_call(functools.partial(output_kernel, step, key_heads), out_sha...  1.64 us
  transfers between devices with their start and end apart: 8, of which 2 were waited for; matrix products, arithmetic and copies ran while one was open for 0% of the time, Pallas kernels for 11%

profile of v3, /device:TPU:0, one launch (start us, length us, event | category | flops | bytes accessed | tf_op | source)
XLA Modules:
  0.0 28.9 jit_solution(18061155969777945511)
XLA Ops:
  0.0 0.0 copy-start.4
  0.0 0.0 copy-start.5
  0.0 0.0 copy-start.6
  0.0 0.0 copy-start.7
  0.0 0.0 copy-start.8
  0.0 0.0 copy-start
  0.0 0.0 copy-start.1
  0.0 0.0 copy-start.2
  0.0 0.0 copy-start.3
  0.1 1.7 %pack.1 = (bf16[64,512]{1,0:T(8,128)(2,1)S(1)}, bf16[64,512]{1,0:T(8,128)(2,1)S(1)}, bf16[64,512]{1,0:T(8,128)(2,1)S(1)}, bf16[64,512]{1,0:T(8,128)(2,1)S(1)}, b...) custom-call(s32[8,64]{1,0:T(8,128)} %stretches_ref.1, bf16[512,512]{1,0:T(8,128)(2,1)} %bitcast.11), custom_call_target="tpu_custom_call" | custom-call | flops 8000000000 | bytes 1000 | tf_op jit(solution)/shard_map/pack/pallas_call | solution.py:377
  1.8 0.5 %collective-permute-start = (bf16[128,512]{1,0:T(8,128)(2,1)S(1)}, bf16[128,512]{1,0:T(8,128)(2,1)S(1)}, u32[]{:S(2)}, u32[]{:S(2)}) collective-permute-start(bf16[128,512]{1,0:T(8,128)(2,1)S(1)} %get-tuple-element.26), channel_id=1, source_target_pairs={{0,2},{2,0},{1,3},{3,1},{4,6},{6,4},{5,7},{7,5},{8,10},{10,8},{9,1... | collective-permute-start | bytes 393224 | tf_op jit(solution)/shard_map/ppermute | solution.py:393
  2.3 0.0 copy-done.4
  2.3 0.0 copy-done.5
  2.3 0.0 copy-done.6
  2.3 0.0 copy-done.7
  2.3 0.0 copy-done.8
  2.3 1.1 %tables.1 = (f32[256,128]{1,0:T(8,128)S(1)}, f32[256,128]{1,0:T(8,128)S(1)}, f32[272,128]{1,0:T(8,128)S(1)}, f32[32,128]{1,0:T(8,128)S(1)}, f32[32,128]{1,0:T(8,128)S(1)}) custom-call(s32[8,64]{1,0:T(8,128)S(1)} %copy-done.4, s32[4,128]{1,0:T(4,128)S(1)} %bitcast.10, s32[8]{0:T(128)S(1)} %copy-done.6, s32[1,32]{1,0:T(1,128)S(1)} %copy-done.7, ...), custom_call_target="tpu_custom_call" | custom-call | bytes 1000 | tf_op jit(solution)/shard_map/tables/pallas_call | solution.py:419
  3.4 0.0 collective-permute-done.refs_2_
  3.5 4.9 %collective-permute-start.1 = (bf16[128,512]{1,0:T(8,128)(2,1)S(1)}, bf16[128,512]{1,0:T(8,128)(2,1)S(1)}, u32[]{:S(2)}, u32[]{:S(2)}) collective-permute-start(bf16[128,512]{1,0:T(8,128)(2,1)S(1)} %get-tuple-element.30.after_ref), channel_id=1, source_target_pairs={{0,24},{2,18},{4,28},{6,22},{8,16},{10,26},{12,20},{14,30},{16,8},... | collective-permute-start | bytes 393224 | tf_op jit(solution)/shard_map/ppermute | solution.py:402
  8.3 1.2 %collective-permute-start.2 = (bf16[128,512]{1,0:T(8,128)(2,1)S(1)}, bf16[128,512]{1,0:T(8,128)(2,1)S(1)}, u32[]{:S(2)}, u32[]{:S(2)}) collective-permute-start(bf16[128,512]{1,0:T(8,128)(2,1)S(1)} %get-tuple-element.31), channel_id=1, source_target_pairs={{0,28},{2,22},{4,24},{6,18},{8,20},{10,30},{12,16},{14,26},{16,12}... | collective-permute-start | bytes 393224 | tf_op jit(solution)/shard_map/ppermute | solution.py:402
  9.5 0.0 collective-permute-start.3
  9.5 1.8 %collective-permute-start.4 = (bf16[64,512]{1,0:T(8,128)(2,1)S(1)}, bf16[64,512]{1,0:T(8,128)(2,1)S(1)}, u32[]{:S(2)}, u32[]{:S(2)}) collective-permute-start(bf16[64,512]{1,0:T(8,128)(2,1)S(1)} %get-tuple-element.33), channel_id=1, source_target_pairs={{0,8},{4,12},{8,0},{12,4},{16,24},{20,28},{24,16},{28,20},{1,9},{5... | collective-permute-start | bytes 196616 | tf_op jit(solution)/shard_map/ppermute | solution.py:404
  11.4 1.7 %collective-permute-start.5 = (bf16[64,512]{1,0:T(8,128)(2,1)S(1)}, bf16[64,512]{1,0:T(8,128)(2,1)S(1)}, u32[]{:S(2)}, u32[]{:S(2)}) collective-permute-start(bf16[64,512]{1,0:T(8,128)(2,1)S(1)} %get-tuple-element.34), channel_id=1, source_target_pairs={{0,4},{4,0},{8,12},{12,8},{16,20},{20,16},{24,28},{28,24},{1,5},{5... | collective-permute-start | bytes 196616 | tf_op jit(solution)/shard_map/ppermute | solution.py:404
  13.0 0.0 copy-done
  13.0 0.0 copy-done.1
  13.0 0.0 copy-done.2
  13.0 0.0 copy-done.3
  13.0 2.2 %project.1 = f32[32,3072]{1,0:T(8,128)S(1)} custom-call(bf16[128,512]{1,0:T(8,128)(2,1)S(1)} %get-tuple-element.30.after_ref, bf16[32,2048]{1,0:T(8,128)(2,1)S(1)} %bitcast.9, bf16[2048,2048]{1,0:T(8,128)(2,1)S(1)} %copy-done, bf16[2048,512]{1,0:T(8,128)(2,1)S(1)} %copy-done.1, bf16[2048,512]{1,0:T(8,128)(2,1)S(1)} %copy-done.2), custom_call_target="tpu_custom_call" | custom-call | bytes 1000 | tf_op jit(solution)/shard_map/project/pallas_call | solution.py:408
  15.3 0.0 slice-start
  15.3 2.5 %all-gather = f32[64,3072]{1,0:T(8,128)S(1)} all-gather(f32[32,3072]{1,0:T(8,128)S(1)} %project.1), channel_id=2, replica_groups=mesh['slot'=8,'row'=2,'col'=2] {'row'}, dimensions={0}, use_global_device_ids=true | all-gather | bytes 1179648 | tf_op jit(solution)/shard_map/all_gather | solution.py:417
  17.8 0.0 collective-permute-done.3.refs_2_
  17.8 0.0 collective-permute-done.4.refs_3_
  17.8 0.0 collective-permute-done.5.refs_4_
  17.8 0.0 collective-permute-done.1.refs_0_
  17.8 0.0 collective-permute-done.2.refs_1_
  17.8 0.0 slice-start.1
  17.8 1.2 %attend.1.own_ref = f32[520,128]{1,0:T(8,128)S(1)} custom-call(bf16[128,512]{1,0:T(8,128)(2,1)S(1)} %collective-permute-done.1.refs_0_, bf16[128,512]{1,0:T(8,128)(2,1)S(1)} %collective-permute-done.2.refs_1_, bf16[64,512]{1,0:T(8,128)(2,1)S(1)} %collective-permute-done.3.refs_2_, bf16[64,512]{1,0:T(8,128)(2,1)S(1)} %collective-permute-done.4.refs_3_, ...), custom_call_target="tpu_custom_call" | custom-call | flops 8000000000 | bytes 1000 | tf_op jit(solution)/shard_map/attend/pallas_call | solution.py:435
  19.0 2.0 %collective-permute-start.6 = (f32[520,128]{1,0:T(8,128)S(1)}, f32[520,128]{1,0:T(8,128)S(1)}, u32[]{:S(2)}, u32[]{:S(2)}) collective-permute-start(f32[520,128]{1,0:T(8,128)S(1)} %attend.1.own_ref), channel_id=1, source_target_pairs={{0,2},{2,0},{1,3},{3,1},{4,6},{6,4},{5,7},{7,5},{8,10},{10,8},{9,1... | collective-permute-start | bytes 798728 | tf_op jit(solution)/shard_map/ppermute | solution.py:444
  21.0 1.2 %collective-permute-done.6.other_ref = f32[520,128]{1,0:T(8,128)S(1)} collective-permute-done((f32[520,128]{1,0:T(8,128)S(1)}, f32[520,128]{1,0:T(8,128)S(1)}, u32[]{:S(2)}, u32[]{:S(2)}) %collective-permute-start.6) | collective-permute-done | bytes 266272 | tf_op jit(solution)/shard_map/ppermute | solution.py:444
  22.2 0.0 slice-done
  22.2 0.0 slice-done.1
  22.2 1.6 %output.1 = (f32[16,2048]{1,0:T(8,128)S(1)}, bf16[16,2048]{1,0:T(8,128)(2,1)S(1)}) custom-call(f32[520,128]{1,0:T(8,128)S(1)} %attend.1.own_ref, f32[520,128]{1,0:T(8,128)S(1)} %collective-permute-done.6.other_ref, bf16[2048,2048]{1,0:T(8,128)(2,1)S(1)} %bitcast.7), custom_call_target="tpu_custom_call" | custom-call | tf_op jit(solution)/shard_map/output/pallas_call | solution.py:448
  23.8 1.5 %collective-permute-start.7 = (bf16[16,2048]{1,0:T(8,128)(2,1)S(1)}, bf16[16,2048]{1,0:T(8,128)(2,1)S(1)}, u32[]{:S(2)}, u32[]{:S(2)}) collective-permute-start(bf16[16,2048]{1,0:T(8,128)(2,1)S(1)} %get-tuple-element.42), channel_id=1, source_target_pairs={{0,1},{1,0},{2,3},{3,2},{4,5},{5,4},{6,7},{7,6},{8,9},{9,8},{10,11... | collective-permute-start | bytes 196616 | tf_op jit(solution)/shard_map/ppermute | solution.py:460
  25.4 2.9 %collective-permute-done.7 = bf16[16,2048]{1,0:T(8,128)(2,1)S(1)} collective-permute-done((bf16[16,2048]{1,0:T(8,128)(2,1)S(1)}, bf16[16,2048]{1,0:T(8,128)(2,1)S(1)}, u32[]{:S(2)}, u32[]{:S(2)}) %collective-permute-start.7) | collective-permute-done | bytes 65568 | tf_op jit(solution)/shard_map/ppermute | solution.py:460
  28.2 0.6 %fusion = bf16[1,16,2048]{2,1,0:T(8,128)(2,1)} fusion(f32[16,2048]{1,0:T(8,128)S(1)} %get-tuple-element.41, bf16[16,2048]{1,0:T(8,128)(2,1)S(1)} %collective-permute-done.7), kind=kLoop, calls=%fused_computation.1 | loop fusion | flops 98304 | bytes 262144 | tf_op jit(solution)/shard_map/broadcast_in_dim | solution.py:461
  (2 shorter events, 0.0 us)
Async XLA Ops:
  0.0 2.3 %copy-start.4 = (s32[8,64]{1,0:T(8,128)S(1)}, s32[8,64]{1,0:T(8,128)}, u32[]{:S(2)}) copy-start(s32[8,64]{1,0:T(8,128)} %stretches_ref.1) | copy-start | bytes 6148
  0.0 2.3 %copy-start.5 = (s32[512]{0:T(512)S(1)}, s32[512]{0:T(512)}, u32[]{:S(2)}) copy-start(s32[512]{0:T(512)} %param.17) | copy-start | bytes 6148
  0.0 2.3 %copy-start.6 = (s32[8]{0:T(128)S(1)}, s32[8]{0:T(128)}, u32[]{:S(2)}) copy-start(s32[8]{0:T(128)} %counts_ref.1) | copy-start | bytes 100
  0.0 2.3 %copy-start.7 = (s32[1,32]{1,0:T(1,128)S(1)}, s32[1,32]{1,0:T(1,128)}, u32[]{:S(2)}) copy-start(s32[1,32]{1,0:T(1,128)} %positions_ref.1) | copy-start | bytes 388
  0.0 2.3 %copy-start.8 = (f32[1,128]{1,0:T(1,128)S(1)}, f32[1,128]{1,0:T(1,128)}, u32[]{:S(2)}) copy-start(f32[1,128]{1,0:T(1,128)} %constant.2.clone.freq_ref) | copy-start | bytes 1540
  0.0 13.0 %copy-start = (bf16[2048,2048]{1,0:T(8,128)(2,1)S(1)}, bf16[2048,2048]{1,0:T(8,128)(2,1)}, u32[]{:S(2)}) copy-start(bf16[2048,2048]{1,0:T(8,128)(2,1)} %wq_ref.1) | copy-start | bytes 25165828
  0.0 13.0 %copy-start.1 = (bf16[2048,512]{1,0:T(8,128)(2,1)S(1)}, bf16[2048,512]{1,0:T(8,128)(2,1)}, u32[]{:S(2)}) copy-start(bf16[2048,512]{1,0:T(8,128)(2,1)} %wk_ref.1) | copy-start | bytes 6291460
  0.0 13.0 %copy-start.2 = (bf16[2048,512]{1,0:T(8,128)(2,1)S(1)}, bf16[2048,512]{1,0:T(8,128)(2,1)}, u32[]{:S(2)}) copy-start(bf16[2048,512]{1,0:T(8,128)(2,1)} %wv_ref.1) | copy-start | bytes 6291460
  0.0 13.0 %copy-start.3 = (bf16[1,32,2048]{2,1,0:T(8,128)(2,1)S(1)}, bf16[1,32,2048]{2,1,0:T(8,128)(2,1)}, u32[]{:S(2)}) copy-start(bf16[1,32,2048]{2,1,0:T(8,128)(2,1)} %param.11) | copy-start | bytes 393220
  1.8 1.6 %collective-permute-start = (bf16[128,512]{1,0:T(8,128)(2,1)S(1)}, bf16[128,512]{1,0:T(8,128)(2,1)S(1)}, u32[]{:S(2)}, u32[]{:S(2)}) collective-permute-start(bf16[128,512]{1,0:T(8,128)(2,1)S(1)} %get-tuple-element.26), channel_id=1, source_target_pairs={{0,2},{2,0},{1,3},{3,1},{4,6},{6,4},{5,7},{7,5},{8,10},{10,8},{9,1... | collective-permute-start | bytes 393224 | tf_op jit(solution)/shard_map/ppermute | solution.py:393
  3.5 14.3 %collective-permute-start.1 = (bf16[128,512]{1,0:T(8,128)(2,1)S(1)}, bf16[128,512]{1,0:T(8,128)(2,1)S(1)}, u32[]{:S(2)}, u32[]{:S(2)}) collective-permute-start(bf16[128,512]{1,0:T(8,128)(2,1)S(1)} %get-tuple-element.30.after_ref), channel_id=1, source_target_pairs={{0,24},{2,18},{4,28},{6,22},{8,16},{10,26},{12,20},{14,30},{16,8},... | collective-permute-start | bytes 393224 | tf_op jit(solution)/shard_map/ppermute | solution.py:402
  8.3 9.5 %collective-permute-start.2 = (bf16[128,512]{1,0:T(8,128)(2,1)S(1)}, bf16[128,512]{1,0:T(8,128)(2,1)S(1)}, u32[]{:S(2)}, u32[]{:S(2)}) collective-permute-start(bf16[128,512]{1,0:T(8,128)(2,1)S(1)} %get-tuple-element.31), channel_id=1, source_target_pairs={{0,28},{2,22},{4,24},{6,18},{8,20},{10,30},{12,16},{14,26},{16,12}... | collective-permute-start | bytes 393224 | tf_op jit(solution)/shard_map/ppermute | solution.py:402
  9.5 8.3 %collective-permute-start.3 = (bf16[64,512]{1,0:T(8,128)(2,1)S(1)}, bf16[64,512]{1,0:T(8,128)(2,1)S(1)}, u32[]{:S(2)}, u32[]{:S(2)}) collective-permute-start(bf16[64,512]{1,0:T(8,128)(2,1)S(1)} %get-tuple-element.32), channel_id=1, source_target_pairs={{0,12},{4,8},{8,4},{12,0},{16,28},{20,24},{24,20},{28,16},{1,13},{... | collective-permute-start | bytes 196616 | tf_op jit(solution)/shard_map/ppermute | solution.py:404
  9.5 8.3 %collective-permute-start.4 = (bf16[64,512]{1,0:T(8,128)(2,1)S(1)}, bf16[64,512]{1,0:T(8,128)(2,1)S(1)}, u32[]{:S(2)}, u32[]{:S(2)}) collective-permute-start(bf16[64,512]{1,0:T(8,128)(2,1)S(1)} %get-tuple-element.33), channel_id=1, source_target_pairs={{0,8},{4,12},{8,0},{12,4},{16,24},{20,28},{24,16},{28,20},{1,9},{5... | collective-permute-start | bytes 196616 | tf_op jit(solution)/shard_map/ppermute | solution.py:404
  11.4 6.4 %collective-permute-start.5 = (bf16[64,512]{1,0:T(8,128)(2,1)S(1)}, bf16[64,512]{1,0:T(8,128)(2,1)S(1)}, u32[]{:S(2)}, u32[]{:S(2)}) collective-permute-start(bf16[64,512]{1,0:T(8,128)(2,1)S(1)} %get-tuple-element.34), channel_id=1, source_target_pairs={{0,4},{4,0},{8,12},{12,8},{16,20},{20,16},{24,28},{28,24},{1,5},{5... | collective-permute-start | bytes 196616 | tf_op jit(solution)/shard_map/ppermute | solution.py:404
  15.3 6.9 %slice-start = ((s8[8388608]{0:T(1024)(128)(4,1)}), s8[4194304]{0:T(1024)(128)(4,1)S(1)}, s32[]{:S(2)}) async-start(s8[8388608]{0:T(1024)(128)(4,1)} %bitcast.6), calls=%async_computation | async-start | bytes 8388608
  17.8 4.4 %slice-start.1 = ((s8[8388608]{0:T(1024)(128)(4,1)}), s8[4194304]{0:T(1024)(128)(4,1)S(1)}, s32[]{:S(2)}) async-start(s8[8388608]{0:T(1024)(128)(4,1)} %bitcast.6), calls=%async_computation.1 | async-start | bytes 8388608
  19.0 3.2 %collective-permute-start.6 = (f32[520,128]{1,0:T(8,128)S(1)}, f32[520,128]{1,0:T(8,128)S(1)}, u32[]{:S(2)}, u32[]{:S(2)}) collective-permute-start(f32[520,128]{1,0:T(8,128)S(1)} %attend.1.own_ref), channel_id=1, source_target_pairs={{0,2},{2,0},{1,3},{3,1},{4,6},{6,4},{5,7},{7,5},{8,10},{10,8},{9,1... | collective-permute-start | bytes 798728 | tf_op jit(solution)/shard_map/ppermute | solution.py:444
  23.8 4.4 %collective-permute-start.7 = (bf16[16,2048]{1,0:T(8,128)(2,1)S(1)}, bf16[16,2048]{1,0:T(8,128)(2,1)S(1)}, u32[]{:S(2)}, u32[]{:S(2)}) collective-permute-start(bf16[16,2048]{1,0:T(8,128)(2,1)S(1)} %get-tuple-element.42), channel_id=1, source_target_pairs={{0,1},{1,0},{2,3},{3,2},{4,5},{5,4},{6,7},{7,6},{8,9},{9,8},{10,11... | collective-permute-start | bytes 196616 | tf_op jit(solution)/shard_map/ppermute | solution.py:460

commit v4 on v3

--- a/solution.py
+++ b/solution.py
@@ -236,6 +236,7 @@
         cols = slice(start, start + HEAD_WIDTH)
         return both_ref[0, :, cols] + both_ref[1, :, cols]
 
+    all_scores, all_values = [], []
     for head in range(key_heads):
         at = head * HEAD_WIDTH
         cols = slice(at, at + HEAD_WIDTH)
@@ -254,20 +255,29 @@
         values = [
             ref[at + stretch_rows : at + 2 * stretch_rows, cols] for ref, at in parts
         ]
-        values = jnp.concatenate(values + [of_row(new_values, row, share).astype(BF16)], axis=0)
-        scores = lax.dot_general(
-            keys, queries, (((1,), (1,)), ((), ())), preferred_element_type=F32
+        all_values.append(
+            jnp.concatenate(values + [of_row(new_values, row, share).astype(BF16)], axis=0)
         )
+        all_scores.append(
+            lax.dot_general(
+                keys, queries, (((1,), (1,)), ((), ())), preferred_element_type=F32
+            )
+        )
+    all_probs = []
+    base = key_heads * HEAD_WIDTH
+    for head, scores in enumerate(all_scores):
         scores = scores * scale + bias
         peak = jnp.max(scores, axis=0, keepdims=True)
         probs = jnp.exp(scores - peak)
-        total = jnp.sum(probs, axis=0, keepdims=True)
-        out_ref[cols, :] = lax.dot_general(
-            values, probs.astype(BF16), (((0,), (0,)), ((), ())), preferred_element_type=F32
+        out_ref[base + head : base + head + 1, :] = peak
+        out_ref[base + key_heads + head : base + key_heads + head + 1, :] = jnp.sum(
+            probs, axis=0, keepdims=True
         )
-        base = key_heads * HEAD_WIDTH
-        out_ref[base + head : base + head + 1, :] = peak
-        out_ref[base + key_heads + head : base + key_heads + head + 1, :] = total
+        all_probs.append(probs.astype(BF16))
+    for head in range(key_heads):
+        out_ref[head * HEAD_WIDTH : (head + 1) * HEAD_WIDTH, :] = lax.dot_general(
+            all_values[head], all_probs[head], (((0,), (0,)), ((), ())), preferred_element_type=F32
+        )
 
 
 def output_kernel(step, key_heads, own_ref, other_ref, w_ref, keep_ref, send_ref, attended):

time: 29 us -> 28.5 us (0.983)
  Pallas kernels: 7.88 us -> 7.33 us
    pallas_call x1, Pallas kernels: 1.2 us -> 0.64 us  [on_device(): pl.pallas_call(functools.partial(attend_kernel, ranks * stretch_len, quar...]
  transfers between devices with their start and end apart: 8 -> 8, of which waited for: 2 -> 2; matrix products, arithmetic and copies ran while one was open for 0% -> 0% of each run, Pallas kernels for 11% -> 12%
where the time goes in v4:
time: 28.5 us; the launch traced here: 28.3 us
  starting transfers between devices  13.6 us (48%)
  Pallas kernels  7.33 us (26%)
  waiting for transfers between devices  4.05 us (14%)
  blocking collectives  2.5 us (9%)
  other arithmetic  0.64 us (2%)
    ppermute x2, starting transfers between devices, on_device(): far.append(lax.ppermute(merged[i], ('slot', 'row'), pairs))  6.07 us
    ppermute x3, starting transfers between devices, on_device(): lax.ppermute(near_blocks[k - 1], 'slot', [(s, s ^ k) for s in range(slot_...  3.49 us
    ppermute x1, waiting for transfers between devices, on_device(): received = lax.ppermute(send, 'col', swap)  2.86 us
    all_gather x1, blocking collectives, on_device(): both = lax.all_gather(projected, 'row')  2.5 us
    pallas_call x1, Pallas kernels, on_device(): pl.pallas_call(functools.partial(project_kernel, step), out_shape=jax.Sha...  2.24 us
    ppermute x1, starting transfers between devices, on_device(): partial_other = lax.ppermute(partial, 'row', swap)  1.99 us
    pallas_call x1, Pallas kernels, on_device(): pl.pallas_call(functools.partial(pack_kernel, tiles, ranks, stretch_len),...  1.72 us
    pallas_call x1, Pallas kernels, on_device(): pl.pallas_call(functools.partial(output_kernel, step, key_heads), out_sha...  1.64 us
  transfers between devices with their start and end apart: 8, of which 2 were waited for; matrix products, arithmetic and copies ran while one was open for 0% of the time, Pallas kernels for 12%

profile of v4, /device:TPU:0, one launch (start us, length us, event | category | flops | bytes accessed | tf_op | source)
XLA Modules:
  0.0 28.3 jit_solution(14030664310843149224)
XLA Ops:
  0.0 0.0 copy-start.4
  0.0 0.0 copy-start.5
  0.0 0.0 copy-start.6
  0.0 0.0 copy-start.7
  0.0 0.0 copy-start.8
  0.0 0.0 copy-start
  0.0 0.0 copy-start.1
  0.0 0.0 copy-start.2
  0.0 0.0 copy-start.3
  0.1 1.7 %pack.1 = (bf16[64,512]{1,0:T(8,128)(2,1)S(1)}, bf16[64,512]{1,0:T(8,128)(2,1)S(1)}, bf16[64,512]{1,0:T(8,128)(2,1)S(1)}, bf16[64,512]{1,0:T(8,128)(2,1)S(1)}, b...) custom-call(s32[8,64]{1,0:T(8,128)} %stretches_ref.1, bf16[512,512]{1,0:T(8,128)(2,1)} %bitcast.11), custom_call_target="tpu_custom_call" | custom-call | flops 8000000000 | bytes 1000 | tf_op jit(solution)/shard_map/pack/pallas_call | solution.py:387
  1.8 0.5 %collective-permute-start = (bf16[128,512]{1,0:T(8,128)(2,1)S(1)}, bf16[128,512]{1,0:T(8,128)(2,1)S(1)}, u32[]{:S(2)}, u32[]{:S(2)}) collective-permute-start(bf16[128,512]{1,0:T(8,128)(2,1)S(1)} %get-tuple-element.26), channel_id=1, source_target_pairs={{0,2},{2,0},{1,3},{3,1},{4,6},{6,4},{5,7},{7,5},{8,10},{10,8},{9,1... | collective-permute-start | bytes 393224 | tf_op jit(solution)/shard_map/ppermute | solution.py:403
  2.3 0.0 copy-done.4
  2.3 0.0 copy-done.5
  2.3 0.0 copy-done.6
  2.3 0.0 copy-done.7
  2.3 0.0 copy-done.8
  2.3 1.1 %tables.1 = (f32[256,128]{1,0:T(8,128)S(1)}, f32[256,128]{1,0:T(8,128)S(1)}, f32[272,128]{1,0:T(8,128)S(1)}, f32[32,128]{1,0:T(8,128)S(1)}, f32[32,128]{1,0:T(8,128)S(1)}) custom-call(s32[8,64]{1,0:T(8,128)S(1)} %copy-done.4, s32[4,128]{1,0:T(4,128)S(1)} %bitcast.10, s32[8]{0:T(128)S(1)} %copy-done.6, s32[1,32]{1,0:T(1,128)S(1)} %copy-done.7, ...), custom_call_target="tpu_custom_call" | custom-call | bytes 1000 | tf_op jit(solution)/shard_map/tables/pallas_call | solution.py:429
  3.4 0.0 collective-permute-done.refs_2_
  3.5 4.9 %collective-permute-start.1 = (bf16[128,512]{1,0:T(8,128)(2,1)S(1)}, bf16[128,512]{1,0:T(8,128)(2,1)S(1)}, u32[]{:S(2)}, u32[]{:S(2)}) collective-permute-start(bf16[128,512]{1,0:T(8,128)(2,1)S(1)} %get-tuple-element.30.after_ref), channel_id=1, source_target_pairs={{0,24},{2,18},{4,28},{6,22},{8,16},{10,26},{12,20},{14,30},{16,8},... | collective-permute-start | bytes 393224 | tf_op jit(solution)/shard_map/ppermute | solution.py:412
  8.3 1.2 %collective-permute-start.2 = (bf16[128,512]{1,0:T(8,128)(2,1)S(1)}, bf16[128,512]{1,0:T(8,128)(2,1)S(1)}, u32[]{:S(2)}, u32[]{:S(2)}) collective-permute-start(bf16[128,512]{1,0:T(8,128)(2,1)S(1)} %get-tuple-element.31), channel_id=1, source_target_pairs={{0,28},{2,22},{4,24},{6,18},{8,20},{10,30},{12,16},{14,26},{16,12}... | collective-permute-start | bytes 393224 | tf_op jit(solution)/shard_map/ppermute | solution.py:412
  9.5 0.0 collective-permute-start.3
  9.5 1.8 %collective-permute-start.4 = (bf16[64,512]{1,0:T(8,128)(2,1)S(1)}, bf16[64,512]{1,0:T(8,128)(2,1)S(1)}, u32[]{:S(2)}, u32[]{:S(2)}) collective-permute-start(bf16[64,512]{1,0:T(8,128)(2,1)S(1)} %get-tuple-element.33), channel_id=1, source_target_pairs={{0,8},{4,12},{8,0},{12,4},{16,24},{20,28},{24,16},{28,20},{1,9},{5... | collective-permute-start | bytes 196616 | tf_op jit(solution)/shard_map/ppermute | solution.py:414
  11.4 1.7 %collective-permute-start.5 = (bf16[64,512]{1,0:T(8,128)(2,1)S(1)}, bf16[64,512]{1,0:T(8,128)(2,1)S(1)}, u32[]{:S(2)}, u32[]{:S(2)}) collective-permute-start(bf16[64,512]{1,0:T(8,128)(2,1)S(1)} %get-tuple-element.34), channel_id=1, source_target_pairs={{0,4},{4,0},{8,12},{12,8},{16,20},{20,16},{24,28},{28,24},{1,5},{5... | collective-permute-start | bytes 196616 | tf_op jit(solution)/shard_map/ppermute | solution.py:414
  13.0 0.0 copy-done
  13.0 0.0 copy-done.1
  13.0 0.0 copy-done.2
  13.0 0.0 copy-done.3
  13.0 2.2 %project.1 = f32[32,3072]{1,0:T(8,128)S(1)} custom-call(bf16[128,512]{1,0:T(8,128)(2,1)S(1)} %get-tuple-element.30.after_ref, bf16[32,2048]{1,0:T(8,128)(2,1)S(1)} %bitcast.9, bf16[2048,2048]{1,0:T(8,128)(2,1)S(1)} %copy-done, bf16[2048,512]{1,0:T(8,128)(2,1)S(1)} %copy-done.1, bf16[2048,512]{1,0:T(8,128)(2,1)S(1)} %copy-done.2), custom_call_target="tpu_custom_call" | custom-call | bytes 1000 | tf_op jit(solution)/shard_map/project/pallas_call | solution.py:418
  15.3 0.0 slice-start
  15.3 2.5 %all-gather = f32[64,3072]{1,0:T(8,128)S(1)} all-gather(f32[32,3072]{1,0:T(8,128)S(1)} %project.1), channel_id=2, replica_groups=mesh['slot'=8,'row'=2,'col'=2] {'row'}, dimensions={0}, use_global_device_ids=true | all-gather | bytes 1179648 | tf_op jit(solution)/shard_map/all_gather | solution.py:427
  17.8 0.0 collective-permute-done.3.refs_2_
  17.8 0.0 collective-permute-done.4.refs_3_
  17.8 0.0 collective-permute-done.5.refs_4_
  17.8 0.0 collective-permute-done.1.refs_0_
  17.8 0.0 collective-permute-done.2.refs_1_
  17.8 0.0 slice-start.1
  17.8 0.6 %attend.1.own_ref = f32[520,128]{1,0:T(8,128)S(1)} custom-call(bf16[128,512]{1,0:T(8,128)(2,1)S(1)} %collective-permute-done.1.refs_0_, bf16[128,512]{1,0:T(8,128)(2,1)S(1)} %collective-permute-done.2.refs_1_, bf16[64,512]{1,0:T(8,128)(2,1)S(1)} %collective-permute-done.3.refs_2_, bf16[64,512]{1,0:T(8,128)(2,1)S(1)} %collective-permute-done.4.refs_3_, ...), custom_call_target="tpu_custom_call" | custom-call | flops 8000000000 | bytes 1000 | tf_op jit(solution)/shard_map/attend/pallas_call | solution.py:445
  18.5 2.0 %collective-permute-start.6 = (f32[520,128]{1,0:T(8,128)S(1)}, f32[520,128]{1,0:T(8,128)S(1)}, u32[]{:S(2)}, u32[]{:S(2)}) collective-permute-start(f32[520,128]{1,0:T(8,128)S(1)} %attend.1.own_ref), channel_id=1, source_target_pairs={{0,2},{2,0},{1,3},{3,1},{4,6},{6,4},{5,7},{7,5},{8,10},{10,8},{9,1... | collective-permute-start | bytes 798728 | tf_op jit(solution)/shard_map/ppermute | solution.py:454
  20.5 1.2 %collective-permute-done.6.other_ref = f32[520,128]{1,0:T(8,128)S(1)} collective-permute-done((f32[520,128]{1,0:T(8,128)S(1)}, f32[520,128]{1,0:T(8,128)S(1)}, u32[]{:S(2)}, u32[]{:S(2)}) %collective-permute-start.6) | collective-permute-done | bytes 266272 | tf_op jit(solution)/shard_map/ppermute | solution.py:454
  21.6 0.0 slice-done
  21.6 0.0 slice-done.1
  21.6 1.6 %output.1 = (f32[16,2048]{1,0:T(8,128)S(1)}, bf16[16,2048]{1,0:T(8,128)(2,1)S(1)}) custom-call(f32[520,128]{1,0:T(8,128)S(1)} %attend.1.own_ref, f32[520,128]{1,0:T(8,128)S(1)} %collective-permute-done.6.other_ref, bf16[2048,2048]{1,0:T(8,128)(2,1)S(1)} %bitcast.7), custom_call_target="tpu_custom_call" | custom-call | tf_op jit(solution)/shard_map/output/pallas_call | solution.py:458
  23.3 1.5 %collective-permute-start.7 = (bf16[16,2048]{1,0:T(8,128)(2,1)S(1)}, bf16[16,2048]{1,0:T(8,128)(2,1)S(1)}, u32[]{:S(2)}, u32[]{:S(2)}) collective-permute-start(bf16[16,2048]{1,0:T(8,128)(2,1)S(1)} %get-tuple-element.42), channel_id=1, source_target_pairs={{0,1},{1,0},{2,3},{3,2},{4,5},{5,4},{6,7},{7,6},{8,9},{9,8},{10,11... | collective-permute-start | bytes 196616 | tf_op jit(solution)/shard_map/ppermute | solution.py:470
  24.8 2.9 %collective-permute-done.7 = bf16[16,2048]{1,0:T(8,128)(2,1)S(1)} collective-permute-done((bf16[16,2048]{1,0:T(8,128)(2,1)S(1)}, bf16[16,2048]{1,0:T(8,128)(2,1)S(1)}, u32[]{:S(2)}, u32[]{:S(2)}) %collective-permute-start.7) | collective-permute-done | bytes 65568 | tf_op jit(solution)/shard_map/ppermute | solution.py:470
  27.7 0.6 %fusion = bf16[1,16,2048]{2,1,0:T(8,128)(2,1)} fusion(f32[16,2048]{1,0:T(8,128)S(1)} %get-tuple-element.41, bf16[16,2048]{1,0:T(8,128)(2,1)S(1)} %collective-permute-done.7), kind=kLoop, calls=%fused_computation.1 | loop fusion | flops 98304 | bytes 262144 | tf_op jit(solution)/shard_map/broadcast_in_dim | solution.py:471
  (2 shorter events, 0.0 us)
Async XLA Ops:
  0.0 2.3 %copy-start.4 = (s32[8,64]{1,0:T(8,128)S(1)}, s32[8,64]{1,0:T(8,128)}, u32[]{:S(2)}) copy-start(s32[8,64]{1,0:T(8,128)} %stretches_ref.1) | copy-start | bytes 6148
  0.0 2.3 %copy-start.5 = (s32[512]{0:T(512)S(1)}, s32[512]{0:T(512)}, u32[]{:S(2)}) copy-start(s32[512]{0:T(512)} %param.17) | copy-start | bytes 6148
  0.0 2.3 %copy-start.6 = (s32[8]{0:T(128)S(1)}, s32[8]{0:T(128)}, u32[]{:S(2)}) copy-start(s32[8]{0:T(128)} %counts_ref.1) | copy-start | bytes 100
  0.0 2.3 %copy-start.7 = (s32[1,32]{1,0:T(1,128)S(1)}, s32[1,32]{1,0:T(1,128)}, u32[]{:S(2)}) copy-start(s32[1,32]{1,0:T(1,128)} %positions_ref.1) | copy-start | bytes 388
  0.0 2.3 %copy-start.8 = (f32[1,128]{1,0:T(1,128)S(1)}, f32[1,128]{1,0:T(1,128)}, u32[]{:S(2)}) copy-start(f32[1,128]{1,0:T(1,128)} %constant.2.clone.freq_ref) | copy-start | bytes 1540
  0.0 13.0 %copy-start = (bf16[2048,2048]{1,0:T(8,128)(2,1)S(1)}, bf16[2048,2048]{1,0:T(8,128)(2,1)}, u32[]{:S(2)}) copy-start(bf16[2048,2048]{1,0:T(8,128)(2,1)} %wq_ref.1) | copy-start | bytes 25165828
  0.0 13.0 %copy-start.1 = (bf16[2048,512]{1,0:T(8,128)(2,1)S(1)}, bf16[2048,512]{1,0:T(8,128)(2,1)}, u32[]{:S(2)}) copy-start(bf16[2048,512]{1,0:T(8,128)(2,1)} %wk_ref.1) | copy-start | bytes 6291460
  0.0 13.0 %copy-start.2 = (bf16[2048,512]{1,0:T(8,128)(2,1)S(1)}, bf16[2048,512]{1,0:T(8,128)(2,1)}, u32[]{:S(2)}) copy-start(bf16[2048,512]{1,0:T(8,128)(2,1)} %wv_ref.1) | copy-start | bytes 6291460
  0.0 13.0 %copy-start.3 = (bf16[1,32,2048]{2,1,0:T(8,128)(2,1)S(1)}, bf16[1,32,2048]{2,1,0:T(8,128)(2,1)}, u32[]{:S(2)}) copy-start(bf16[1,32,2048]{2,1,0:T(8,128)(2,1)} %param.11) | copy-start | bytes 393220
  1.8 1.6 %collective-permute-start = (bf16[128,512]{1,0:T(8,128)(2,1)S(1)}, bf16[128,512]{1,0:T(8,128)(2,1)S(1)}, u32[]{:S(2)}, u32[]{:S(2)}) collective-permute-start(bf16[128,512]{1,0:T(8,128)(2,1)S(1)} %get-tuple-element.26), channel_id=1, source_target_pairs={{0,2},{2,0},{1,3},{3,1},{4,6},{6,4},{5,7},{7,5},{8,10},{10,8},{9,1... | collective-permute-start | bytes 393224 | tf_op jit(solution)/shard_map/ppermute | solution.py:403
  3.5 14.3 %collective-permute-start.1 = (bf16[128,512]{1,0:T(8,128)(2,1)S(1)}, bf16[128,512]{1,0:T(8,128)(2,1)S(1)}, u32[]{:S(2)}, u32[]{:S(2)}) collective-permute-start(bf16[128,512]{1,0:T(8,128)(2,1)S(1)} %get-tuple-element.30.after_ref), channel_id=1, source_target_pairs={{0,24},{2,18},{4,28},{6,22},{8,16},{10,26},{12,20},{14,30},{16,8},... | collective-permute-start | bytes 393224 | tf_op jit(solution)/shard_map/ppermute | solution.py:412
  8.3 9.5 %collective-permute-start.2 = (bf16[128,512]{1,0:T(8,128)(2,1)S(1)}, bf16[128,512]{1,0:T(8,128)(2,1)S(1)}, u32[]{:S(2)}, u32[]{:S(2)}) collective-permute-start(bf16[128,512]{1,0:T(8,128)(2,1)S(1)} %get-tuple-element.31), channel_id=1, source_target_pairs={{0,28},{2,22},{4,24},{6,18},{8,20},{10,30},{12,16},{14,26},{16,12}... | collective-permute-start | bytes 393224 | tf_op jit(solution)/shard_map/ppermute | solution.py:412
  9.5 8.3 %collective-permute-start.3 = (bf16[64,512]{1,0:T(8,128)(2,1)S(1)}, bf16[64,512]{1,0:T(8,128)(2,1)S(1)}, u32[]{:S(2)}, u32[]{:S(2)}) collective-permute-start(bf16[64,512]{1,0:T(8,128)(2,1)S(1)} %get-tuple-element.32), channel_id=1, source_target_pairs={{0,12},{4,8},{8,4},{12,0},{16,28},{20,24},{24,20},{28,16},{1,13},{... | collective-permute-start | bytes 196616 | tf_op jit(solution)/shard_map/ppermute | solution.py:414
  9.5 8.3 %collective-permute-start.4 = (bf16[64,512]{1,0:T(8,128)(2,1)S(1)}, bf16[64,512]{1,0:T(8,128)(2,1)S(1)}, u32[]{:S(2)}, u32[]{:S(2)}) collective-permute-start(bf16[64,512]{1,0:T(8,128)(2,1)S(1)} %get-tuple-element.33), channel_id=1, source_target_pairs={{0,8},{4,12},{8,0},{12,4},{16,24},{20,28},{24,16},{28,20},{1,9},{5... | collective-permute-start | bytes 196616 | tf_op jit(solution)/shard_map/ppermute | solution.py:414
  11.4 6.4 %collective-permute-start.5 = (bf16[64,512]{1,0:T(8,128)(2,1)S(1)}, bf16[64,512]{1,0:T(8,128)(2,1)S(1)}, u32[]{:S(2)}, u32[]{:S(2)}) collective-permute-start(bf16[64,512]{1,0:T(8,128)(2,1)S(1)} %get-tuple-element.34), channel_id=1, source_target_pairs={{0,4},{4,0},{8,12},{12,8},{16,20},{20,16},{24,28},{28,24},{1,5},{5... | collective-permute-start | bytes 196616 | tf_op jit(solution)/shard_map/ppermute | solution.py:414
  15.3 6.4 %slice-start = ((s8[8388608]{0:T(1024)(128)(4,1)}), s8[4194304]{0:T(1024)(128)(4,1)S(1)}, s32[]{:S(2)}) async-start(s8[8388608]{0:T(1024)(128)(4,1)} %bitcast.6), calls=%async_computation | async-start | bytes 8388608
  17.8 3.8 %slice-start.1 = ((s8[8388608]{0:T(1024)(128)(4,1)}), s8[4194304]{0:T(1024)(128)(4,1)S(1)}, s32[]{:S(2)}) async-start(s8[8388608]{0:T(1024)(128)(4,1)} %bitcast.6), calls=%async_computation.1 | async-start | bytes 8388608
  18.5 3.2 %collective-permute-start.6 = (f32[520,128]{1,0:T(8,128)S(1)}, f32[520,128]{1,0:T(8,128)S(1)}, u32[]{:S(2)}, u32[]{:S(2)}) collective-permute-start(f32[520,128]{1,0:T(8,128)S(1)} %attend.1.own_ref), channel_id=1, source_target_pairs={{0,2},{2,0},{1,3},{3,1},{4,6},{6,4},{5,7},{7,5},{8,10},{10,8},{9,1... | collective-permute-start | bytes 798728 | tf_op jit(solution)/shard_map/ppermute | solution.py:454
  23.3 4.4 %collective-permute-start.7 = (bf16[16,2048]{1,0:T(8,128)(2,1)S(1)}, bf16[16,2048]{1,0:T(8,128)(2,1)S(1)}, u32[]{:S(2)}, u32[]{:S(2)}) collective-permute-start(bf16[16,2048]{1,0:T(8,128)(2,1)S(1)} %get-tuple-element.42), channel_id=1, source_target_pairs={{0,1},{1,0},{2,3},{3,2},{4,5},{5,4},{6,7},{7,6},{8,9},{9,8},{10,11... | collective-permute-start | bytes 196616 | tf_op jit(solution)/shard_map/ppermute | solution.py:470

commit v5 on v4

--- a/solution.py
+++ b/solution.py
@@ -22,8 +22,21 @@
 SMEM = pl.BlockSpec(memory_space=pltpu.SMEM)
 
 
-def far_bits(i, row, slots):
-    return slots // 2 + i + (1 - row) * (slots // 4)
+def exchanges(slots):
+    if slots == 8:
+        return [4, 6, 3], [(7, 5), (2, 1)]
+    return [1], [(k, k - 1) for k in range(slots - 1, 1, -2)]
+
+
+def for_row(pair, row):
+    return pair[1] + (1 - row) * (pair[0] - pair[1])
+
+
+def arrivals(slots):
+    direct, shared = exchanges(slots)
+    blocks = [(k, k, 0) for k in direct]
+    blocks += [(*pair, flip) for pair in shared for flip in (0, 1)]
+    return blocks + [(0, 0, 0)]
 
 
 def iota(shape, dim):
@@ -71,11 +84,11 @@
         picked = jnp.where(rank == k, mine * local.astype(F32), 0.0)
         ids = jnp.where(lane == k, jnp.sum(picked, axis=1, keepdims=True), ids)
     ids_ref[...] = ids
+    direct, shared = exchanges(slots)
     ids = jnp.concatenate(
         [
             jnp.broadcast_to(ids_ref[pl.ds(slot ^ k, 1), :], (per_slot, 128))
-            for k in list(range(slots // 2))
-            + [far_bits(i, r, slots) for r in (row, 1 - row) for i in range(slots // 4)]
+            for k in direct + [0] + [for_row(pair, r) for r in (row, 1 - row) for pair in shared]
         ],
         axis=0,
     )
@@ -115,11 +128,29 @@
             base += step
 
 
+def sine_cosine(angle):
+    turns = jnp.floor(angle * (2.0 / math.pi) + 0.5)
+    rest = angle - turns * 1.5703125
+    rest = rest - turns * 4.837512969970703125e-4
+    rest = rest - turns * 7.54978995489188216e-8
+    square = rest * rest
+    sine = (-1.9515295891e-4 * square + 8.3321608736e-3) * square - 1.6666654611e-1
+    sine = sine * square * rest + rest
+    cosine = (2.443315711809948e-5 * square - 1.388731625493765e-3) * square
+    cosine = (cosine + 4.166664568298827e-2) * square * square - 0.5 * square + 1.0
+    quarter = turns.astype(jnp.int32) & 3
+    odd = (quarter & 1) == 1
+    sine, cosine = jnp.where(odd, cosine, sine), jnp.where(odd, sine, cosine)
+    sine = jnp.where(quarter >= 2, -sine, sine)
+    cosine = jnp.where(jnp.logical_or(quarter == 1, quarter == 2), -cosine, cosine)
+    return sine, cosine
+
+
 def angle_tables(shift, freq):
     angle = shift.astype(F32) * freq
     low = iota(angle.shape, 1) < HEAD_WIDTH // 2
-    sine = jnp.sin(angle)
-    return jnp.cos(angle), jnp.where(low, -sine, sine)
+    sine, cosine = sine_cosine(angle)
+    return cosine, jnp.where(low, -sine, sine)
 
 
 def rotated(vectors, cosine, sine):
@@ -152,28 +183,28 @@
     owner, _ = divide(stretches, tiles)
     slots = arriving // ranks
     place, rank_wanted = divide(iota((arriving, slot_tiles), 0), ranks)
-    near = place < slots // 2
-    beyond = place - slots // 2
-    from_slot = slot ^ jnp.where(near, place, far_bits(beyond >> 1, row, slots))
-    from_row = row ^ jnp.where(near, 0, beyond & 1)
+    bits, flip = jnp.zeros_like(place), jnp.zeros_like(place)
+    for i, (first, second, other) in enumerate(arrivals(slots)):
+        bits = jnp.where(place == i, for_row((first, second), row), bits)
+        flip = jnp.where(place == i, other, flip)
+    from_slot = slot ^ bits
+    from_row = row ^ flip
     match = (owner == from_slot * row_total + from_row).astype(F32)
     rank = earlier_count(match)
     picked = jnp.where(rank == rank_wanted.astype(F32), match, 0.0)
-    tile = jnp.sum(picked * iota((arriving, slot_tiles), 1).astype(F32), axis=1, keepdims=True)
-    stretch = jnp.sum(picked * stretches.astype(F32), axis=1, keepdims=True)
-    tile = tile.astype(jnp.int32)
-    stretch = stretch.astype(jnp.int32)
-    page_count = offsets_ref.shape[0]
-    page, lane = divide(stretch, 128)
-    in_lane = (iota((arriving, 128), 1) == lane).astype(BF16)
-    offsets = offsets_ref[...]
-    upper, lower = divide(offsets, 64)
-    nt = (((1,), (1,)), ((), ()))
-    upper = lax.dot_general(in_lane, upper.astype(BF16), nt, preferred_element_type=F32)
-    lower = lax.dot_general(in_lane, lower.astype(BF16), nt, preferred_element_type=F32)
-    in_page = (iota((arriving, page_count), 1) == page).astype(F32)
-    offset = jnp.sum(in_page * (upper * 64.0 + lower), axis=1, keepdims=True).astype(jnp.int32)
-    cosine, sine = angle_tables(tile * stretch_len - offset, freq)
+    tile_ids = iota((1, slot_tiles), 1).astype(F32)
+    tile = jnp.sum(picked * tile_ids, axis=1, keepdims=True)
+    page, lane = divide(stretches, 128)
+    in_lane = (iota((128, slot_tiles), 0) == lane).astype(F32).astype(BF16)
+    upper, lower = divide(offsets_ref[...], 64)
+    page_count = upper.shape[0]
+    split = jnp.concatenate([upper, lower], axis=0).astype(F32).astype(BF16)
+    split = jnp.dot(split, in_lane, preferred_element_type=F32)
+    offset = split[:page_count] * 64.0 + split[page_count:]
+    in_page = iota((page_count, slot_tiles), 0) == page
+    offset = jnp.sum(jnp.where(in_page, offset, 0.0), axis=0, keepdims=True)
+    shift = jnp.sum(picked * (tile_ids * stretch_len - offset), axis=1, keepdims=True)
+    cosine, sine = angle_tables(shift, freq)
     local_keys = arriving * stretch_len
     spread = lambda x: jnp.broadcast_to(
         x[:, None, :], (arriving, stretch_len, x.shape[1])
@@ -185,15 +216,18 @@
     positions = positions_ref[...]
     group = bias_ref.shape[1] // token_total
     query_positions = jnp.concatenate([positions] * group, axis=1)
-    wide = jnp.broadcast_to(tile, (arriving, 128))
-    _, token = divide(iota((local_keys, 1), 0), stretch_len)
-    key_positions = spread(wide)[:, :1] * stretch_len + token
-    redone = jnp.sum(
-        (key_positions == positions).astype(F32), axis=1, keepdims=True
-    )
+    first = jnp.broadcast_to(tile * stretch_len, (arriving, 128))
+    _, token = divide(iota((local_keys, 128), 0), stretch_len)
+    key_positions = spread(first).astype(jnp.int32) + token
+    redone = (key_positions[:, :token_total] == positions).astype(F32).astype(BF16)
+    redone = jnp.dot(redone, jnp.ones((token_total, 128), BF16), preferred_element_type=F32)
     usable = jnp.logical_and(key_positions < count * stretch_len, redone == 0.0)
     key_positions = jnp.where(usable, key_positions, FAR)
-    bias_ref[:local_keys, :] = jnp.where(key_positions <= query_positions, 0.0, NEGATIVE)
+    for start in range(0, bias_ref.shape[1], 128):
+        cols = slice(start, start + 128)
+        bias_ref[:local_keys, cols] = jnp.where(
+            key_positions <= query_positions[:, cols], 0.0, NEGATIVE
+        )
     square = iota((token_total, token_total), 0) == iota((token_total, token_total), 1)
     column = jnp.sum(
         jnp.where(square, positions.astype(F32), 0.0), axis=1, keepdims=True
@@ -212,9 +246,8 @@
     return kept
 
 
-def attend_kernel(stretch_rows, far_count, *refs):
+def attend_kernel(stretch_rows, *refs):
     *arrived, cos_ref, sin_ref, bias_ref, token_cos_ref, token_sin_ref, both_ref, out_ref = refs
-    arrived = arrived[far_count:][::-1] + arrived[:far_count]
     parts = [
         (ref, at) for ref in arrived for at in range(0, ref.shape[0], 2 * stretch_rows)
     ]
@@ -382,14 +415,14 @@
 
     store_shape = (tiles * 2 * stretch_len, key_columns)
     step = key_columns
-    half, quarter = slot_total // 2, slot_total // 4
+    direct, shared = exchanges(slot_total)
     block = jax.ShapeDtypeStruct((per_slot, key_columns), BF16)
     *outgoing, give = pl.pallas_call(
         functools.partial(pack_kernel, tiles, ranks, stretch_len),
-        out_shape=[block] * (half + quarter)
-        + [jax.ShapeDtypeStruct((quarter * per_slot, key_columns), BF16)],
+        out_shape=[block] * (len(direct) + 1 + len(shared))
+        + [jax.ShapeDtypeStruct((len(shared) * per_slot, key_columns), BF16)],
         in_specs=[HBM, HBM],
-        out_specs=[VMEM] * (half + quarter + 1),
+        out_specs=[VMEM] * (len(direct) + len(shared) + 2),
         scratch_shapes=[
             pltpu.VMEM(tile_stretch.shape, jnp.int32),
             pltpu.VMEM(store_shape, BF16),
@@ -400,20 +433,24 @@
         cost_estimate=cost(8),
         name="pack",
     )(in_hbm(tile_stretch), in_hbm(kv_store.reshape(store_shape)))
+    own_block, kept = outgoing[len(direct)], outgoing[len(direct) + 1 :]
     given = lax.ppermute(give, "row", swap)
-    *merged, near_blocks = merge(outgoing[half:], given, outgoing[1:half], grant)
-    far = []
-    for i in range(quarter):
+    early = [True for k in direct]
+    late_blocks = [outgoing[i] for i in range(len(direct)) if not early[i]]
+    *merged, late_blocks = merge(kept, given, late_blocks, grant)
+    late_blocks = iter(late_blocks)
+    arrived = []
+    for i, k in enumerate(direct):
+        sent = outgoing[i] if early[i] else next(late_blocks)
+        arrived.append(lax.ppermute(sent, "slot", [(s, s ^ k) for s in range(slot_total)]))
+    for sent, pair in zip(merged, shared):
         pairs = [
-            (s * row_total + r, (s ^ far_bits(i, r, slot_total)) * row_total + r)
+            (s * row_total + r, (s ^ pair[r]) * row_total + r)
             for s in range(slot_total)
             for r in range(row_total)
         ]
-        far.append(lax.ppermute(merged[i], ("slot", "row"), pairs))
-    near = [outgoing[0]] + [
-        lax.ppermute(near_blocks[k - 1], "slot", [(s, s ^ k) for s in range(slot_total)])
-        for k in range(1, half)
-    ]
+        arrived.append(lax.ppermute(sent, ("slot", "row"), pairs))
+    arrived.append(own_block)
 
     projected = pl.pallas_call(
         functools.partial(project_kernel, step),
@@ -443,14 +480,14 @@
     )(tile_stretch, stretch_offset.reshape(-1, 128), slot_count, recomp_pos, freq)
 
     partial = pl.pallas_call(
-        functools.partial(attend_kernel, ranks * stretch_len, quarter),
+        functools.partial(attend_kernel, ranks * stretch_len),
         out_shape=jax.ShapeDtypeStruct((key_heads * HEAD_WIDTH + 2 * key_heads, query_rows), F32),
-        in_specs=[VMEM] * (quarter + half + 6),
+        in_specs=[VMEM] * (len(direct) + len(shared) + 7),
         out_specs=VMEM,
         compiler_params=params(grant),
         cost_estimate=cost(8),
         name="attend",
-    )(*far, *reversed(near), *tables, both)
+    )(*arrived, *tables, both)
     partial_other = lax.ppermute(partial, "row", swap)
 
     out_columns = w_out.shape[1]

time: 28.5 us -> 27.5 us (0.965)
  starting transfers between devices: 13.6 us -> 11.7 us
  waiting for transfers between devices: 4.05 us -> 5.11 us
    ppermute x1, starting transfers between devices: 1.99 us -> 0.07 us  [on_device(): partial_other = lax.ppermute(partial, 'row', swap)]
    ppermute x5, waiting for transfers between devices: 0.01 us -> 0.85 us  [the longest x2 0.85 us: on_device(): arrived.append(lax.ppermute(sent, ('slot', 'row'), pairs))]
    ppermute x1, waiting for transfers between devices: 1.17 us -> 1.53 us  [on_device(): partial_other = lax.ppermute(partial, 'row', swap)]
  transfers between devices with their start and end apart: 8 -> 8, of which waited for: 2 -> 4; matrix products, arithmetic and copies ran while one was open for 0% -> 0% of each run, Pallas kernels for 12% -> 12%
where the time goes in v5:
time: 27.5 us; the launch traced here: 27.3 us
  starting transfers between devices  11.7 us (43%)
  Pallas kernels  7.2 us (26%)
  waiting for transfers between devices  5.11 us (19%)
  blocking collectives  2.5 us (9%)
  other arithmetic  0.64 us (2%)
    ppermute x3, starting transfers between devices, on_device(): lax.ppermute(sent, 'slot', [(s, s ^ k) for s in range(slot_total)])  6.2 us
    ppermute x2, starting transfers between devices, on_device(): arrived.append(lax.ppermute(sent, ('slot', 'row'), pairs))  3.38 us
    ppermute x1, waiting for transfers between devices, on_device(): received = lax.ppermute(send, 'col', swap)  2.73 us
    all_gather x1, blocking collectives, on_device(): both = lax.all_gather(projected, 'row')  2.5 us
    pallas_call x1, Pallas kernels, on_device(): pl.pallas_call(functools.partial(project_kernel, step), out_shape=jax.Sha...  2.24 us
    pallas_call x1, Pallas kernels, on_device(): pl.pallas_call(functools.partial(pack_kernel, tiles, ranks, stretch_len),...  1.72 us
    pallas_call x1, Pallas kernels, on_device(): pl.pallas_call(functools.partial(output_kernel, step, key_heads), out_sha...  1.64 us
    ppermute x1, starting transfers between devices, on_device(): received = lax.ppermute(send, 'col', swap)  1.55 us
  transfers between devices with their start and end apart: 8, of which 4 were waited for; matrix products, arithmetic and copies ran while one was open for 0% of the time, Pallas kernels for 12%

profile of v5, /device:TPU:0, one launch (start us, length us, event | category | flops | bytes accessed | tf_op | source)
XLA Modules:
  0.0 27.3 jit_solution(17235449992885857036)
XLA Ops:
  0.0 0.0 copy-start.4
  0.0 0.0 copy-start.5
  0.0 0.0 copy-start.6
  0.0 0.0 copy-start.7
  0.0 0.0 copy-start.8
  0.0 0.0 copy-start
  0.0 0.0 copy-start.1
  0.0 0.0 copy-start.2
  0.0 0.0 copy-start.3
  0.1 1.7 %pack.1 = (bf16[64,512]{1,0:T(8,128)(2,1)S(1)}, bf16[64,512]{1,0:T(8,128)(2,1)S(1)}, bf16[64,512]{1,0:T(8,128)(2,1)S(1)}, bf16[64,512]{1,0:T(8,128)(2,1)S(1)}, b...) custom-call(s32[8,64]{1,0:T(8,128)} %stretches_ref.1, bf16[512,512]{1,0:T(8,128)(2,1)} %bitcast.11), custom_call_target="tpu_custom_call" | custom-call | flops 8000000000 | bytes 1000 | tf_op jit(solution)/shard_map/pack/pallas_call | solution.py:420
  1.8 0.5 %collective-permute-start.3 = (bf16[128,512]{1,0:T(8,128)(2,1)S(1)}, bf16[128,512]{1,0:T(8,128)(2,1)S(1)}, u32[]{:S(2)}, u32[]{:S(2)}) collective-permute-start(bf16[128,512]{1,0:T(8,128)(2,1)S(1)} %get-tuple-element.26), channel_id=1, source_target_pairs={{0,2},{2,0},{1,3},{3,1},{4,6},{6,4},{5,7},{7,5},{8,10},{10,8},{9,1... | collective-permute-start | bytes 393224 | tf_op jit(solution)/shard_map/ppermute | solution.py:437
  2.3 3.7 %collective-permute-start = (bf16[64,512]{1,0:T(8,128)(2,1)S(1)}, bf16[64,512]{1,0:T(8,128)(2,1)S(1)}, u32[]{:S(2)}, u32[]{:S(2)}) collective-permute-start(bf16[64,512]{1,0:T(8,128)(2,1)S(1)} %get-tuple-element.21), channel_id=1, source_target_pairs={{0,16},{4,20},{8,24},{12,28},{16,0},{20,4},{24,8},{28,12},{1,17},{... | collective-permute-start | bytes 196616 | tf_op jit(solution)/shard_map/ppermute | solution.py:445
  6.0 1.3 %collective-permute-start.1 = (bf16[64,512]{1,0:T(8,128)(2,1)S(1)}, bf16[64,512]{1,0:T(8,128)(2,1)S(1)}, u32[]{:S(2)}, u32[]{:S(2)}) collective-permute-start(bf16[64,512]{1,0:T(8,128)(2,1)S(1)} %get-tuple-element.22), channel_id=1, source_target_pairs={{0,24},{4,28},{8,16},{12,20},{16,8},{20,12},{24,0},{28,4},{1,25},{... | collective-permute-start | bytes 196616 | tf_op jit(solution)/shard_map/ppermute | solution.py:445
  7.3 1.2 %collective-permute-start.2 = (bf16[64,512]{1,0:T(8,128)(2,1)S(1)}, bf16[64,512]{1,0:T(8,128)(2,1)S(1)}, u32[]{:S(2)}, u32[]{:S(2)}) collective-permute-start(bf16[64,512]{1,0:T(8,128)(2,1)S(1)} %get-tuple-element.23), channel_id=1, source_target_pairs={{0,12},{4,8},{8,4},{12,0},{16,28},{20,24},{24,20},{28,16},{1,13},{... | collective-permute-start | bytes 196616 | tf_op jit(solution)/shard_map/ppermute | solution.py:445
  8.5 0.0 copy-done.4
  8.5 0.0 copy-done.5
  8.5 0.0 copy-done.6
  8.5 0.0 copy-done.7
  8.5 0.0 copy-done.8
  8.5 0.9 %tables.1 = (f32[256,128]{1,0:T(8,128)S(1)}, f32[256,128]{1,0:T(8,128)S(1)}, f32[272,128]{1,0:T(8,128)S(1)}, f32[32,128]{1,0:T(8,128)S(1)}, f32[32,128]{1,0:T(8,128)S(1)}) custom-call(s32[8,64]{1,0:T(8,128)S(1)} %copy-done.4, s32[4,128]{1,0:T(4,128)S(1)} %bitcast.10, s32[8]{0:T(128)S(1)} %copy-done.6, s32[1,32]{1,0:T(1,128)S(1)} %copy-done.7, ...), custom_call_target="tpu_custom_call" | custom-call | bytes 1000 | tf_op jit(solution)/shard_map/tables/pallas_call | solution.py:466
  9.5 0.0 collective-permute-done.3.refs_2_
  9.5 2.9 %collective-permute-start.4 = (bf16[128,512]{1,0:T(8,128)(2,1)S(1)}, bf16[128,512]{1,0:T(8,128)(2,1)S(1)}, u32[]{:S(2)}, u32[]{:S(2)}) collective-permute-start(bf16[128,512]{1,0:T(8,128)(2,1)S(1)} %get-tuple-element.27.after_ref), channel_id=1, source_target_pairs={{0,28},{2,22},{4,24},{6,18},{8,20},{10,30},{12,16},{14,26},{16,12}... | collective-permute-start | bytes 393224 | tf_op jit(solution)/shard_map/ppermute | solution.py:452
  12.4 0.5 %collective-permute-start.5 = (bf16[128,512]{1,0:T(8,128)(2,1)S(1)}, bf16[128,512]{1,0:T(8,128)(2,1)S(1)}, u32[]{:S(2)}, u32[]{:S(2)}) collective-permute-start(bf16[128,512]{1,0:T(8,128)(2,1)S(1)} %get-tuple-element.28), channel_id=1, source_target_pairs={{0,8},{2,6},{4,12},{6,2},{8,0},{10,14},{12,4},{14,10},{16,24},{18,... | collective-permute-start | bytes 393224 | tf_op jit(solution)/shard_map/ppermute | solution.py:452
  12.9 0.0 copy-done
  12.9 0.0 copy-done.1
  12.9 0.0 copy-done.2
  12.9 0.0 copy-done.3
  12.9 2.2 %project.1 = f32[32,3072]{1,0:T(8,128)S(1)} custom-call(bf16[128,512]{1,0:T(8,128)(2,1)S(1)} %get-tuple-element.27.after_ref, bf16[32,2048]{1,0:T(8,128)(2,1)S(1)} %bitcast.9, bf16[2048,2048]{1,0:T(8,128)(2,1)S(1)} %copy-done, bf16[2048,512]{1,0:T(8,128)(2,1)S(1)} %copy-done.1, bf16[2048,512]{1,0:T(8,128)(2,1)S(1)} %copy-done.2), custom_call_target="tpu_custom_call" | custom-call | bytes 1000 | tf_op jit(solution)/shard_map/project/pallas_call | solution.py:455
  15.2 0.0 slice-start
  15.2 2.5 %all-gather = f32[64,3072]{1,0:T(8,128)S(1)} all-gather(f32[32,3072]{1,0:T(8,128)S(1)} %project.1), channel_id=2, replica_groups=mesh['slot'=8,'row'=2,'col'=2] {'row'}, dimensions={0}, use_global_device_ids=true | all-gather | bytes 1179648 | tf_op jit(solution)/shard_map/all_gather | solution.py:464
  17.7 0.0 collective-permute-done.refs_0_
  17.7 0.0 collective-permute-done.1.refs_1_
  17.7 0.0 collective-permute-done.2.refs_2_
  17.7 0.1 collective-permute-done.4.refs_3_
  17.8 0.7 %collective-permute-done.5.refs_4_ = bf16[128,512]{1,0:T(8,128)(2,1)S(1)} collective-permute-done((bf16[128,512]{1,0:T(8,128)(2,1)S(1)}, bf16[128,512]{1,0:T(8,128)(2,1)S(1)}, u32[]{:S(2)}, u32[]{:S(2)}) %collective-permute-start.5) | collective-permute-done | bytes 131104 | tf_op jit(solution)/shard_map/ppermute | solution.py:452
  18.5 0.0 slice-start.1
  18.5 0.6 %attend.1.own_ref = f32[520,128]{1,0:T(8,128)S(1)} custom-call(bf16[64,512]{1,0:T(8,128)(2,1)S(1)} %collective-permute-done.refs_0_, bf16[64,512]{1,0:T(8,128)(2,1)S(1)} %collective-permute-done.1.refs_1_, bf16[64,512]{1,0:T(8,128)(2,1)S(1)} %collective-permute-done.2.refs_2_, bf16[128,512]{1,0:T(8,128)(2,1)S(1)} %collective-permute-done.4.refs_3_, ...), custom_call_target="tpu_custom_call" | custom-call | flops 8000000000 | bytes 1000 | tf_op jit(solution)/shard_map/attend/pallas_call | solution.py:482
  19.2 0.1 collective-permute-start.6
  19.2 1.5 %collective-permute-done.6.other_ref = f32[520,128]{1,0:T(8,128)S(1)} collective-permute-done((f32[520,128]{1,0:T(8,128)S(1)}, f32[520,128]{1,0:T(8,128)S(1)}, u32[]{:S(2)}, u32[]{:S(2)}) %collective-permute-start.6) | collective-permute-done | bytes 266272 | tf_op jit(solution)/shard_map/ppermute | solution.py:491
  20.8 0.0 slice-done
  20.8 0.0 slice-done.1
  20.8 1.6 %output.1 = (f32[16,2048]{1,0:T(8,128)S(1)}, bf16[16,2048]{1,0:T(8,128)(2,1)S(1)}) custom-call(f32[520,128]{1,0:T(8,128)S(1)} %attend.1.own_ref, f32[520,128]{1,0:T(8,128)S(1)} %collective-permute-done.6.other_ref, bf16[2048,2048]{1,0:T(8,128)(2,1)S(1)} %bitcast.7), custom_call_target="tpu_custom_call" | custom-call | tf_op jit(solution)/shard_map/output/pallas_call | solution.py:495
  22.4 1.6 %collective-permute-start.7 = (bf16[16,2048]{1,0:T(8,128)(2,1)S(1)}, bf16[16,2048]{1,0:T(8,128)(2,1)S(1)}, u32[]{:S(2)}, u32[]{:S(2)}) collective-permute-start(bf16[16,2048]{1,0:T(8,128)(2,1)S(1)} %get-tuple-element.36), channel_id=1, source_target_pairs={{0,1},{1,0},{2,3},{3,2},{4,5},{5,4},{6,7},{7,6},{8,9},{9,8},{10,11... | collective-permute-start | bytes 196616 | tf_op jit(solution)/shard_map/ppermute | solution.py:507
  24.0 2.7 %collective-permute-done.7 = bf16[16,2048]{1,0:T(8,128)(2,1)S(1)} collective-permute-done((bf16[16,2048]{1,0:T(8,128)(2,1)S(1)}, bf16[16,2048]{1,0:T(8,128)(2,1)S(1)}, u32[]{:S(2)}, u32[]{:S(2)}) %collective-permute-start.7) | collective-permute-done | bytes 65568 | tf_op jit(solution)/shard_map/ppermute | solution.py:507
  26.7 0.6 %fusion = bf16[1,16,2048]{2,1,0:T(8,128)(2,1)} fusion(f32[16,2048]{1,0:T(8,128)S(1)} %get-tuple-element.35, bf16[16,2048]{1,0:T(8,128)(2,1)S(1)} %collective-permute-done.7), kind=kLoop, calls=%fused_computation.1 | loop fusion | flops 98304 | bytes 262144 | tf_op jit(solution)/shard_map/broadcast_in_dim | solution.py:508
  (2 shorter events, 0.0 us)
Async XLA Ops:
  0.0 8.5 %copy-start.4 = (s32[8,64]{1,0:T(8,128)S(1)}, s32[8,64]{1,0:T(8,128)}, u32[]{:S(2)}) copy-start(s32[8,64]{1,0:T(8,128)} %stretches_ref.1) | copy-start | bytes 6148
  0.0 8.5 %copy-start.5 = (s32[512]{0:T(512)S(1)}, s32[512]{0:T(512)}, u32[]{:S(2)}) copy-start(s32[512]{0:T(512)} %param.17) | copy-start | bytes 6148
  0.0 8.5 %copy-start.6 = (s32[8]{0:T(128)S(1)}, s32[8]{0:T(128)}, u32[]{:S(2)}) copy-start(s32[8]{0:T(128)} %counts_ref.1) | copy-start | bytes 100
  0.0 8.5 %copy-start.7 = (s32[1,32]{1,0:T(1,128)S(1)}, s32[1,32]{1,0:T(1,128)}, u32[]{:S(2)}) copy-start(s32[1,32]{1,0:T(1,128)} %positions_ref.1) | copy-start | bytes 388
  0.0 8.5 %copy-start.8 = (f32[1,128]{1,0:T(1,128)S(1)}, f32[1,128]{1,0:T(1,128)}, u32[]{:S(2)}) copy-start(f32[1,128]{1,0:T(1,128)} %constant.2.clone.freq_ref) | copy-start | bytes 1540
  0.0 12.9 %copy-start = (bf16[2048,2048]{1,0:T(8,128)(2,1)S(1)}, bf16[2048,2048]{1,0:T(8,128)(2,1)}, u32[]{:S(2)}) copy-start(bf16[2048,2048]{1,0:T(8,128)(2,1)} %wq_ref.1) | copy-start | bytes 25165828
  0.0 12.9 %copy-start.1 = (bf16[2048,512]{1,0:T(8,128)(2,1)S(1)}, bf16[2048,512]{1,0:T(8,128)(2,1)}, u32[]{:S(2)}) copy-start(bf16[2048,512]{1,0:T(8,128)(2,1)} %wk_ref.1) | copy-start | bytes 6291460
  0.0 12.9 %copy-start.2 = (bf16[2048,512]{1,0:T(8,128)(2,1)S(1)}, bf16[2048,512]{1,0:T(8,128)(2,1)}, u32[]{:S(2)}) copy-start(bf16[2048,512]{1,0:T(8,128)(2,1)} %wv_ref.1) | copy-start | bytes 6291460
  0.0 12.9 %copy-start.3 = (bf16[1,32,2048]{2,1,0:T(8,128)(2,1)S(1)}, bf16[1,32,2048]{2,1,0:T(8,128)(2,1)}, u32[]{:S(2)}) copy-start(bf16[1,32,2048]{2,1,0:T(8,128)(2,1)} %param.11) | copy-start | bytes 393220
  1.8 7.7 %collective-permute-start.3 = (bf16[128,512]{1,0:T(8,128)(2,1)S(1)}, bf16[128,512]{1,0:T(8,128)(2,1)S(1)}, u32[]{:S(2)}, u32[]{:S(2)}) collective-permute-start(bf16[128,512]{1,0:T(8,128)(2,1)S(1)} %get-tuple-element.26), channel_id=1, source_target_pairs={{0,2},{2,0},{1,3},{3,1},{4,6},{6,4},{5,7},{7,5},{8,10},{10,8},{9,1... | collective-permute-start | bytes 393224 | tf_op jit(solution)/shard_map/ppermute | solution.py:437
  2.3 15.3 %collective-permute-start = (bf16[64,512]{1,0:T(8,128)(2,1)S(1)}, bf16[64,512]{1,0:T(8,128)(2,1)S(1)}, u32[]{:S(2)}, u32[]{:S(2)}) collective-permute-start(bf16[64,512]{1,0:T(8,128)(2,1)S(1)} %get-tuple-element.21), channel_id=1, source_target_pairs={{0,16},{4,20},{8,24},{12,28},{16,0},{20,4},{24,8},{28,12},{1,17},{... | collective-permute-start | bytes 196616 | tf_op jit(solution)/shard_map/ppermute | solution.py:445
  6.0 11.7 %collective-permute-start.1 = (bf16[64,512]{1,0:T(8,128)(2,1)S(1)}, bf16[64,512]{1,0:T(8,128)(2,1)S(1)}, u32[]{:S(2)}, u32[]{:S(2)}) collective-permute-start(bf16[64,512]{1,0:T(8,128)(2,1)S(1)} %get-tuple-element.22), channel_id=1, source_target_pairs={{0,24},{4,28},{8,16},{12,20},{16,8},{20,12},{24,0},{28,4},{1,25},{... | collective-permute-start | bytes 196616 | tf_op jit(solution)/shard_map/ppermute | solution.py:445
  7.3 10.3 %collective-permute-start.2 = (bf16[64,512]{1,0:T(8,128)(2,1)S(1)}, bf16[64,512]{1,0:T(8,128)(2,1)S(1)}, u32[]{:S(2)}, u32[]{:S(2)}) collective-permute-start(bf16[64,512]{1,0:T(8,128)(2,1)S(1)} %get-tuple-element.23), channel_id=1, source_target_pairs={{0,12},{4,8},{8,4},{12,0},{16,28},{20,24},{24,20},{28,16},{1,13},{... | collective-permute-start | bytes 196616 | tf_op jit(solution)/shard_map/ppermute | solution.py:445
  9.5 8.3 %collective-permute-start.4 = (bf16[128,512]{1,0:T(8,128)(2,1)S(1)}, bf16[128,512]{1,0:T(8,128)(2,1)S(1)}, u32[]{:S(2)}, u32[]{:S(2)}) collective-permute-start(bf16[128,512]{1,0:T(8,128)(2,1)S(1)} %get-tuple-element.27.after_ref), channel_id=1, source_target_pairs={{0,28},{2,22},{4,24},{6,18},{8,20},{10,30},{12,16},{14,26},{16,12}... | collective-permute-start | bytes 393224 | tf_op jit(solution)/shard_map/ppermute | solution.py:452
  12.4 6.1 %collective-permute-start.5 = (bf16[128,512]{1,0:T(8,128)(2,1)S(1)}, bf16[128,512]{1,0:T(8,128)(2,1)S(1)}, u32[]{:S(2)}, u32[]{:S(2)}) collective-permute-start(bf16[128,512]{1,0:T(8,128)(2,1)S(1)} %get-tuple-element.28), channel_id=1, source_target_pairs={{0,8},{2,6},{4,12},{6,2},{8,0},{10,14},{12,4},{14,10},{16,24},{18,... | collective-permute-start | bytes 393224 | tf_op jit(solution)/shard_map/ppermute | solution.py:452
  15.2 5.6 %slice-start = ((s8[8388608]{0:T(1024)(128)(4,1)}), s8[4194304]{0:T(1024)(128)(4,1)S(1)}, s32[]{:S(2)}) async-start(s8[8388608]{0:T(1024)(128)(4,1)} %bitcast.6), calls=%async_computation | async-start | bytes 8388608
  18.5 2.3 %slice-start.1 = ((s8[8388608]{0:T(1024)(128)(4,1)}), s8[4194304]{0:T(1024)(128)(4,1)S(1)}, s32[]{:S(2)}) async-start(s8[8388608]{0:T(1024)(128)(4,1)} %bitcast.6), calls=%async_computation.1 | async-start | bytes 8388608
  19.2 1.6 %collective-permute-start.6 = (f32[520,128]{1,0:T(8,128)S(1)}, f32[520,128]{1,0:T(8,128)S(1)}, u32[]{:S(2)}, u32[]{:S(2)}) collective-permute-start(f32[520,128]{1,0:T(8,128)S(1)} %attend.1.own_ref), channel_id=1, source_target_pairs={{0,2},{2,0},{1,3},{3,1},{4,6},{6,4},{5,7},{7,5},{8,10},{10,8},{9,1... | collective-permute-start | bytes 798728 | tf_op jit(solution)/shard_map/ppermute | solution.py:491
  22.4 4.3 %collective-permute-start.7 = (bf16[16,2048]{1,0:T(8,128)(2,1)S(1)}, bf16[16,2048]{1,0:T(8,128)(2,1)S(1)}, u32[]{:S(2)}, u32[]{:S(2)}) collective-permute-start(bf16[16,2048]{1,0:T(8,128)(2,1)S(1)} %get-tuple-element.36), channel_id=1, source_target_pairs={{0,1},{1,0},{2,3},{3,2},{4,5},{5,4},{6,7},{7,6},{8,9},{9,8},{10,11... | collective-permute-start | bytes 196616 | tf_op jit(solution)/shard_map/ppermute | solution.py:507

commit v6 on v5

--- a/solution.py
+++ b/solution.py
@@ -24,7 +24,7 @@
 
 def exchanges(slots):
     if slots == 8:
-        return [4, 6, 3], [(7, 5), (2, 1)]
+        return [4, 6, 3], [(2, 1), (7, 5)]
     return [1], [(k, k - 1) for k in range(slots - 1, 1, -2)]
 
 
@@ -34,9 +34,8 @@
 
 def arrivals(slots):
     direct, shared = exchanges(slots)
-    blocks = [(k, k, 0) for k in direct]
-    blocks += [(*pair, flip) for pair in shared for flip in (0, 1)]
-    return blocks + [(0, 0, 0)]
+    blocks = [(k, k, 0) for k in direct + [0]]
+    return blocks + [(*pair, flip) for pair in shared for flip in (0, 1)]
 
 
 def iota(shape, dim):
@@ -246,93 +245,142 @@
     return kept
 
 
-def attend_kernel(stretch_rows, *refs):
-    *arrived, cos_ref, sin_ref, bias_ref, token_cos_ref, token_sin_ref, both_ref, out_ref = refs
-    parts = [
-        (ref, at) for ref in arrived for at in range(0, ref.shape[0], 2 * stretch_rows)
-    ]
+def block_parts(blocks, stretch_rows):
+    return [(ref, at) for ref in blocks for at in range(0, ref.shape[0], 2 * stretch_rows)]
+
+
+def keys_of(parts, stretch_rows, cols, cosine, sine):
+    keys = jnp.concatenate([ref[at : at + stretch_rows, cols] for ref, at in parts], axis=0)
+    return rotated(keys.astype(F32), cosine, sine).astype(BF16)
+
+
+def values_of(parts, stretch_rows, cols):
+    return [ref[at + stretch_rows : at + 2 * stretch_rows, cols] for ref, at in parts]
+
+
+def scores_of(keys, queries, bias):
+    nt = (((1,), (1,)), ((), ()))
+    scores = lax.dot_general(keys, queries, nt, preferred_element_type=F32)
+    return scores * (1.0 / math.sqrt(HEAD_WIDTH)) + bias
+
+
+def queries_kernel(stretch_rows, *refs):
+    *arrived, cos_ref, sin_ref, bias_ref, token_cos_ref, token_sin_ref, both_ref = refs[:-3]
+    q_ref, scores_ref, values_ref = refs[-3:]
+    parts = block_parts(arrived, stretch_rows)
     row = lax.axis_index("row")
     token_total = token_cos_ref.shape[0]
-    share = bias_ref.shape[0] - cos_ref.shape[0]
-    group = bias_ref.shape[1] // token_total
+    local_keys = cos_ref.shape[0]
+    share, count = values_ref.shape[0], len(parts) * stretch_rows
+    query_rows = bias_ref.shape[1]
+    group = query_rows // token_total
     key_columns = arrived[0].shape[1]
     key_heads = key_columns // HEAD_WIDTH
     query_columns = group * key_columns
-    scale = 1.0 / math.sqrt(HEAD_WIDTH)
-    cosine = cos_ref[...]
-    sine = sin_ref[...]
-    token_cosine = token_cos_ref[...]
-    token_sine = token_sin_ref[...]
-    bias = bias_ref[...]
-
-    def projected(start):
-        cols = slice(start, start + HEAD_WIDTH)
+    cosine, sine = cos_ref[:count, :], sin_ref[:count, :]
+    token_cosine, token_sine = token_cos_ref[...], token_sin_ref[...]
+    bias = jnp.concatenate([bias_ref[:count, :], bias_ref[local_keys:, :]], axis=0)
+
+    def projected(start, width=HEAD_WIDTH):
+        cols = slice(start, start + width)
         return both_ref[0, :, cols] + both_ref[1, :, cols]
 
+    all_queries, all_scores = [], []
+    for head in range(key_heads):
+        at = head * HEAD_WIDTH
+        queries = [
+            rotated(projected((head * group + j) * HEAD_WIDTH), token_cosine, token_sine)
+            for j in range(group)
+        ]
+        queries = jnp.concatenate(queries, axis=0).astype(BF16)
+        new_keys = rotated(projected(query_columns + at), token_cosine, token_sine)
+        keys = keys_of(parts, stretch_rows, slice(at, at + HEAD_WIDTH), cosine, sine)
+        keys = jnp.concatenate([keys, of_row(new_keys, row, share).astype(BF16)], axis=0)
+        all_queries.append(queries)
+        all_scores.append(scores_of(keys, queries, bias))
+    new_values = projected(query_columns + key_columns, key_columns)
+    values_ref[...] = of_row(new_values, row, share).astype(BF16)
+    for head in range(key_heads):
+        q_ref[head * query_rows : (head + 1) * query_rows, :] = all_queries[head]
+        scores_ref[head * (count + share) : (head + 1) * (count + share), :] = all_scores[head]
+
+
+def attend_kernel(stretch_rows, first_blocks, *refs):
+    *arrived, cos_ref, sin_ref, bias_ref, q_ref, scores_ref, values_ref, out_ref, send_ref = refs
+    first = block_parts(arrived[:first_blocks], stretch_rows)
+    later = block_parts(arrived[first_blocks:], stretch_rows)
+    count, local_keys = len(first) * stretch_rows, cos_ref.shape[0]
+    known = count + values_ref.shape[0]
+    query_rows = bias_ref.shape[1]
+    key_heads = arrived[0].shape[1] // HEAD_WIDTH
+    cosine, sine = cos_ref[count:, :], sin_ref[count:, :]
+    bias = bias_ref[count:local_keys, :]
     all_scores, all_values = [], []
     for head in range(key_heads):
-        at = head * HEAD_WIDTH
-        cols = slice(at, at + HEAD_WIDTH)
-        queries = jnp.concatenate(
-            [
-                rotated(projected((head * group + j) * HEAD_WIDTH), token_cosine, token_sine)
-                for j in range(group)
-            ],
-            axis=0,
-        ).astype(BF16)
-        new_keys = rotated(projected(query_columns + at), token_cosine, token_sine)
-        new_values = projected(query_columns + key_columns + at)
-        keys = jnp.concatenate([ref[at : at + stretch_rows, cols] for ref, at in parts], axis=0)
-        keys = rotated(keys.astype(F32), cosine, sine).astype(BF16)
-        keys = jnp.concatenate([keys, of_row(new_keys, row, share).astype(BF16)], axis=0)
-        values = [
-            ref[at + stretch_rows : at + 2 * stretch_rows, cols] for ref, at in parts
-        ]
-        all_values.append(
-            jnp.concatenate(values + [of_row(new_values, row, share).astype(BF16)], axis=0)
-        )
-        all_scores.append(
-            lax.dot_general(
-                keys, queries, (((1,), (1,)), ((), ())), preferred_element_type=F32
-            )
-        )
+        cols = slice(head * HEAD_WIDTH, (head + 1) * HEAD_WIDTH)
+        keys = keys_of(later, stretch_rows, cols, cosine, sine)
+        queries = q_ref[head * query_rows : (head + 1) * query_rows, :]
+        scores = [scores_ref[head * known : (head + 1) * known, :]]
+        scores.append(scores_of(keys, queries, bias))
+        all_scores.append(jnp.concatenate(scores, axis=0))
+        values = values_of(first, stretch_rows, cols) + [values_ref[:, cols]]
+        values += values_of(later, stretch_rows, cols)
+        all_values.append(jnp.concatenate(values, axis=0))
     all_probs = []
-    base = key_heads * HEAD_WIDTH
-    for head, scores in enumerate(all_scores):
-        scores = scores * scale + bias
+    stats = []
+    for scores in all_scores:
         peak = jnp.max(scores, axis=0, keepdims=True)
         probs = jnp.exp(scores - peak)
-        out_ref[base + head : base + head + 1, :] = peak
-        out_ref[base + key_heads + head : base + key_heads + head + 1, :] = jnp.sum(
-            probs, axis=0, keepdims=True
-        )
+        stats.append((peak, jnp.sum(probs, axis=0, keepdims=True)))
         all_probs.append(probs.astype(BF16))
+    stats = jnp.concatenate([x[0] for x in stats] + [x[1] for x in stats], axis=0)
+    base = key_heads * HEAD_WIDTH
+    out_ref[base:, :] = stats
+    for part in range(3):
+        term = stats.astype(BF16)
+        at = base + 16 * part
+        send_ref[at : at + 16, :] = jnp.concatenate(
+            [term.astype(F32), jnp.zeros_like(stats)], axis=0
+        ).astype(BF16)
+        stats = stats - term.astype(F32)
     for head in range(key_heads):
-        out_ref[head * HEAD_WIDTH : (head + 1) * HEAD_WIDTH, :] = lax.dot_general(
+        weighted = lax.dot_general(
             all_values[head], all_probs[head], (((0,), (0,)), ((), ())), preferred_element_type=F32
         )
+        rows = slice(head * HEAD_WIDTH, (head + 1) * HEAD_WIDTH)
+        out_ref[rows, :] = weighted
+        send_ref[rows, :] = weighted.astype(BF16)
 
 
 def output_kernel(step, key_heads, own_ref, other_ref, w_ref, keep_ref, send_ref, attended):
     token_total = attended.shape[0]
     group = own_ref.shape[1] // token_total
     base = key_heads * HEAD_WIDTH
+    results = []
+    own_stats = own_ref[base:, :]
+    terms = [
+        other_ref[base + 16 * part : base + 16 * (part + 1), :].astype(F32) for part in range(3)
+    ]
+    other_stats = (terms[0] + terms[1] + terms[2])[: 2 * key_heads]
+    peaks = jnp.maximum(own_stats[:key_heads], other_stats[:key_heads])
+    own_scales = jnp.exp(own_stats[:key_heads] - peaks)
+    other_scales = jnp.exp(other_stats[:key_heads] - peaks)
+    totals = own_stats[key_heads:] * own_scales + other_stats[key_heads:] * other_scales
     for head in range(key_heads):
         rows = slice(head * HEAD_WIDTH, (head + 1) * HEAD_WIDTH)
-        at_peak = slice(base + head, base + head + 1)
-        at_total = slice(base + key_heads + head, base + key_heads + head + 1)
-        peak = jnp.maximum(own_ref[at_peak, :], other_ref[at_peak, :])
-        own_scale = jnp.exp(own_ref[at_peak, :] - peak)
-        other_scale = jnp.exp(other_ref[at_peak, :] - peak)
-        total = own_ref[at_total, :] * own_scale + other_ref[at_total, :] * other_scale
-        weighted = own_ref[rows, :] * own_scale + other_ref[rows, :] * other_scale
-        result = jnp.transpose(weighted / total).astype(BF16)
-        for j in range(group):
-            start = (head * group + j) * HEAD_WIDTH
-            attended[:, start : start + HEAD_WIDTH] = result[
-                j * token_total : (j + 1) * token_total
-            ]
-    tokens = attended[...]
+        at = slice(head, head + 1)
+        total = totals[at]
+        weighted = own_ref[rows, :] * own_scales[at]
+        weighted += other_ref[rows, :].astype(F32) * other_scales[at]
+        results.append(jnp.transpose(weighted / total).astype(BF16))
+    tokens = jnp.concatenate(
+        [
+            result[j * token_total : (j + 1) * token_total]
+            for result in results
+            for j in range(group)
+        ],
+        axis=1,
+    )
     share = keep_ref.shape[0]
     first = lax.axis_index("col") == 0
     for start in range(0, w_ref.shape[1], step):
@@ -443,6 +491,7 @@
     for i, k in enumerate(direct):
         sent = outgoing[i] if early[i] else next(late_blocks)
         arrived.append(lax.ppermute(sent, "slot", [(s, s ^ k) for s in range(slot_total)]))
+    arrived.append(own_block)
     for sent, pair in zip(merged, shared):
         pairs = [
             (s * row_total + r, (s ^ pair[r]) * row_total + r)
@@ -450,7 +499,6 @@
             for r in range(row_total)
         ]
         arrived.append(lax.ppermute(sent, ("slot", "row"), pairs))
-    arrived.append(own_block)
 
     projected = pl.pallas_call(
         functools.partial(project_kernel, step),
@@ -479,21 +527,39 @@
         name="tables",
     )(tile_stretch, stretch_offset.reshape(-1, 128), slot_count, recomp_pos, freq)
 
-    partial = pl.pallas_call(
-        functools.partial(attend_kernel, ranks * stretch_len),
-        out_shape=jax.ShapeDtypeStruct((key_heads * HEAD_WIDTH + 2 * key_heads, query_rows), F32),
+    first_blocks = len(direct) + 1
+    known = first_blocks * ranks * stretch_len + share
+    queries, scores, new_values = pl.pallas_call(
+        functools.partial(queries_kernel, ranks * stretch_len),
+        out_shape=(
+            jax.ShapeDtypeStruct((key_heads * query_rows, HEAD_WIDTH), BF16),
+            jax.ShapeDtypeStruct((key_heads * known, query_rows), F32),
+            jax.ShapeDtypeStruct((share, key_columns), BF16),
+        ),
+        in_specs=[VMEM] * (first_blocks + 6),
+        out_specs=(VMEM,) * 3,
+        compiler_params=params(grant),
+        cost_estimate=cost(0),
+        name="queries",
+    )(*arrived[:first_blocks], *tables, both)
+    partial, to_swap = pl.pallas_call(
+        functools.partial(attend_kernel, ranks * stretch_len, first_blocks),
+        out_shape=(
+            jax.ShapeDtypeStruct((key_heads * HEAD_WIDTH + 2 * key_heads, query_rows), F32),
+            jax.ShapeDtypeStruct((key_heads * HEAD_WIDTH + 3 * 16, query_rows), BF16),
+        ),
         in_specs=[VMEM] * (len(direct) + len(shared) + 7),
-        out_specs=VMEM,
-        compiler_params=params(grant),
-        cost_estimate=cost(8),
+        out_specs=(VMEM, VMEM),
+        compiler_params=params(grant),
+        cost_estimate=cost(0),
         name="attend",
-    )(*arrived, *tables, both)
-    partial_other = lax.ppermute(partial, "row", swap)
+    )(*arrived, *tables[:3], queries, scores, new_values)
+    partial_other = lax.ppermute(to_swap, "row", swap)
 
     out_columns = w_out.shape[1]
     out_share = token_total // lax.axis_size("col")
     keep, send = pl.pallas_call(
-        functools.partial(output_kernel, step, key_heads),
+        functools.partial(output_kernel, out_columns, key_heads),
         out_shape=(
             jax.ShapeDtypeStruct((out_share, out_columns), F32),
             jax.ShapeDtypeStruct((out_share, out_columns), BF16),

time: 27.5 us -> 27.2 us (0.989)
  waiting for transfers between devices: 5.11 us -> 4.56 us
    ppermute x2, waiting for transfers between devices: 0.85 us -> 0.47 us  [on_device(): arrived.append(lax.ppermute(sent, ('slot', 'row'), pairs))]
    pallas_call x2 -> x3, Pallas kernels: 2.27 us -> 2.49 us  [the longest x1 1.63 us: on_device(): pl.pallas_call(functools.partial(output_kernel, out_columns, key_heads),...]
  transfers between devices with their start and end apart: 8 -> 8, of which waited for: 4 -> 3; matrix products, arithmetic and copies ran while one was open for 0% -> 0% of each run, Pallas kernels for 12% -> 13%
where the time goes in v6:
time: 27.2 us; the launch traced here: 27 us
  starting transfers between devices  11.7 us (43%)
  Pallas kernels  7.41 us (27%)
  waiting for transfers between devices  4.56 us (17%)
  blocking collectives  2.5 us (9%)
  other arithmetic  0.65 us (2%)
    ppermute x3, starting transfers between devices, on_device(): lax.ppermute(sent, 'slot', [(s, s ^ k) for s in range(slot_total)])  6.2 us
    ppermute x2, starting transfers between devices, on_device(): arrived.append(lax.ppermute(sent, ('slot', 'row'), pairs))  3.38 us
    ppermute x1, waiting for transfers between devices, on_device(): received = lax.ppermute(send, 'col', swap)  2.73 us
    all_gather x1, blocking collectives, on_device(): both = lax.all_gather(projected, 'row')  2.5 us
    pallas_call x1, Pallas kernels, on_device(): pl.pallas_call(functools.partial(project_kernel, step), out_shape=jax.Sha...  2.24 us
    pallas_call x1, Pallas kernels, on_device(): pl.pallas_call(functools.partial(pack_kernel, tiles, ranks, stretch_len),...  1.72 us
    pallas_call x1, Pallas kernels, on_device(): pl.pallas_call(functools.partial(output_kernel, out_columns, key_heads),...  1.63 us
    ppermute x1, starting transfers between devices, on_device(): received = lax.ppermute(send, 'col', swap)  1.55 us
  transfers between devices with their start and end apart: 8, of which 3 were waited for; matrix products, arithmetic and copies ran while one was open for 0% of the time, Pallas kernels for 13%

profile of v6, /device:TPU:0, one launch (start us, length us, event | category | flops | bytes accessed | tf_op | source)
XLA Modules:
  0.0 27.0 jit_solution(4883686251432957437)
XLA Ops:
  0.0 0.0 copy-start.4
  0.0 0.0 copy-start.5
  0.0 0.0 copy-start.6
  0.0 0.0 copy-start.7
  0.0 0.0 copy-start.8
  0.0 0.0 copy-start
  0.0 0.0 copy-start.1
  0.0 0.0 copy-start.2
  0.0 0.0 copy-start.3
  0.1 1.7 %pack.1 = (bf16[64,512]{1,0:T(8,128)(2,1)S(1)}, bf16[64,512]{1,0:T(8,128)(2,1)S(1)}, bf16[64,512]{1,0:T(8,128)(2,1)S(1)}, bf16[64,512]{1,0:T(8,128)(2,1)S(1)}, b...) custom-call(s32[8,64]{1,0:T(8,128)} %stretches_ref.1, bf16[512,512]{1,0:T(8,128)(2,1)} %bitcast.11), custom_call_target="tpu_custom_call" | custom-call | flops 8000000000 | bytes 1000 | tf_op jit(solution)/shard_map/pack/pallas_call | solution.py:468
  1.8 0.5 %collective-permute-start.3 = (bf16[128,512]{1,0:T(8,128)(2,1)S(1)}, bf16[128,512]{1,0:T(8,128)(2,1)S(1)}, u32[]{:S(2)}, u32[]{:S(2)}) collective-permute-start(bf16[128,512]{1,0:T(8,128)(2,1)S(1)} %get-tuple-element.32), channel_id=1, source_target_pairs={{0,2},{2,0},{1,3},{3,1},{4,6},{6,4},{5,7},{7,5},{8,10},{10,8},{9,1... | collective-permute-start | bytes 393224 | tf_op jit(solution)/shard_map/ppermute | solution.py:485
  2.3 3.7 %collective-permute-start = (bf16[64,512]{1,0:T(8,128)(2,1)S(1)}, bf16[64,512]{1,0:T(8,128)(2,1)S(1)}, u32[]{:S(2)}, u32[]{:S(2)}) collective-permute-start(bf16[64,512]{1,0:T(8,128)(2,1)S(1)} %get-tuple-element.26), channel_id=1, source_target_pairs={{0,16},{4,20},{8,24},{12,28},{16,0},{20,4},{24,8},{28,12},{1,17},{... | collective-permute-start | bytes 196616 | tf_op jit(solution)/shard_map/ppermute | solution.py:493
  6.0 1.3 %collective-permute-start.1 = (bf16[64,512]{1,0:T(8,128)(2,1)S(1)}, bf16[64,512]{1,0:T(8,128)(2,1)S(1)}, u32[]{:S(2)}, u32[]{:S(2)}) collective-permute-start(bf16[64,512]{1,0:T(8,128)(2,1)S(1)} %get-tuple-element.27), channel_id=1, source_target_pairs={{0,24},{4,28},{8,16},{12,20},{16,8},{20,12},{24,0},{28,4},{1,25},{... | collective-permute-start | bytes 196616 | tf_op jit(solution)/shard_map/ppermute | solution.py:493
  7.3 1.2 %collective-permute-start.2 = (bf16[64,512]{1,0:T(8,128)(2,1)S(1)}, bf16[64,512]{1,0:T(8,128)(2,1)S(1)}, u32[]{:S(2)}, u32[]{:S(2)}) collective-permute-start(bf16[64,512]{1,0:T(8,128)(2,1)S(1)} %get-tuple-element.28), channel_id=1, source_target_pairs={{0,12},{4,8},{8,4},{12,0},{16,28},{20,24},{24,20},{28,16},{1,13},{... | collective-permute-start | bytes 196616 | tf_op jit(solution)/shard_map/ppermute | solution.py:493
  8.5 0.0 copy-done.4
  8.5 0.0 copy-done.5
  8.5 0.0 copy-done.6
  8.5 0.0 copy-done.7
  8.5 0.0 copy-done.8
  8.5 0.9 %tables.1 = (f32[256,128]{1,0:T(8,128)S(1)}, f32[256,128]{1,0:T(8,128)S(1)}, f32[272,128]{1,0:T(8,128)S(1)}, f32[32,128]{1,0:T(8,128)S(1)}, f32[32,128]{1,0:T(8,128)S(1)}) custom-call(s32[8,64]{1,0:T(8,128)S(1)} %copy-done.4, s32[4,128]{1,0:T(4,128)S(1)} %bitcast.10, s32[8]{0:T(128)S(1)} %copy-done.6, s32[1,32]{1,0:T(1,128)S(1)} %copy-done.7, ...), custom_call_target="tpu_custom_call" | custom-call | bytes 1000 | tf_op jit(solution)/shard_map/tables/pallas_call | solution.py:514
  9.5 0.0 collective-permute-done.3.refs_2_
  9.5 2.9 %collective-permute-start.5 = (bf16[128,512]{1,0:T(8,128)(2,1)S(1)}, bf16[128,512]{1,0:T(8,128)(2,1)S(1)}, u32[]{:S(2)}, u32[]{:S(2)}) collective-permute-start(bf16[128,512]{1,0:T(8,128)(2,1)S(1)} %get-tuple-element.34), channel_id=1, source_target_pairs={{0,28},{2,22},{4,24},{6,18},{8,20},{10,30},{12,16},{14,26},{16,12}... | collective-permute-start | bytes 393224 | tf_op jit(solution)/shard_map/ppermute | solution.py:501
  12.4 0.5 %collective-permute-start.4 = (bf16[128,512]{1,0:T(8,128)(2,1)S(1)}, bf16[128,512]{1,0:T(8,128)(2,1)S(1)}, u32[]{:S(2)}, u32[]{:S(2)}) collective-permute-start(bf16[128,512]{1,0:T(8,128)(2,1)S(1)} %get-tuple-element.33.after_ref), channel_id=1, source_target_pairs={{0,8},{2,6},{4,12},{6,2},{8,0},{10,14},{12,4},{14,10},{16,24},{18,... | collective-permute-start | bytes 393224 | tf_op jit(solution)/shard_map/ppermute | solution.py:501
  12.9 0.0 slice-start
  12.9 0.0 copy-done
  12.9 0.0 copy-done.1
  12.9 0.0 copy-done.2
  12.9 0.0 copy-done.3
  12.9 0.0 slice-start.1
  12.9 2.2 %project.1 = f32[32,3072]{1,0:T(8,128)S(1)} custom-call(bf16[128,512]{1,0:T(8,128)(2,1)S(1)} %get-tuple-element.33.after_ref, bf16[32,2048]{1,0:T(8,128)(2,1)S(1)} %bitcast.9, bf16[2048,2048]{1,0:T(8,128)(2,1)S(1)} %copy-done, bf16[2048,512]{1,0:T(8,128)(2,1)S(1)} %copy-done.1, bf16[2048,512]{1,0:T(8,128)(2,1)S(1)} %copy-done.2), custom_call_target="tpu_custom_call" | custom-call | bytes 1000 | tf_op jit(solution)/shard_map/project/pallas_call | solution.py:503
  15.2 2.5 %all-gather = f32[64,3072]{1,0:T(8,128)S(1)} all-gather(f32[32,3072]{1,0:T(8,128)S(1)} %project.1), channel_id=2, replica_groups=mesh['slot'=8,'row'=2,'col'=2] {'row'}, dimensions={0}, use_global_device_ids=true | all-gather | bytes 1179648 | tf_op jit(solution)/shard_map/all_gather | solution.py:512
  17.7 0.0 collective-permute-done.refs_0_
  17.7 0.0 collective-permute-done.1.refs_1_
  17.7 0.0 collective-permute-done.2.refs_2_
  17.7 0.3 %queries.1 = (bf16[512,128]{1,0:T(8,128)(2,1)S(1)}, f32[576,128]{1,0:T(8,128)S(1)}, bf16[16,512]{1,0:T(8,128)(2,1)S(1)}) custom-call(bf16[64,512]{1,0:T(8,128)(2,1)S(1)} %collective-permute-done.refs_0_, bf16[64,512]{1,0:T(8,128)(2,1)S(1)} %collective-permute-done.1.refs_1_, bf16[64,512]{1,0:T(8,128)(2,1)S(1)} %collective-permute-done.2.refs_2_, ...), custom_call_target="tpu_custom_call" | custom-call | bytes 1000 | tf_op jit(solution)/shard_map/queries/pallas_call | solution.py:532
  18.0 0.0 collective-permute-done.5.refs_5_
  18.1 0.5 %collective-permute-done.4.refs_4_ = bf16[128,512]{1,0:T(8,128)(2,1)S(1)} collective-permute-done((bf16[128,512]{1,0:T(8,128)(2,1)S(1)}, bf16[128,512]{1,0:T(8,128)(2,1)S(1)}, u32[]{:S(2)}, u32[]{:S(2)}) %collective-permute-start.4) | collective-permute-done | bytes 131104 | tf_op jit(solution)/shard_map/ppermute | solution.py:501
  18.5 0.5 %attend.1 = (f32[520,128]{1,0:T(8,128)S(1)}, bf16[560,128]{1,0:T(8,128)(2,1)S(1)}) custom-call(bf16[64,512]{1,0:T(8,128)(2,1)S(1)} %collective-permute-done.refs_0_, bf16[64,512]{1,0:T(8,128)(2,1)S(1)} %collective-permute-done.1.refs_1_, bf16[64,512]{1,0:T(8,128)(2,1)S(1)} %collective-permute-done.2.refs_2_, bf16[64,512]{1,0:T(8,128)(2,1)S(1)} %get-tuple-element.29.refs_3_, ...), custom_call_target="tpu_custom_call" | custom-call | bytes 1000 | tf_op jit(solution)/shard_map/attend/pallas_call | solution.py:545
  19.0 0.1 collective-permute-start.6
  19.1 1.4 %collective-permute-done.6.other_ref = bf16[560,128]{1,0:T(8,128)(2,1)S(1)} collective-permute-done((bf16[560,128]{1,0:T(8,128)(2,1)S(1)}, bf16[560,128]{1,0:T(8,128)(2,1)S(1)}, u32[]{:S(2)}, u32[]{:S(2)}) %collective-permute-start.6) | collective-permute-done | bytes 143392 | tf_op jit(solution)/shard_map/ppermute | solution.py:557
  20.5 0.0 slice-done
  20.5 0.0 slice-done.1
  20.5 1.6 %output.1 = (f32[16,2048]{1,0:T(8,128)S(1)}, bf16[16,2048]{1,0:T(8,128)(2,1)S(1)}) custom-call(f32[520,128]{1,0:T(8,128)S(1)} %get-tuple-element.43.own_ref, bf16[560,128]{1,0:T(8,128)(2,1)S(1)} %collective-permute-done.6.other_ref, bf16[2048,2048]{1,0:T(8,128)(2,1)S(1)} %bitcast.7), custom_call_target="tpu_custom_call" | custom-call | tf_op jit(solution)/shard_map/output/pallas_call | solution.py:561
  22.1 1.6 %collective-permute-start.7 = (bf16[16,2048]{1,0:T(8,128)(2,1)S(1)}, bf16[16,2048]{1,0:T(8,128)(2,1)S(1)}, u32[]{:S(2)}, u32[]{:S(2)}) collective-permute-start(bf16[16,2048]{1,0:T(8,128)(2,1)S(1)} %get-tuple-element.46), channel_id=1, source_target_pairs={{0,1},{1,0},{2,3},{3,2},{4,5},{5,4},{6,7},{7,6},{8,9},{9,8},{10,11... | collective-permute-start | bytes 196616 | tf_op jit(solution)/shard_map/ppermute | solution.py:573
  23.7 2.7 %collective-permute-done.7 = bf16[16,2048]{1,0:T(8,128)(2,1)S(1)} collective-permute-done((bf16[16,2048]{1,0:T(8,128)(2,1)S(1)}, bf16[16,2048]{1,0:T(8,128)(2,1)S(1)}, u32[]{:S(2)}, u32[]{:S(2)}) %collective-permute-start.7) | collective-permute-done | bytes 65568 | tf_op jit(solution)/shard_map/ppermute | solution.py:573
  26.4 0.6 %fusion = bf16[1,16,2048]{2,1,0:T(8,128)(2,1)} fusion(f32[16,2048]{1,0:T(8,128)S(1)} %get-tuple-element.45, bf16[16,2048]{1,0:T(8,128)(2,1)S(1)} %collective-permute-done.7), kind=kLoop, calls=%fused_computation.1 | loop fusion | flops 98304 | bytes 262144 | tf_op jit(solution)/shard_map/broadcast_in_dim | solution.py:574
  (2 shorter events, 0.0 us)
Async XLA Ops:
  0.0 8.5 %copy-start.4 = (s32[8,64]{1,0:T(8,128)S(1)}, s32[8,64]{1,0:T(8,128)}, u32[]{:S(2)}) copy-start(s32[8,64]{1,0:T(8,128)} %stretches_ref.1) | copy-start | bytes 6148
  0.0 8.5 %copy-start.5 = (s32[512]{0:T(512)S(1)}, s32[512]{0:T(512)}, u32[]{:S(2)}) copy-start(s32[512]{0:T(512)} %param.17) | copy-start | bytes 6148
  0.0 8.5 %copy-start.6 = (s32[8]{0:T(128)S(1)}, s32[8]{0:T(128)}, u32[]{:S(2)}) copy-start(s32[8]{0:T(128)} %counts_ref.1) | copy-start | bytes 100
  0.0 8.5 %copy-start.7 = (s32[1,32]{1,0:T(1,128)S(1)}, s32[1,32]{1,0:T(1,128)}, u32[]{:S(2)}) copy-start(s32[1,32]{1,0:T(1,128)} %positions_ref.1) | copy-start | bytes 388
  0.0 8.5 %copy-start.8 = (f32[1,128]{1,0:T(1,128)S(1)}, f32[1,128]{1,0:T(1,128)}, u32[]{:S(2)}) copy-start(f32[1,128]{1,0:T(1,128)} %constant.2.clone.freq_ref) | copy-start | bytes 1540
  0.0 12.9 %copy-start = (bf16[2048,2048]{1,0:T(8,128)(2,1)S(1)}, bf16[2048,2048]{1,0:T(8,128)(2,1)}, u32[]{:S(2)}) copy-start(bf16[2048,2048]{1,0:T(8,128)(2,1)} %wq_ref.1) | copy-start | bytes 25165828
  0.0 12.9 %copy-start.1 = (bf16[2048,512]{1,0:T(8,128)(2,1)S(1)}, bf16[2048,512]{1,0:T(8,128)(2,1)}, u32[]{:S(2)}) copy-start(bf16[2048,512]{1,0:T(8,128)(2,1)} %wk_ref.1) | copy-start | bytes 6291460
  0.0 12.9 %copy-start.2 = (bf16[2048,512]{1,0:T(8,128)(2,1)S(1)}, bf16[2048,512]{1,0:T(8,128)(2,1)}, u32[]{:S(2)}) copy-start(bf16[2048,512]{1,0:T(8,128)(2,1)} %wv_ref.1) | copy-start | bytes 6291460
  0.0 12.9 %copy-start.3 = (bf16[1,32,2048]{2,1,0:T(8,128)(2,1)S(1)}, bf16[1,32,2048]{2,1,0:T(8,128)(2,1)}, u32[]{:S(2)}) copy-start(bf16[1,32,2048]{2,1,0:T(8,128)(2,1)} %param.11) | copy-start | bytes 393220
  1.8 7.7 %collective-permute-start.3 = (bf16[128,512]{1,0:T(8,128)(2,1)S(1)}, bf16[128,512]{1,0:T(8,128)(2,1)S(1)}, u32[]{:S(2)}, u32[]{:S(2)}) collective-permute-start(bf16[128,512]{1,0:T(8,128)(2,1)S(1)} %get-tuple-element.32), channel_id=1, source_target_pairs={{0,2},{2,0},{1,3},{3,1},{4,6},{6,4},{5,7},{7,5},{8,10},{10,8},{9,1... | collective-permute-start | bytes 393224 | tf_op jit(solution)/shard_map/ppermute | solution.py:485
  2.3 15.4 %collective-permute-start = (bf16[64,512]{1,0:T(8,128)(2,1)S(1)}, bf16[64,512]{1,0:T(8,128)(2,1)S(1)}, u32[]{:S(2)}, u32[]{:S(2)}) collective-permute-start(bf16[64,512]{1,0:T(8,128)(2,1)S(1)} %get-tuple-element.26), channel_id=1, source_target_pairs={{0,16},{4,20},{8,24},{12,28},{16,0},{20,4},{24,8},{28,12},{1,17},{... | collective-permute-start | bytes 196616 | tf_op jit(solution)/shard_map/ppermute | solution.py:493
  6.0 11.7 %collective-permute-start.1 = (bf16[64,512]{1,0:T(8,128)(2,1)S(1)}, bf16[64,512]{1,0:T(8,128)(2,1)S(1)}, u32[]{:S(2)}, u32[]{:S(2)}) collective-permute-start(bf16[64,512]{1,0:T(8,128)(2,1)S(1)} %get-tuple-element.27), channel_id=1, source_target_pairs={{0,24},{4,28},{8,16},{12,20},{16,8},{20,12},{24,0},{28,4},{1,25},{... | collective-permute-start | bytes 196616 | tf_op jit(solution)/shard_map/ppermute | solution.py:493
  7.3 10.4 %collective-permute-start.2 = (bf16[64,512]{1,0:T(8,128)(2,1)S(1)}, bf16[64,512]{1,0:T(8,128)(2,1)S(1)}, u32[]{:S(2)}, u32[]{:S(2)}) collective-permute-start(bf16[64,512]{1,0:T(8,128)(2,1)S(1)} %get-tuple-element.28), channel_id=1, source_target_pairs={{0,12},{4,8},{8,4},{12,0},{16,28},{20,24},{24,20},{28,16},{1,13},{... | collective-permute-start | bytes 196616 | tf_op jit(solution)/shard_map/ppermute | solution.py:493
  9.5 8.5 %collective-permute-start.5 = (bf16[128,512]{1,0:T(8,128)(2,1)S(1)}, bf16[128,512]{1,0:T(8,128)(2,1)S(1)}, u32[]{:S(2)}, u32[]{:S(2)}) collective-permute-start(bf16[128,512]{1,0:T(8,128)(2,1)S(1)} %get-tuple-element.34), channel_id=1, source_target_pairs={{0,28},{2,22},{4,24},{6,18},{8,20},{10,30},{12,16},{14,26},{16,12}... | collective-permute-start | bytes 393224 | tf_op jit(solution)/shard_map/ppermute | solution.py:501
  12.4 6.1 %collective-permute-start.4 = (bf16[128,512]{1,0:T(8,128)(2,1)S(1)}, bf16[128,512]{1,0:T(8,128)(2,1)S(1)}, u32[]{:S(2)}, u32[]{:S(2)}) collective-permute-start(bf16[128,512]{1,0:T(8,128)(2,1)S(1)} %get-tuple-element.33.after_ref), channel_id=1, source_target_pairs={{0,8},{2,6},{4,12},{6,2},{8,0},{10,14},{12,4},{14,10},{16,24},{18,... | collective-permute-start | bytes 393224 | tf_op jit(solution)/shard_map/ppermute | solution.py:501
  12.9 7.6 %slice-start = ((s8[8388608]{0:T(1024)(128)(4,1)}), s8[4194304]{0:T(1024)(128)(4,1)S(1)}, s32[]{:S(2)}) async-start(s8[8388608]{0:T(1024)(128)(4,1)} %bitcast.6), calls=%async_computation | async-start | bytes 8388608
  12.9 7.6 %slice-start.1 = ((s8[8388608]{0:T(1024)(128)(4,1)}), s8[4194304]{0:T(1024)(128)(4,1)S(1)}, s32[]{:S(2)}) async-start(s8[8388608]{0:T(1024)(128)(4,1)} %bitcast.6), calls=%async_computation.1 | async-start | bytes 8388608
  19.0 1.4 %collective-permute-start.6 = (bf16[560,128]{1,0:T(8,128)(2,1)S(1)}, bf16[560,128]{1,0:T(8,128)(2,1)S(1)}, u32[]{:S(2)}, u32[]{:S(2)}) collective-permute-start(bf16[560,128]{1,0:T(8,128)(2,1)S(1)} %get-tuple-element.44), channel_id=1, source_target_pairs={{0,2},{2,0},{1,3},{3,1},{4,6},{6,4},{5,7},{7,5},{8,10},{10,8},{9,1... | collective-permute-start | bytes 430088 | tf_op jit(solution)/shard_map/ppermute | solution.py:557
  22.1 4.3 %collective-permute-start.7 = (bf16[16,2048]{1,0:T(8,128)(2,1)S(1)}, bf16[16,2048]{1,0:T(8,128)(2,1)S(1)}, u32[]{:S(2)}, u32[]{:S(2)}) collective-permute-start(bf16[16,2048]{1,0:T(8,128)(2,1)S(1)} %get-tuple-element.46), channel_id=1, source_target_pairs={{0,1},{1,0},{2,3},{3,2},{4,5},{5,4},{6,7},{7,6},{8,9},{9,8},{10,11... | collective-permute-start | bytes 196616 | tf_op jit(solution)/shard_map/ppermute | solution.py:573

commit v7 on v6

--- a/solution.py
+++ b/solution.py
@@ -66,13 +66,11 @@
     row = lax.axis_index("row")
     own = slot * lax.axis_size("row") + row
     slots, slot_tiles = stretches_ref.shape
-    per_slot = ranks * 2 * stretch_len
+    per_slot = ranks * stretch_len
     rows = slots * per_slot
     part, token = divide(iota((rows, 128), 0), stretch_len)
-    part, rank_of_row = divide(part, ranks)
-    kind = part & 1
+    _, rank_of_row = divide(part, ranks)
     rank_here = iota((rows, 128), 1) == rank_of_row
-    within = (kind * stretch_len + token)[:, :1]
     get_stretches.wait()
     owner, local = divide(stretches_ref[...], tiles)
     mine = (owner == own).astype(F32)
@@ -92,14 +90,27 @@
         axis=0,
     )
     stretch = jnp.sum(jnp.where(rank_here, ids, 0.0), axis=1, keepdims=True).astype(jnp.int32)
-    source = stretch * (2 * stretch_len) + within
-    store_rows = tiles * 2 * stretch_len
+    source = stretch * stretch_len + token[:, :1]
+    store_rows = tiles * stretch_len
     pick = (iota((rows, store_rows), 1) == source).astype(F32).astype(BF16)
     get_store.wait()
-    picked = jnp.dot(pick, store_ref[...], preferred_element_type=F32).astype(BF16)
+    columns = store_ref.shape[1]
+    store = store_ref[...].astype(F32).reshape(tiles, 2, stretch_len, columns)
+    keys, values = [
+        jnp.dot(
+            pick,
+            store[:, kind].reshape(store_rows, columns).astype(BF16),
+            preferred_element_type=F32,
+        ).astype(BF16)
+        for kind in range(2)
+    ]
     for i, out_ref in enumerate(outs):
-        out_ref[...] = picked[i * per_slot : (i + 1) * per_slot]
-    give_ref[...] = picked[len(outs) * per_slot :]
+        out_ref[:per_slot] = keys[i * per_slot : (i + 1) * per_slot]
+        out_ref[per_slot:] = values[i * per_slot : (i + 1) * per_slot]
+    for i in range(len(shared)):
+        at = (len(outs) + i) * per_slot
+        give_ref[2 * i * per_slot : (2 * i + 1) * per_slot] = keys[at : at + per_slot]
+        give_ref[(2 * i + 1) * per_slot : (2 * i + 2) * per_slot] = values[at : at + per_slot]
 
 
 def fetch(pieces, sems):

time: 27.2 us -> 27 us (level)
  no operation moved by 1% of the time
where the time goes in v7:
time: 27 us; the launch traced here: 26.9 us
  starting transfers between devices  11.7 us (43%)
  Pallas kernels  7.23 us (27%)
  waiting for transfers between devices  4.56 us (17%)
  blocking collectives  2.5 us (9%)
  other arithmetic  0.65 us (2%)
    ppermute x3, starting transfers between devices, on_device(): lax.ppermute(sent, 'slot', [(s, s ^ k) for s in range(slot_total)])  6.2 us
    ppermute x2, starting transfers between devices, on_device(): arrived.append(lax.ppermute(sent, ('slot', 'row'), pairs))  3.38 us
    ppermute x1, waiting for transfers between devices, on_device(): received = lax.ppermute(send, 'col', swap)  2.73 us
    all_gather x1, blocking collectives, on_device(): both = lax.all_gather(projected, 'row')  2.5 us
    pallas_call x1, Pallas kernels, on_device(): pl.pallas_call(functools.partial(project_kernel, step), out_shape=jax.Sha...  2.24 us
    pallas_call x1, Pallas kernels, on_device(): pl.pallas_call(functools.partial(output_kernel, out_columns, key_heads),...  1.63 us
    ppermute x1, starting transfers between devices, on_device(): received = lax.ppermute(send, 'col', swap)  1.55 us
    pallas_call x1, Pallas kernels, on_device(): pl.pallas_call(functools.partial(pack_kernel, tiles, ranks, stretch_len),...  1.54 us
  transfers between devices with their start and end apart: 8, of which 3 were waited for; matrix products, arithmetic and copies ran while one was open for 0% of the time, Pallas kernels for 13%

profile of v7, /device:TPU:0, one launch (start us, length us, event | category | flops | bytes accessed | tf_op | source)
XLA Modules:
  0.0 26.9 jit_solution(13914992750822166791)
XLA Ops:
  0.0 0.0 copy-start.4
  0.0 0.0 copy-start.5
  0.0 0.0 copy-start.6
  0.0 0.0 copy-start.7
  0.0 0.0 copy-start.8
  0.0 0.0 copy-start
  0.0 0.0 copy-start.1
  0.0 0.0 copy-start.2
  0.0 0.0 copy-start.3
  0.1 1.5 %pack.1 = (bf16[64,512]{1,0:T(8,128)(2,1)S(1)}, bf16[64,512]{1,0:T(8,128)(2,1)S(1)}, bf16[64,512]{1,0:T(8,128)(2,1)S(1)}, bf16[64,512]{1,0:T(8,128)(2,1)S(1)}, b...) custom-call(s32[8,64]{1,0:T(8,128)} %stretches_ref.1, bf16[512,512]{1,0:T(8,128)(2,1)} %bitcast.11), custom_call_target="tpu_custom_call" | custom-call | flops 8000000000 | bytes 1000 | tf_op jit(solution)/shard_map/pack/pallas_call | solution.py:479
  1.6 0.5 %collective-permute-start.3 = (bf16[128,512]{1,0:T(8,128)(2,1)S(1)}, bf16[128,512]{1,0:T(8,128)(2,1)S(1)}, u32[]{:S(2)}, u32[]{:S(2)}) collective-permute-start(bf16[128,512]{1,0:T(8,128)(2,1)S(1)} %get-tuple-element.32), channel_id=1, source_target_pairs={{0,2},{2,0},{1,3},{3,1},{4,6},{6,4},{5,7},{7,5},{8,10},{10,8},{9,1... | collective-permute-start | bytes 393224 | tf_op jit(solution)/shard_map/ppermute | solution.py:496
  2.1 3.7 %collective-permute-start = (bf16[64,512]{1,0:T(8,128)(2,1)S(1)}, bf16[64,512]{1,0:T(8,128)(2,1)S(1)}, u32[]{:S(2)}, u32[]{:S(2)}) collective-permute-start(bf16[64,512]{1,0:T(8,128)(2,1)S(1)} %get-tuple-element.26), channel_id=1, source_target_pairs={{0,16},{4,20},{8,24},{12,28},{16,0},{20,4},{24,8},{28,12},{1,17},{... | collective-permute-start | bytes 196616 | tf_op jit(solution)/shard_map/ppermute | solution.py:504
  5.8 1.3 %collective-permute-start.1 = (bf16[64,512]{1,0:T(8,128)(2,1)S(1)}, bf16[64,512]{1,0:T(8,128)(2,1)S(1)}, u32[]{:S(2)}, u32[]{:S(2)}) collective-permute-start(bf16[64,512]{1,0:T(8,128)(2,1)S(1)} %get-tuple-element.27), channel_id=1, source_target_pairs={{0,24},{4,28},{8,16},{12,20},{16,8},{20,12},{24,0},{28,4},{1,25},{... | collective-permute-start | bytes 196616 | tf_op jit(solution)/shard_map/ppermute | solution.py:504
  7.1 1.2 %collective-permute-start.2 = (bf16[64,512]{1,0:T(8,128)(2,1)S(1)}, bf16[64,512]{1,0:T(8,128)(2,1)S(1)}, u32[]{:S(2)}, u32[]{:S(2)}) collective-permute-start(bf16[64,512]{1,0:T(8,128)(2,1)S(1)} %get-tuple-element.28), channel_id=1, source_target_pairs={{0,12},{4,8},{8,4},{12,0},{16,28},{20,24},{24,20},{28,16},{1,13},{... | collective-permute-start | bytes 196616 | tf_op jit(solution)/shard_map/ppermute | solution.py:504
  8.3 0.0 copy-done.4
  8.3 0.0 copy-done.5
  8.3 0.0 copy-done.6
  8.3 0.0 copy-done.7
  8.3 0.0 copy-done.8
  8.4 0.9 %tables.1 = (f32[256,128]{1,0:T(8,128)S(1)}, f32[256,128]{1,0:T(8,128)S(1)}, f32[272,128]{1,0:T(8,128)S(1)}, f32[32,128]{1,0:T(8,128)S(1)}, f32[32,128]{1,0:T(8,128)S(1)}) custom-call(s32[8,64]{1,0:T(8,128)S(1)} %copy-done.4, s32[4,128]{1,0:T(4,128)S(1)} %bitcast.10, s32[8]{0:T(128)S(1)} %copy-done.6, s32[1,32]{1,0:T(1,128)S(1)} %copy-done.7, ...), custom_call_target="tpu_custom_call" | custom-call | bytes 1000 | tf_op jit(solution)/shard_map/tables/pallas_call | solution.py:525
  9.3 0.0 collective-permute-done.3.refs_2_
  9.3 2.9 %collective-permute-start.5 = (bf16[128,512]{1,0:T(8,128)(2,1)S(1)}, bf16[128,512]{1,0:T(8,128)(2,1)S(1)}, u32[]{:S(2)}, u32[]{:S(2)}) collective-permute-start(bf16[128,512]{1,0:T(8,128)(2,1)S(1)} %get-tuple-element.34), channel_id=1, source_target_pairs={{0,28},{2,22},{4,24},{6,18},{8,20},{10,30},{12,16},{14,26},{16,12}... | collective-permute-start | bytes 393224 | tf_op jit(solution)/shard_map/ppermute | solution.py:512
  12.3 0.5 %collective-permute-start.4 = (bf16[128,512]{1,0:T(8,128)(2,1)S(1)}, bf16[128,512]{1,0:T(8,128)(2,1)S(1)}, u32[]{:S(2)}, u32[]{:S(2)}) collective-permute-start(bf16[128,512]{1,0:T(8,128)(2,1)S(1)} %get-tuple-element.33.after_ref), channel_id=1, source_target_pairs={{0,8},{2,6},{4,12},{6,2},{8,0},{10,14},{12,4},{14,10},{16,24},{18,... | collective-permute-start | bytes 393224 | tf_op jit(solution)/shard_map/ppermute | solution.py:512
  12.7 0.0 slice-start
  12.7 0.0 copy-done
  12.7 0.0 copy-done.1
  12.7 0.0 copy-done.2
  12.7 0.0 copy-done.3
  12.7 0.0 slice-start.1
  12.7 2.2 %project.1 = f32[32,3072]{1,0:T(8,128)S(1)} custom-call(bf16[128,512]{1,0:T(8,128)(2,1)S(1)} %get-tuple-element.33.after_ref, bf16[32,2048]{1,0:T(8,128)(2,1)S(1)} %bitcast.9, bf16[2048,2048]{1,0:T(8,128)(2,1)S(1)} %copy-done, bf16[2048,512]{1,0:T(8,128)(2,1)S(1)} %copy-done.1, bf16[2048,512]{1,0:T(8,128)(2,1)S(1)} %copy-done.2), custom_call_target="tpu_custom_call" | custom-call | bytes 1000 | tf_op jit(solution)/shard_map/project/pallas_call | solution.py:514
  15.0 2.5 %all-gather = f32[64,3072]{1,0:T(8,128)S(1)} all-gather(f32[32,3072]{1,0:T(8,128)S(1)} %project.1), channel_id=2, replica_groups=mesh['slot'=8,'row'=2,'col'=2] {'row'}, dimensions={0}, use_global_device_ids=true | all-gather | bytes 1179648 | tf_op jit(solution)/shard_map/all_gather | solution.py:523
  17.5 0.0 collective-permute-done.refs_0_
  17.5 0.0 collective-permute-done.1.refs_1_
  17.5 0.0 collective-permute-done.2.refs_2_
  17.5 0.3 %queries.1 = (bf16[512,128]{1,0:T(8,128)(2,1)S(1)}, f32[576,128]{1,0:T(8,128)S(1)}, bf16[16,512]{1,0:T(8,128)(2,1)S(1)}) custom-call(bf16[64,512]{1,0:T(8,128)(2,1)S(1)} %collective-permute-done.refs_0_, bf16[64,512]{1,0:T(8,128)(2,1)S(1)} %collective-permute-done.1.refs_1_, bf16[64,512]{1,0:T(8,128)(2,1)S(1)} %collective-permute-done.2.refs_2_, ...), custom_call_target="tpu_custom_call" | custom-call | bytes 1000 | tf_op jit(solution)/shard_map/queries/pallas_call | solution.py:543
  17.9 0.0 collective-permute-done.5.refs_5_
  17.9 0.5 %collective-permute-done.4.refs_4_ = bf16[128,512]{1,0:T(8,128)(2,1)S(1)} collective-permute-done((bf16[128,512]{1,0:T(8,128)(2,1)S(1)}, bf16[128,512]{1,0:T(8,128)(2,1)S(1)}, u32[]{:S(2)}, u32[]{:S(2)}) %collective-permute-start.4) | collective-permute-done | bytes 131104 | tf_op jit(solution)/shard_map/ppermute | solution.py:512
  18.3 0.5 %attend.1 = (f32[520,128]{1,0:T(8,128)S(1)}, bf16[560,128]{1,0:T(8,128)(2,1)S(1)}) custom-call(bf16[64,512]{1,0:T(8,128)(2,1)S(1)} %collective-permute-done.refs_0_, bf16[64,512]{1,0:T(8,128)(2,1)S(1)} %collective-permute-done.1.refs_1_, bf16[64,512]{1,0:T(8,128)(2,1)S(1)} %collective-permute-done.2.refs_2_, bf16[64,512]{1,0:T(8,128)(2,1)S(1)} %get-tuple-element.29.refs_3_, ...), custom_call_target="tpu_custom_call" | custom-call | bytes 1000 | tf_op jit(solution)/shard_map/attend/pallas_call | solution.py:556
  18.9 0.1 collective-permute-start.6
  18.9 1.4 %collective-permute-done.6.other_ref = bf16[560,128]{1,0:T(8,128)(2,1)S(1)} collective-permute-done((bf16[560,128]{1,0:T(8,128)(2,1)S(1)}, bf16[560,128]{1,0:T(8,128)(2,1)S(1)}, u32[]{:S(2)}, u32[]{:S(2)}) %collective-permute-start.6) | collective-permute-done | bytes 143392 | tf_op jit(solution)/shard_map/ppermute | solution.py:568
  20.3 0.0 slice-done
  20.3 0.0 slice-done.1
  20.3 1.6 %output.1 = (f32[16,2048]{1,0:T(8,128)S(1)}, bf16[16,2048]{1,0:T(8,128)(2,1)S(1)}) custom-call(f32[520,128]{1,0:T(8,128)S(1)} %get-tuple-element.43.own_ref, bf16[560,128]{1,0:T(8,128)(2,1)S(1)} %collective-permute-done.6.other_ref, bf16[2048,2048]{1,0:T(8,128)(2,1)S(1)} %bitcast.7), custom_call_target="tpu_custom_call" | custom-call | tf_op jit(solution)/shard_map/output/pallas_call | solution.py:572
  21.9 1.5 %collective-permute-start.7 = (bf16[16,2048]{1,0:T(8,128)(2,1)S(1)}, bf16[16,2048]{1,0:T(8,128)(2,1)S(1)}, u32[]{:S(2)}, u32[]{:S(2)}) collective-permute-start(bf16[16,2048]{1,0:T(8,128)(2,1)S(1)} %get-tuple-element.46), channel_id=1, source_target_pairs={{0,1},{1,0},{2,3},{3,2},{4,5},{5,4},{6,7},{7,6},{8,9},{9,8},{10,11... | collective-permute-start | bytes 196616 | tf_op jit(solution)/shard_map/ppermute | solution.py:584
  23.5 2.7 %collective-permute-done.7 = bf16[16,2048]{1,0:T(8,128)(2,1)S(1)} collective-permute-done((bf16[16,2048]{1,0:T(8,128)(2,1)S(1)}, bf16[16,2048]{1,0:T(8,128)(2,1)S(1)}, u32[]{:S(2)}, u32[]{:S(2)}) %collective-permute-start.7) | collective-permute-done | bytes 65568 | tf_op jit(solution)/shard_map/ppermute | solution.py:584
  26.2 0.6 %fusion = bf16[1,16,2048]{2,1,0:T(8,128)(2,1)} fusion(f32[16,2048]{1,0:T(8,128)S(1)} %get-tuple-element.45, bf16[16,2048]{1,0:T(8,128)(2,1)S(1)} %collective-permute-done.7), kind=kLoop, calls=%fused_computation.1 | loop fusion | flops 98304 | bytes 262144 | tf_op jit(solution)/shard_map/broadcast_in_dim | solution.py:585
  (2 shorter events, 0.0 us)
Async XLA Ops:
  0.0 8.3 %copy-start.4 = (s32[8,64]{1,0:T(8,128)S(1)}, s32[8,64]{1,0:T(8,128)}, u32[]{:S(2)}) copy-start(s32[8,64]{1,0:T(8,128)} %stretches_ref.1) | copy-start | bytes 6148
  0.0 8.3 %copy-start.5 = (s32[512]{0:T(512)S(1)}, s32[512]{0:T(512)}, u32[]{:S(2)}) copy-start(s32[512]{0:T(512)} %param.17) | copy-start | bytes 6148
  0.0 8.3 %copy-start.6 = (s32[8]{0:T(128)S(1)}, s32[8]{0:T(128)}, u32[]{:S(2)}) copy-start(s32[8]{0:T(128)} %counts_ref.1) | copy-start | bytes 100
  0.0 8.3 %copy-start.7 = (s32[1,32]{1,0:T(1,128)S(1)}, s32[1,32]{1,0:T(1,128)}, u32[]{:S(2)}) copy-start(s32[1,32]{1,0:T(1,128)} %positions_ref.1) | copy-start | bytes 388
  0.0 8.3 %copy-start.8 = (f32[1,128]{1,0:T(1,128)S(1)}, f32[1,128]{1,0:T(1,128)}, u32[]{:S(2)}) copy-start(f32[1,128]{1,0:T(1,128)} %constant.2.clone.freq_ref) | copy-start | bytes 1540
  0.0 12.7 %copy-start = (bf16[2048,2048]{1,0:T(8,128)(2,1)S(1)}, bf16[2048,2048]{1,0:T(8,128)(2,1)}, u32[]{:S(2)}) copy-start(bf16[2048,2048]{1,0:T(8,128)(2,1)} %wq_ref.1) | copy-start | bytes 25165828
  0.0 12.7 %copy-start.1 = (bf16[2048,512]{1,0:T(8,128)(2,1)S(1)}, bf16[2048,512]{1,0:T(8,128)(2,1)}, u32[]{:S(2)}) copy-start(bf16[2048,512]{1,0:T(8,128)(2,1)} %wk_ref.1) | copy-start | bytes 6291460
  0.0 12.7 %copy-start.2 = (bf16[2048,512]{1,0:T(8,128)(2,1)S(1)}, bf16[2048,512]{1,0:T(8,128)(2,1)}, u32[]{:S(2)}) copy-start(bf16[2048,512]{1,0:T(8,128)(2,1)} %wv_ref.1) | copy-start | bytes 6291460
  0.0 12.7 %copy-start.3 = (bf16[1,32,2048]{2,1,0:T(8,128)(2,1)S(1)}, bf16[1,32,2048]{2,1,0:T(8,128)(2,1)}, u32[]{:S(2)}) copy-start(bf16[1,32,2048]{2,1,0:T(8,128)(2,1)} %param.11) | copy-start | bytes 393220
  1.6 7.7 %collective-permute-start.3 = (bf16[128,512]{1,0:T(8,128)(2,1)S(1)}, bf16[128,512]{1,0:T(8,128)(2,1)S(1)}, u32[]{:S(2)}, u32[]{:S(2)}) collective-permute-start(bf16[128,512]{1,0:T(8,128)(2,1)S(1)} %get-tuple-element.32), channel_id=1, source_target_pairs={{0,2},{2,0},{1,3},{3,1},{4,6},{6,4},{5,7},{7,5},{8,10},{10,8},{9,1... | collective-permute-start | bytes 393224 | tf_op jit(solution)/shard_map/ppermute | solution.py:496
  2.1 15.4 %collective-permute-start = (bf16[64,512]{1,0:T(8,128)(2,1)S(1)}, bf16[64,512]{1,0:T(8,128)(2,1)S(1)}, u32[]{:S(2)}, u32[]{:S(2)}) collective-permute-start(bf16[64,512]{1,0:T(8,128)(2,1)S(1)} %get-tuple-element.26), channel_id=1, source_target_pairs={{0,16},{4,20},{8,24},{12,28},{16,0},{20,4},{24,8},{28,12},{1,17},{... | collective-permute-start | bytes 196616 | tf_op jit(solution)/shard_map/ppermute | solution.py:504
  5.8 11.7 %collective-permute-start.1 = (bf16[64,512]{1,0:T(8,128)(2,1)S(1)}, bf16[64,512]{1,0:T(8,128)(2,1)S(1)}, u32[]{:S(2)}, u32[]{:S(2)}) collective-permute-start(bf16[64,512]{1,0:T(8,128)(2,1)S(1)} %get-tuple-element.27), channel_id=1, source_target_pairs={{0,24},{4,28},{8,16},{12,20},{16,8},{20,12},{24,0},{28,4},{1,25},{... | collective-permute-start | bytes 196616 | tf_op jit(solution)/shard_map/ppermute | solution.py:504
  7.1 10.4 %collective-permute-start.2 = (bf16[64,512]{1,0:T(8,128)(2,1)S(1)}, bf16[64,512]{1,0:T(8,128)(2,1)S(1)}, u32[]{:S(2)}, u32[]{:S(2)}) collective-permute-start(bf16[64,512]{1,0:T(8,128)(2,1)S(1)} %get-tuple-element.28), channel_id=1, source_target_pairs={{0,12},{4,8},{8,4},{12,0},{16,28},{20,24},{24,20},{28,16},{1,13},{... | collective-permute-start | bytes 196616 | tf_op jit(solution)/shard_map/ppermute | solution.py:504
  9.3 8.5 %collective-permute-start.5 = (bf16[128,512]{1,0:T(8,128)(2,1)S(1)}, bf16[128,512]{1,0:T(8,128)(2,1)S(1)}, u32[]{:S(2)}, u32[]{:S(2)}) collective-permute-start(bf16[128,512]{1,0:T(8,128)(2,1)S(1)} %get-tuple-element.34), channel_id=1, source_target_pairs={{0,28},{2,22},{4,24},{6,18},{8,20},{10,30},{12,16},{14,26},{16,12}... | collective-permute-start | bytes 393224 | tf_op jit(solution)/shard_map/ppermute | solution.py:512
  12.3 6.1 %collective-permute-start.4 = (bf16[128,512]{1,0:T(8,128)(2,1)S(1)}, bf16[128,512]{1,0:T(8,128)(2,1)S(1)}, u32[]{:S(2)}, u32[]{:S(2)}) collective-permute-start(bf16[128,512]{1,0:T(8,128)(2,1)S(1)} %get-tuple-element.33.after_ref), channel_id=1, source_target_pairs={{0,8},{2,6},{4,12},{6,2},{8,0},{10,14},{12,4},{14,10},{16,24},{18,... | collective-permute-start | bytes 393224 | tf_op jit(solution)/shard_map/ppermute | solution.py:512
  12.7 7.6 %slice-start = ((s8[8388608]{0:T(1024)(128)(4,1)}), s8[4194304]{0:T(1024)(128)(4,1)S(1)}, s32[]{:S(2)}) async-start(s8[8388608]{0:T(1024)(128)(4,1)} %bitcast.6), calls=%async_computation | async-start | bytes 8388608
  12.7 7.6 %slice-start.1 = ((s8[8388608]{0:T(1024)(128)(4,1)}), s8[4194304]{0:T(1024)(128)(4,1)S(1)}, s32[]{:S(2)}) async-start(s8[8388608]{0:T(1024)(128)(4,1)} %bitcast.6), calls=%async_computation.1 | async-start | bytes 8388608
  18.9 1.4 %collective-permute-start.6 = (bf16[560,128]{1,0:T(8,128)(2,1)S(1)}, bf16[560,128]{1,0:T(8,128)(2,1)S(1)}, u32[]{:S(2)}, u32[]{:S(2)}) collective-permute-start(bf16[560,128]{1,0:T(8,128)(2,1)S(1)} %get-tuple-element.44), channel_id=1, source_target_pairs={{0,2},{2,0},{1,3},{3,1},{4,6},{6,4},{5,7},{7,5},{8,10},{10,8},{9,1... | collective-permute-start | bytes 430088 | tf_op jit(solution)/shard_map/ppermute | solution.py:568
  21.9 4.3 %collective-permute-start.7 = (bf16[16,2048]{1,0:T(8,128)(2,1)S(1)}, bf16[16,2048]{1,0:T(8,128)(2,1)S(1)}, u32[]{:S(2)}, u32[]{:S(2)}) collective-permute-start(bf16[16,2048]{1,0:T(8,128)(2,1)S(1)} %get-tuple-element.46), channel_id=1, source_target_pairs={{0,1},{1,0},{2,3},{3,2},{4,5},{5,4},{6,7},{7,6},{8,9},{9,8},{10,11... | collective-permute-start | bytes 196616 | tf_op jit(solution)/shard_map/ppermute | solution.py:584

commit v8 on v7

--- a/solution.py
+++ b/solution.py
@@ -111,20 +111,6 @@
         at = (len(outs) + i) * per_slot
         give_ref[2 * i * per_slot : (2 * i + 1) * per_slot] = keys[at : at + per_slot]
         give_ref[(2 * i + 1) * per_slot : (2 * i + 2) * per_slot] = values[at : at + per_slot]
-
-
-def fetch(pieces, sems):
-    copies = [pltpu.make_async_copy(a, b, sems.at[i]) for i, (a, b) in enumerate(pieces)]
-    for copy in copies:
-        copy.start()
-    return copies
-
-
-def column_pieces(source, target, step):
-    return [
-        (source.at[:, pl.ds(start, step)], target.at[:, pl.ds(start, step)])
-        for start in range(0, source.shape[1], step)
-    ]
 
 
 def project_kernel(step, after_ref, hidden_ref, wq_ref, wk_ref, wv_ref, out_ref):
@@ -363,8 +349,8 @@
         send_ref[rows, :] = weighted.astype(BF16)
 
 
-def output_kernel(step, key_heads, own_ref, other_ref, w_ref, keep_ref, send_ref, attended):
-    token_total = attended.shape[0]
+def output_kernel(key_heads, own_ref, other_ref, w_ref, keep_ref, send_ref):
+    token_total = keep_ref.shape[0] * lax.axis_size("col")
     group = own_ref.shape[1] // token_total
     base = key_heads * HEAD_WIDTH
     results = []
@@ -394,11 +380,9 @@
     )
     share = keep_ref.shape[0]
     first = lax.axis_index("col") == 0
-    for start in range(0, w_ref.shape[1], step):
-        cols = slice(start, start + step)
-        part = jnp.dot(tokens, w_ref[:, cols], preferred_element_type=F32)
-        keep_ref[:, cols] = jnp.where(first, part[:share], part[share:])
-        send_ref[:, cols] = jnp.where(first, part[share:], part[:share]).astype(BF16)
+    part = jnp.dot(tokens, w_ref[...], preferred_element_type=F32)
+    keep_ref[...] = jnp.where(first, part[:share], part[share:])
+    send_ref[...] = jnp.where(first, part[share:], part[:share]).astype(BF16)
 
 
 def cost(us):
@@ -409,29 +393,26 @@
     return pltpu.with_memory_space_constraint(value, pltpu.HBM)
 
 
-def merge_kernel(count, near_count, *refs):
-    kept, given, outs = refs[:count], refs[count], refs[count + 1 + near_count :]
+def merge_kernel(*refs):
+    count = len(refs) // 2
+    kept, given, outs = refs[:count], refs[count], refs[count + 1 :]
     rows = kept[0].shape[0]
     for i in range(count):
         outs[i][:rows] = kept[i][...]
         outs[i][rows:] = given[i * rows : (i + 1) * rows]
 
 
-def merge(kept, given, near, grant):
-    count, near_count = len(kept), len(near)
-    block = kept[0]
-    results = pl.pallas_call(
-        functools.partial(merge_kernel, count, near_count),
-        out_shape=[jax.ShapeDtypeStruct((2 * block.shape[0], block.shape[1]), BF16)] * count
-        + [jax.ShapeDtypeStruct(block.shape, BF16)] * near_count,
-        in_specs=[VMEM] * (count + 1) + [ANY] * near_count,
-        out_specs=[VMEM] * count + [ANY] * near_count,
-        input_output_aliases={count + 1 + i: count + i for i in range(near_count)},
+def merge(kept, given, grant):
+    rows, columns = kept[0].shape
+    return pl.pallas_call(
+        merge_kernel,
+        out_shape=[jax.ShapeDtypeStruct((2 * rows, columns), BF16)] * len(kept),
+        in_specs=[VMEM] * (len(kept) + 1),
+        out_specs=[VMEM] * len(kept),
         compiler_params=params(grant),
         cost_estimate=cost(0),
         name="merge",
-    )(*kept, given, *near)
-    return *results[:count], results[count:]
+    )(*kept, given)
 
 
 def params(mib):
@@ -455,7 +436,6 @@
     tiles, _, stretch_len, key_columns = kv_store.shape
     slot_tiles = tile_stretch.shape[1]
     ranks = slot_tiles // (slot_total * row_total)
-    width = hidden.shape[2]
     token_total = hidden.shape[1]
     query_columns = w_query.shape[1]
     key_heads = key_columns // HEAD_WIDTH
@@ -494,14 +474,11 @@
     )(in_hbm(tile_stretch), in_hbm(kv_store.reshape(store_shape)))
     own_block, kept = outgoing[len(direct)], outgoing[len(direct) + 1 :]
     given = lax.ppermute(give, "row", swap)
-    early = [True for k in direct]
-    late_blocks = [outgoing[i] for i in range(len(direct)) if not early[i]]
-    *merged, late_blocks = merge(kept, given, late_blocks, grant)
-    late_blocks = iter(late_blocks)
-    arrived = []
-    for i, k in enumerate(direct):
-        sent = outgoing[i] if early[i] else next(late_blocks)
-        arrived.append(lax.ppermute(sent, "slot", [(s, s ^ k) for s in range(slot_total)]))
+    merged = merge(kept, given, grant)
+    arrived = [
+        lax.ppermute(block, "slot", [(s, s ^ k) for s in range(slot_total)])
+        for block, k in zip(outgoing, direct)
+    ]
     arrived.append(own_block)
     for sent, pair in zip(merged, shared):
         pairs = [
@@ -570,14 +547,13 @@
     out_columns = w_out.shape[1]
     out_share = token_total // lax.axis_size("col")
     keep, send = pl.pallas_call(
-        functools.partial(output_kernel, out_columns, key_heads),
+        functools.partial(output_kernel, key_heads),
         out_shape=(
             jax.ShapeDtypeStruct((out_share, out_columns), F32),
             jax.ShapeDtypeStruct((out_share, out_columns), BF16),
         ),
         in_specs=[VMEM, VMEM, VMEM],
         out_specs=(VMEM, VMEM),
-        scratch_shapes=[pltpu.VMEM((token_total, query_columns), BF16)],
         compiler_params=params(grant),
         name="output",
     )(partial, partial_other, w_out)

time: 27 us -> 27 us (level)
  no operation moved by 1% of the time
where the time goes in v8:
time: 27 us; the launch traced here: 26.9 us
  starting transfers between devices  11.7 us (43%)
  Pallas kernels  7.23 us (27%)
  waiting for transfers between devices  4.56 us (17%)
  blocking collectives  2.5 us (9%)
  other arithmetic  0.65 us (2%)
    ppermute x3, starting transfers between devices, on_device(): lax.ppermute(block, 'slot', [(s, s ^ k) for s in range(slot_total)])  6.2 us
    ppermute x2, starting transfers between devices, on_device(): arrived.append(lax.ppermute(sent, ('slot', 'row'), pairs))  3.38 us
    ppermute x1, waiting for transfers between devices, on_device(): received = lax.ppermute(send, 'col', swap)  2.73 us
    all_gather x1, blocking collectives, on_device(): both = lax.all_gather(projected, 'row')  2.5 us
    pallas_call x1, Pallas kernels, on_device(): pl.pallas_call(functools.partial(project_kernel, step), out_shape=jax.Sha...  2.24 us
    pallas_call x1, Pallas kernels, on_device(): pl.pallas_call(functools.partial(output_kernel, key_heads), out_shape=(ja...  1.63 us
    ppermute x1, starting transfers between devices, on_device(): received = lax.ppermute(send, 'col', swap)  1.55 us
    pallas_call x1, Pallas kernels, on_device(): pl.pallas_call(functools.partial(pack_kernel, tiles, ranks, stretch_len),...  1.54 us
  transfers between devices with their start and end apart: 8, of which 3 were waited for; matrix products, arithmetic and copies ran while one was open for 0% of the time, Pallas kernels for 13%

profile of v8, /device:TPU:0, one launch (start us, length us, event | category | flops | bytes accessed | tf_op | source)
XLA Modules:
  0.0 26.9 jit_solution(13914992750822166791)
XLA Ops:
  0.0 0.0 copy-start.4
  0.0 0.0 copy-start.5
  0.0 0.0 copy-start.6
  0.0 0.0 copy-start.7
  0.0 0.0 copy-start.8
  0.0 0.0 copy-start
  0.0 0.0 copy-start.1
  0.0 0.0 copy-start.2
  0.0 0.0 copy-start.3
  0.1 1.5 %pack.1 = (bf16[64,512]{1,0:T(8,128)(2,1)S(1)}, bf16[64,512]{1,0:T(8,128)(2,1)S(1)}, bf16[64,512]{1,0:T(8,128)(2,1)S(1)}, bf16[64,512]{1,0:T(8,128)(2,1)S(1)}, b...) custom-call(s32[8,64]{1,0:T(8,128)} %stretches_ref.1, bf16[512,512]{1,0:T(8,128)(2,1)} %bitcast.11), custom_call_target="tpu_custom_call" | custom-call | flops 8000000000 | bytes 1000 | tf_op jit(solution)/shard_map/pack/pallas_call | solution.py:459
  1.6 0.5 %collective-permute-start.3 = (bf16[128,512]{1,0:T(8,128)(2,1)S(1)}, bf16[128,512]{1,0:T(8,128)(2,1)S(1)}, u32[]{:S(2)}, u32[]{:S(2)}) collective-permute-start(bf16[128,512]{1,0:T(8,128)(2,1)S(1)} %get-tuple-element.32), channel_id=1, source_target_pairs={{0,2},{2,0},{1,3},{3,1},{4,6},{6,4},{5,7},{7,5},{8,10},{10,8},{9,1... | collective-permute-start | bytes 393224 | tf_op jit(solution)/shard_map/ppermute | solution.py:476
  2.1 3.7 %collective-permute-start = (bf16[64,512]{1,0:T(8,128)(2,1)S(1)}, bf16[64,512]{1,0:T(8,128)(2,1)S(1)}, u32[]{:S(2)}, u32[]{:S(2)}) collective-permute-start(bf16[64,512]{1,0:T(8,128)(2,1)S(1)} %get-tuple-element.26), channel_id=1, source_target_pairs={{0,16},{4,20},{8,24},{12,28},{16,0},{20,4},{24,8},{28,12},{1,17},{... | collective-permute-start | bytes 196616 | tf_op jit(solution)/shard_map/ppermute | solution.py:479
  5.8 1.3 %collective-permute-start.1 = (bf16[64,512]{1,0:T(8,128)(2,1)S(1)}, bf16[64,512]{1,0:T(8,128)(2,1)S(1)}, u32[]{:S(2)}, u32[]{:S(2)}) collective-permute-start(bf16[64,512]{1,0:T(8,128)(2,1)S(1)} %get-tuple-element.27), channel_id=1, source_target_pairs={{0,24},{4,28},{8,16},{12,20},{16,8},{20,12},{24,0},{28,4},{1,25},{... | collective-permute-start | bytes 196616 | tf_op jit(solution)/shard_map/ppermute | solution.py:479
  7.1 1.2 %collective-permute-start.2 = (bf16[64,512]{1,0:T(8,128)(2,1)S(1)}, bf16[64,512]{1,0:T(8,128)(2,1)S(1)}, u32[]{:S(2)}, u32[]{:S(2)}) collective-permute-start(bf16[64,512]{1,0:T(8,128)(2,1)S(1)} %get-tuple-element.28), channel_id=1, source_target_pairs={{0,12},{4,8},{8,4},{12,0},{16,28},{20,24},{24,20},{28,16},{1,13},{... | collective-permute-start | bytes 196616 | tf_op jit(solution)/shard_map/ppermute | solution.py:479
  8.3 0.0 copy-done.4
  8.3 0.0 copy-done.5
  8.3 0.0 copy-done.6
  8.3 0.0 copy-done.7
  8.3 0.0 copy-done.8
  8.4 0.9 %tables.1 = (f32[256,128]{1,0:T(8,128)S(1)}, f32[256,128]{1,0:T(8,128)S(1)}, f32[272,128]{1,0:T(8,128)S(1)}, f32[32,128]{1,0:T(8,128)S(1)}, f32[32,128]{1,0:T(8,128)S(1)}) custom-call(s32[8,64]{1,0:T(8,128)S(1)} %copy-done.4, s32[4,128]{1,0:T(4,128)S(1)} %bitcast.10, s32[8]{0:T(128)S(1)} %copy-done.6, s32[1,32]{1,0:T(1,128)S(1)} %copy-done.7, ...), custom_call_target="tpu_custom_call" | custom-call | bytes 1000 | tf_op jit(solution)/shard_map/tables/pallas_call | solution.py:502
  9.3 0.0 collective-permute-done.3.refs_2_
  9.3 2.9 %collective-permute-start.5 = (bf16[128,512]{1,0:T(8,128)(2,1)S(1)}, bf16[128,512]{1,0:T(8,128)(2,1)S(1)}, u32[]{:S(2)}, u32[]{:S(2)}) collective-permute-start(bf16[128,512]{1,0:T(8,128)(2,1)S(1)} %get-tuple-element.34), channel_id=1, source_target_pairs={{0,28},{2,22},{4,24},{6,18},{8,20},{10,30},{12,16},{14,26},{16,12}... | collective-permute-start | bytes 393224 | tf_op jit(solution)/shard_map/ppermute | solution.py:489
  12.3 0.5 %collective-permute-start.4 = (bf16[128,512]{1,0:T(8,128)(2,1)S(1)}, bf16[128,512]{1,0:T(8,128)(2,1)S(1)}, u32[]{:S(2)}, u32[]{:S(2)}) collective-permute-start(bf16[128,512]{1,0:T(8,128)(2,1)S(1)} %get-tuple-element.33.after_ref), channel_id=1, source_target_pairs={{0,8},{2,6},{4,12},{6,2},{8,0},{10,14},{12,4},{14,10},{16,24},{18,... | collective-permute-start | bytes 393224 | tf_op jit(solution)/shard_map/ppermute | solution.py:489
  12.7 0.0 slice-start
  12.7 0.0 copy-done
  12.7 0.0 copy-done.1
  12.7 0.0 copy-done.2
  12.7 0.0 copy-done.3
  12.7 0.0 slice-start.1
  12.7 2.2 %project.1 = f32[32,3072]{1,0:T(8,128)S(1)} custom-call(bf16[128,512]{1,0:T(8,128)(2,1)S(1)} %get-tuple-element.33.after_ref, bf16[32,2048]{1,0:T(8,128)(2,1)S(1)} %bitcast.9, bf16[2048,2048]{1,0:T(8,128)(2,1)S(1)} %copy-done, bf16[2048,512]{1,0:T(8,128)(2,1)S(1)} %copy-done.1, bf16[2048,512]{1,0:T(8,128)(2,1)S(1)} %copy-done.2), custom_call_target="tpu_custom_call" | custom-call | bytes 1000 | tf_op jit(solution)/shard_map/project/pallas_call | solution.py:491
  15.0 2.5 %all-gather = f32[64,3072]{1,0:T(8,128)S(1)} all-gather(f32[32,3072]{1,0:T(8,128)S(1)} %project.1), channel_id=2, replica_groups=mesh['slot'=8,'row'=2,'col'=2] {'row'}, dimensions={0}, use_global_device_ids=true | all-gather | bytes 1179648 | tf_op jit(solution)/shard_map/all_gather | solution.py:500
  17.5 0.0 collective-permute-done.refs_0_
  17.5 0.0 collective-permute-done.1.refs_1_
  17.5 0.0 collective-permute-done.2.refs_2_
  17.5 0.3 %queries.1 = (bf16[512,128]{1,0:T(8,128)(2,1)S(1)}, f32[576,128]{1,0:T(8,128)S(1)}, bf16[16,512]{1,0:T(8,128)(2,1)S(1)}) custom-call(bf16[64,512]{1,0:T(8,128)(2,1)S(1)} %collective-permute-done.refs_0_, bf16[64,512]{1,0:T(8,128)(2,1)S(1)} %collective-permute-done.1.refs_1_, bf16[64,512]{1,0:T(8,128)(2,1)S(1)} %collective-permute-done.2.refs_2_, ...), custom_call_target="tpu_custom_call" | custom-call | bytes 1000 | tf_op jit(solution)/shard_map/queries/pallas_call | solution.py:520
  17.9 0.0 collective-permute-done.5.refs_5_
  17.9 0.5 %collective-permute-done.4.refs_4_ = bf16[128,512]{1,0:T(8,128)(2,1)S(1)} collective-permute-done((bf16[128,512]{1,0:T(8,128)(2,1)S(1)}, bf16[128,512]{1,0:T(8,128)(2,1)S(1)}, u32[]{:S(2)}, u32[]{:S(2)}) %collective-permute-start.4) | collective-permute-done | bytes 131104 | tf_op jit(solution)/shard_map/ppermute | solution.py:489
  18.3 0.5 %attend.1 = (f32[520,128]{1,0:T(8,128)S(1)}, bf16[560,128]{1,0:T(8,128)(2,1)S(1)}) custom-call(bf16[64,512]{1,0:T(8,128)(2,1)S(1)} %collective-permute-done.refs_0_, bf16[64,512]{1,0:T(8,128)(2,1)S(1)} %collective-permute-done.1.refs_1_, bf16[64,512]{1,0:T(8,128)(2,1)S(1)} %collective-permute-done.2.refs_2_, bf16[64,512]{1,0:T(8,128)(2,1)S(1)} %get-tuple-element.29.refs_3_, ...), custom_call_target="tpu_custom_call" | custom-call | bytes 1000 | tf_op jit(solution)/shard_map/attend/pallas_call | solution.py:533
  18.9 0.1 collective-permute-start.6
  18.9 1.4 %collective-permute-done.6.other_ref = bf16[560,128]{1,0:T(8,128)(2,1)S(1)} collective-permute-done((bf16[560,128]{1,0:T(8,128)(2,1)S(1)}, bf16[560,128]{1,0:T(8,128)(2,1)S(1)}, u32[]{:S(2)}, u32[]{:S(2)}) %collective-permute-start.6) | collective-permute-done | bytes 143392 | tf_op jit(solution)/shard_map/ppermute | solution.py:545
  20.3 0.0 slice-done
  20.3 0.0 slice-done.1
  20.3 1.6 %output.1 = (f32[16,2048]{1,0:T(8,128)S(1)}, bf16[16,2048]{1,0:T(8,128)(2,1)S(1)}) custom-call(f32[520,128]{1,0:T(8,128)S(1)} %get-tuple-element.43.own_ref, bf16[560,128]{1,0:T(8,128)(2,1)S(1)} %collective-permute-done.6.other_ref, bf16[2048,2048]{1,0:T(8,128)(2,1)S(1)} %bitcast.7), custom_call_target="tpu_custom_call" | custom-call | tf_op jit(solution)/shard_map/output/pallas_call | solution.py:549
  21.9 1.5 %collective-permute-start.7 = (bf16[16,2048]{1,0:T(8,128)(2,1)S(1)}, bf16[16,2048]{1,0:T(8,128)(2,1)S(1)}, u32[]{:S(2)}, u32[]{:S(2)}) collective-permute-start(bf16[16,2048]{1,0:T(8,128)(2,1)S(1)} %get-tuple-element.46), channel_id=1, source_target_pairs={{0,1},{1,0},{2,3},{3,2},{4,5},{5,4},{6,7},{7,6},{8,9},{9,8},{10,11... | collective-permute-start | bytes 196616 | tf_op jit(solution)/shard_map/ppermute | solution.py:560
  23.5 2.7 %collective-permute-done.7 = bf16[16,2048]{1,0:T(8,128)(2,1)S(1)} collective-permute-done((bf16[16,2048]{1,0:T(8,128)(2,1)S(1)}, bf16[16,2048]{1,0:T(8,128)(2,1)S(1)}, u32[]{:S(2)}, u32[]{:S(2)}) %collective-permute-start.7) | collective-permute-done | bytes 65568 | tf_op jit(solution)/shard_map/ppermute | solution.py:560
  26.2 0.6 %fusion = bf16[1,16,2048]{2,1,0:T(8,128)(2,1)} fusion(f32[16,2048]{1,0:T(8,128)S(1)} %get-tuple-element.45, bf16[16,2048]{1,0:T(8,128)(2,1)S(1)} %collective-permute-done.7), kind=kLoop, calls=%fused_computation.1 | loop fusion | flops 98304 | bytes 262144 | tf_op jit(solution)/shard_map/broadcast_in_dim | solution.py:561
  (2 shorter events, 0.0 us)
Async XLA Ops:
  0.0 8.3 %copy-start.4 = (s32[8,64]{1,0:T(8,128)S(1)}, s32[8,64]{1,0:T(8,128)}, u32[]{:S(2)}) copy-start(s32[8,64]{1,0:T(8,128)} %stretches_ref.1) | copy-start | bytes 6148
  0.0 8.3 %copy-start.5 = (s32[512]{0:T(512)S(1)}, s32[512]{0:T(512)}, u32[]{:S(2)}) copy-start(s32[512]{0:T(512)} %param.17) | copy-start | bytes 6148
  0.0 8.3 %copy-start.6 = (s32[8]{0:T(128)S(1)}, s32[8]{0:T(128)}, u32[]{:S(2)}) copy-start(s32[8]{0:T(128)} %counts_ref.1) | copy-start | bytes 100
  0.0 8.3 %copy-start.7 = (s32[1,32]{1,0:T(1,128)S(1)}, s32[1,32]{1,0:T(1,128)}, u32[]{:S(2)}) copy-start(s32[1,32]{1,0:T(1,128)} %positions_ref.1) | copy-start | bytes 388
  0.0 8.3 %copy-start.8 = (f32[1,128]{1,0:T(1,128)S(1)}, f32[1,128]{1,0:T(1,128)}, u32[]{:S(2)}) copy-start(f32[1,128]{1,0:T(1,128)} %constant.2.clone.freq_ref) | copy-start | bytes 1540
  0.0 12.7 %copy-start = (bf16[2048,2048]{1,0:T(8,128)(2,1)S(1)}, bf16[2048,2048]{1,0:T(8,128)(2,1)}, u32[]{:S(2)}) copy-start(bf16[2048,2048]{1,0:T(8,128)(2,1)} %wq_ref.1) | copy-start | bytes 25165828
  0.0 12.7 %copy-start.1 = (bf16[2048,512]{1,0:T(8,128)(2,1)S(1)}, bf16[2048,512]{1,0:T(8,128)(2,1)}, u32[]{:S(2)}) copy-start(bf16[2048,512]{1,0:T(8,128)(2,1)} %wk_ref.1) | copy-start | bytes 6291460
  0.0 12.7 %copy-start.2 = (bf16[2048,512]{1,0:T(8,128)(2,1)S(1)}, bf16[2048,512]{1,0:T(8,128)(2,1)}, u32[]{:S(2)}) copy-start(bf16[2048,512]{1,0:T(8,128)(2,1)} %wv_ref.1) | copy-start | bytes 6291460
  0.0 12.7 %copy-start.3 = (bf16[1,32,2048]{2,1,0:T(8,128)(2,1)S(1)}, bf16[1,32,2048]{2,1,0:T(8,128)(2,1)}, u32[]{:S(2)}) copy-start(bf16[1,32,2048]{2,1,0:T(8,128)(2,1)} %param.11) | copy-start | bytes 393220
  1.6 7.7 %collective-permute-start.3 = (bf16[128,512]{1,0:T(8,128)(2,1)S(1)}, bf16[128,512]{1,0:T(8,128)(2,1)S(1)}, u32[]{:S(2)}, u32[]{:S(2)}) collective-permute-start(bf16[128,512]{1,0:T(8,128)(2,1)S(1)} %get-tuple-element.32), channel_id=1, source_target_pairs={{0,2},{2,0},{1,3},{3,1},{4,6},{6,4},{5,7},{7,5},{8,10},{10,8},{9,1... | collective-permute-start | bytes 393224 | tf_op jit(solution)/shard_map/ppermute | solution.py:476
  2.1 15.4 %collective-permute-start = (bf16[64,512]{1,0:T(8,128)(2,1)S(1)}, bf16[64,512]{1,0:T(8,128)(2,1)S(1)}, u32[]{:S(2)}, u32[]{:S(2)}) collective-permute-start(bf16[64,512]{1,0:T(8,128)(2,1)S(1)} %get-tuple-element.26), channel_id=1, source_target_pairs={{0,16},{4,20},{8,24},{12,28},{16,0},{20,4},{24,8},{28,12},{1,17},{... | collective-permute-start | bytes 196616 | tf_op jit(solution)/shard_map/ppermute | solution.py:479
  5.8 11.7 %collective-permute-start.1 = (bf16[64,512]{1,0:T(8,128)(2,1)S(1)}, bf16[64,512]{1,0:T(8,128)(2,1)S(1)}, u32[]{:S(2)}, u32[]{:S(2)}) collective-permute-start(bf16[64,512]{1,0:T(8,128)(2,1)S(1)} %get-tuple-element.27), channel_id=1, source_target_pairs={{0,24},{4,28},{8,16},{12,20},{16,8},{20,12},{24,0},{28,4},{1,25},{... | collective-permute-start | bytes 196616 | tf_op jit(solution)/shard_map/ppermute | solution.py:479
  7.1 10.4 %collective-permute-start.2 = (bf16[64,512]{1,0:T(8,128)(2,1)S(1)}, bf16[64,512]{1,0:T(8,128)(2,1)S(1)}, u32[]{:S(2)}, u32[]{:S(2)}) collective-permute-start(bf16[64,512]{1,0:T(8,128)(2,1)S(1)} %get-tuple-element.28), channel_id=1, source_target_pairs={{0,12},{4,8},{8,4},{12,0},{16,28},{20,24},{24,20},{28,16},{1,13},{... | collective-permute-start | bytes 196616 | tf_op jit(solution)/shard_map/ppermute | solution.py:479
  9.3 8.5 %collective-permute-start.5 = (bf16[128,512]{1,0:T(8,128)(2,1)S(1)}, bf16[128,512]{1,0:T(8,128)(2,1)S(1)}, u32[]{:S(2)}, u32[]{:S(2)}) collective-permute-start(bf16[128,512]{1,0:T(8,128)(2,1)S(1)} %get-tuple-element.34), channel_id=1, source_target_pairs={{0,28},{2,22},{4,24},{6,18},{8,20},{10,30},{12,16},{14,26},{16,12}... | collective-permute-start | bytes 393224 | tf_op jit(solution)/shard_map/ppermute | solution.py:489
  12.3 6.1 %collective-permute-start.4 = (bf16[128,512]{1,0:T(8,128)(2,1)S(1)}, bf16[128,512]{1,0:T(8,128)(2,1)S(1)}, u32[]{:S(2)}, u32[]{:S(2)}) collective-permute-start(bf16[128,512]{1,0:T(8,128)(2,1)S(1)} %get-tuple-element.33.after_ref), channel_id=1, source_target_pairs={{0,8},{2,6},{4,12},{6,2},{8,0},{10,14},{12,4},{14,10},{16,24},{18,... | collective-permute-start | bytes 393224 | tf_op jit(solution)/shard_map/ppermute | solution.py:489
  12.7 7.6 %slice-start = ((s8[8388608]{0:T(1024)(128)(4,1)}), s8[4194304]{0:T(1024)(128)(4,1)S(1)}, s32[]{:S(2)}) async-start(s8[8388608]{0:T(1024)(128)(4,1)} %bitcast.6), calls=%async_computation | async-start | bytes 8388608
  12.7 7.6 %slice-start.1 = ((s8[8388608]{0:T(1024)(128)(4,1)}), s8[4194304]{0:T(1024)(128)(4,1)S(1)}, s32[]{:S(2)}) async-start(s8[8388608]{0:T(1024)(128)(4,1)} %bitcast.6), calls=%async_computation.1 | async-start | bytes 8388608
  18.9 1.4 %collective-permute-start.6 = (bf16[560,128]{1,0:T(8,128)(2,1)S(1)}, bf16[560,128]{1,0:T(8,128)(2,1)S(1)}, u32[]{:S(2)}, u32[]{:S(2)}) collective-permute-start(bf16[560,128]{1,0:T(8,128)(2,1)S(1)} %get-tuple-element.44), channel_id=1, source_target_pairs={{0,2},{2,0},{1,3},{3,1},{4,6},{6,4},{5,7},{7,5},{8,10},{10,8},{9,1... | collective-permute-start | bytes 430088 | tf_op jit(solution)/shard_map/ppermute | solution.py:545
  21.9 4.3 %collective-permute-start.7 = (bf16[16,2048]{1,0:T(8,128)(2,1)S(1)}, bf16[16,2048]{1,0:T(8,128)(2,1)S(1)}, u32[]{:S(2)}, u32[]{:S(2)}) collective-permute-start(bf16[16,2048]{1,0:T(8,128)(2,1)S(1)} %get-tuple-element.46), channel_id=1, source_target_pairs={{0,1},{1,0},{2,3},{3,2},{4,5},{5,4},{6,7},{7,6},{8,9},{9,8},{10,11... | collective-permute-start | bytes 196616 | tf_op jit(solution)/shard_map/ppermute | solution.py:560

commit v9 on v8

--- a/solution.py
+++ b/solution.py
@@ -60,8 +60,8 @@
     *outs, give_ref, stretches_ref, store_ref, ids_ref, sems = refs
     get_store = pltpu.make_async_copy(store_hbm, store_ref, sems.at[0])
     get_stretches = pltpu.make_async_copy(stretches_hbm, stretches_ref, sems.at[1])
-    get_stretches.start()
-    get_store.start()
+    get_stretches.start(priority=1)
+    get_store.start(priority=1)
     slot = lax.axis_index("slot")
     row = lax.axis_index("row")
     own = slot * lax.axis_size("row") + row

time: 27 us -> 27 us (level)
  no operation moved by 1% of the time
where the time goes in v9:
time: 27 us; the launch traced here: 26.9 us
  starting transfers between devices  11.7 us (43%)
  Pallas kernels  7.23 us (27%)
  waiting for transfers between devices  4.56 us (17%)
  blocking collectives  2.5 us (9%)
  other arithmetic  0.65 us (2%)
    ppermute x3, starting transfers between devices, on_device(): lax.ppermute(block, 'slot', [(s, s ^ k) for s in range(slot_total)])  6.2 us
    ppermute x2, starting transfers between devices, on_device(): arrived.append(lax.ppermute(sent, ('slot', 'row'), pairs))  3.38 us
    ppermute x1, waiting for transfers between devices, on_device(): received = lax.ppermute(send, 'col', swap)  2.73 us
    all_gather x1, blocking collectives, on_device(): both = lax.all_gather(projected, 'row')  2.5 us
    pallas_call x1, Pallas kernels, on_device(): pl.pallas_call(functools.partial(project_kernel, step), out_shape=jax.Sha...  2.24 us
    pallas_call x1, Pallas kernels, on_device(): pl.pallas_call(functools.partial(output_kernel, key_heads), out_shape=(ja...  1.63 us
    ppermute x1, starting transfers between devices, on_device(): received = lax.ppermute(send, 'col', swap)  1.55 us
    pallas_call x1, Pallas kernels, on_device(): pl.pallas_call(functools.partial(pack_kernel, tiles, ranks, stretch_len),...  1.54 us
  transfers between devices with their start and end apart: 8, of which 3 were waited for; matrix products, arithmetic and copies ran while one was open for 0% of the time, Pallas kernels for 13%

profile of v9, /device:TPU:0, one launch (start us, length us, event | category | flops | bytes accessed | tf_op | source)
XLA Modules:
  0.0 26.9 jit_solution(3053471398110653700)
XLA Ops:
  0.0 0.0 copy-start.4
  0.0 0.0 copy-start.5
  0.0 0.0 copy-start.6
  0.0 0.0 copy-start.7
  0.0 0.0 copy-start.8
  0.0 0.0 copy-start
  0.0 0.0 copy-start.1
  0.0 0.0 copy-start.2
  0.0 0.0 copy-start.3
  0.1 1.5 %pack.1 = (bf16[64,512]{1,0:T(8,128)(2,1)S(1)}, bf16[64,512]{1,0:T(8,128)(2,1)S(1)}, bf16[64,512]{1,0:T(8,128)(2,1)S(1)}, bf16[64,512]{1,0:T(8,128)(2,1)S(1)}, b...) custom-call(s32[8,64]{1,0:T(8,128)} %stretches_ref.1, bf16[512,512]{1,0:T(8,128)(2,1)} %bitcast.11), custom_call_target="tpu_custom_call" | custom-call | flops 8000000000 | bytes 1000 | tf_op jit(solution)/shard_map/pack/pallas_call | solution.py:459
  1.6 0.5 %collective-permute-start.3 = (bf16[128,512]{1,0:T(8,128)(2,1)S(1)}, bf16[128,512]{1,0:T(8,128)(2,1)S(1)}, u32[]{:S(2)}, u32[]{:S(2)}) collective-permute-start(bf16[128,512]{1,0:T(8,128)(2,1)S(1)} %get-tuple-element.32), channel_id=1, source_target_pairs={{0,2},{2,0},{1,3},{3,1},{4,6},{6,4},{5,7},{7,5},{8,10},{10,8},{9,1... | collective-permute-start | bytes 393224 | tf_op jit(solution)/shard_map/ppermute | solution.py:476
  2.1 3.7 %collective-permute-start = (bf16[64,512]{1,0:T(8,128)(2,1)S(1)}, bf16[64,512]{1,0:T(8,128)(2,1)S(1)}, u32[]{:S(2)}, u32[]{:S(2)}) collective-permute-start(bf16[64,512]{1,0:T(8,128)(2,1)S(1)} %get-tuple-element.26), channel_id=1, source_target_pairs={{0,16},{4,20},{8,24},{12,28},{16,0},{20,4},{24,8},{28,12},{1,17},{... | collective-permute-start | bytes 196616 | tf_op jit(solution)/shard_map/ppermute | solution.py:479
  5.8 1.3 %collective-permute-start.1 = (bf16[64,512]{1,0:T(8,128)(2,1)S(1)}, bf16[64,512]{1,0:T(8,128)(2,1)S(1)}, u32[]{:S(2)}, u32[]{:S(2)}) collective-permute-start(bf16[64,512]{1,0:T(8,128)(2,1)S(1)} %get-tuple-element.27), channel_id=1, source_target_pairs={{0,24},{4,28},{8,16},{12,20},{16,8},{20,12},{24,0},{28,4},{1,25},{... | collective-permute-start | bytes 196616 | tf_op jit(solution)/shard_map/ppermute | solution.py:479
  7.1 1.2 %collective-permute-start.2 = (bf16[64,512]{1,0:T(8,128)(2,1)S(1)}, bf16[64,512]{1,0:T(8,128)(2,1)S(1)}, u32[]{:S(2)}, u32[]{:S(2)}) collective-permute-start(bf16[64,512]{1,0:T(8,128)(2,1)S(1)} %get-tuple-element.28), channel_id=1, source_target_pairs={{0,12},{4,8},{8,4},{12,0},{16,28},{20,24},{24,20},{28,16},{1,13},{... | collective-permute-start | bytes 196616 | tf_op jit(solution)/shard_map/ppermute | solution.py:479
  8.3 0.0 copy-done.4
  8.3 0.0 copy-done.5
  8.3 0.0 copy-done.6
  8.3 0.0 copy-done.7
  8.3 0.0 copy-done.8
  8.4 0.9 %tables.1 = (f32[256,128]{1,0:T(8,128)S(1)}, f32[256,128]{1,0:T(8,128)S(1)}, f32[272,128]{1,0:T(8,128)S(1)}, f32[32,128]{1,0:T(8,128)S(1)}, f32[32,128]{1,0:T(8,128)S(1)}) custom-call(s32[8,64]{1,0:T(8,128)S(1)} %copy-done.4, s32[4,128]{1,0:T(4,128)S(1)} %bitcast.10, s32[8]{0:T(128)S(1)} %copy-done.6, s32[1,32]{1,0:T(1,128)S(1)} %copy-done.7, ...), custom_call_target="tpu_custom_call" | custom-call | bytes 1000 | tf_op jit(solution)/shard_map/tables/pallas_call | solution.py:502
  9.3 0.0 collective-permute-done.3.refs_2_
  9.3 2.9 %collective-permute-start.5 = (bf16[128,512]{1,0:T(8,128)(2,1)S(1)}, bf16[128,512]{1,0:T(8,128)(2,1)S(1)}, u32[]{:S(2)}, u32[]{:S(2)}) collective-permute-start(bf16[128,512]{1,0:T(8,128)(2,1)S(1)} %get-tuple-element.34), channel_id=1, source_target_pairs={{0,28},{2,22},{4,24},{6,18},{8,20},{10,30},{12,16},{14,26},{16,12}... | collective-permute-start | bytes 393224 | tf_op jit(solution)/shard_map/ppermute | solution.py:489
  12.3 0.5 %collective-permute-start.4 = (bf16[128,512]{1,0:T(8,128)(2,1)S(1)}, bf16[128,512]{1,0:T(8,128)(2,1)S(1)}, u32[]{:S(2)}, u32[]{:S(2)}) collective-permute-start(bf16[128,512]{1,0:T(8,128)(2,1)S(1)} %get-tuple-element.33.after_ref), channel_id=1, source_target_pairs={{0,8},{2,6},{4,12},{6,2},{8,0},{10,14},{12,4},{14,10},{16,24},{18,... | collective-permute-start | bytes 393224 | tf_op jit(solution)/shard_map/ppermute | solution.py:489
  12.7 0.0 slice-start
  12.7 0.0 copy-done
  12.7 0.0 copy-done.1
  12.7 0.0 copy-done.2
  12.7 0.0 copy-done.3
  12.7 0.0 slice-start.1
  12.7 2.2 %project.1 = f32[32,3072]{1,0:T(8,128)S(1)} custom-call(bf16[128,512]{1,0:T(8,128)(2,1)S(1)} %get-tuple-element.33.after_ref, bf16[32,2048]{1,0:T(8,128)(2,1)S(1)} %bitcast.9, bf16[2048,2048]{1,0:T(8,128)(2,1)S(1)} %copy-done, bf16[2048,512]{1,0:T(8,128)(2,1)S(1)} %copy-done.1, bf16[2048,512]{1,0:T(8,128)(2,1)S(1)} %copy-done.2), custom_call_target="tpu_custom_call" | custom-call | bytes 1000 | tf_op jit(solution)/shard_map/project/pallas_call | solution.py:491
  15.0 2.5 %all-gather = f32[64,3072]{1,0:T(8,128)S(1)} all-gather(f32[32,3072]{1,0:T(8,128)S(1)} %project.1), channel_id=2, replica_groups=mesh['slot'=8,'row'=2,'col'=2] {'row'}, dimensions={0}, use_global_device_ids=true | all-gather | bytes 1179648 | tf_op jit(solution)/shard_map/all_gather | solution.py:500
  17.5 0.0 collective-permute-done.refs_0_
  17.5 0.0 collective-permute-done.1.refs_1_
  17.5 0.0 collective-permute-done.2.refs_2_
  17.5 0.3 %queries.1 = (bf16[512,128]{1,0:T(8,128)(2,1)S(1)}, f32[576,128]{1,0:T(8,128)S(1)}, bf16[16,512]{1,0:T(8,128)(2,1)S(1)}) custom-call(bf16[64,512]{1,0:T(8,128)(2,1)S(1)} %collective-permute-done.refs_0_, bf16[64,512]{1,0:T(8,128)(2,1)S(1)} %collective-permute-done.1.refs_1_, bf16[64,512]{1,0:T(8,128)(2,1)S(1)} %collective-permute-done.2.refs_2_, ...), custom_call_target="tpu_custom_call" | custom-call | bytes 1000 | tf_op jit(solution)/shard_map/queries/pallas_call | solution.py:520
  17.9 0.0 collective-permute-done.5.refs_5_
  17.9 0.5 %collective-permute-done.4.refs_4_ = bf16[128,512]{1,0:T(8,128)(2,1)S(1)} collective-permute-done((bf16[128,512]{1,0:T(8,128)(2,1)S(1)}, bf16[128,512]{1,0:T(8,128)(2,1)S(1)}, u32[]{:S(2)}, u32[]{:S(2)}) %collective-permute-start.4) | collective-permute-done | bytes 131104 | tf_op jit(solution)/shard_map/ppermute | solution.py:489
  18.3 0.5 %attend.1 = (f32[520,128]{1,0:T(8,128)S(1)}, bf16[560,128]{1,0:T(8,128)(2,1)S(1)}) custom-call(bf16[64,512]{1,0:T(8,128)(2,1)S(1)} %collective-permute-done.refs_0_, bf16[64,512]{1,0:T(8,128)(2,1)S(1)} %collective-permute-done.1.refs_1_, bf16[64,512]{1,0:T(8,128)(2,1)S(1)} %collective-permute-done.2.refs_2_, bf16[64,512]{1,0:T(8,128)(2,1)S(1)} %get-tuple-element.29.refs_3_, ...), custom_call_target="tpu_custom_call" | custom-call | bytes 1000 | tf_op jit(solution)/shard_map/attend/pallas_call | solution.py:533
  18.9 0.1 collective-permute-start.6
  18.9 1.4 %collective-permute-done.6.other_ref = bf16[560,128]{1,0:T(8,128)(2,1)S(1)} collective-permute-done((bf16[560,128]{1,0:T(8,128)(2,1)S(1)}, bf16[560,128]{1,0:T(8,128)(2,1)S(1)}, u32[]{:S(2)}, u32[]{:S(2)}) %collective-permute-start.6) | collective-permute-done | bytes 143392 | tf_op jit(solution)/shard_map/ppermute | solution.py:545
  20.3 0.0 slice-done
  20.3 0.0 slice-done.1
  20.3 1.6 %output.1 = (f32[16,2048]{1,0:T(8,128)S(1)}, bf16[16,2048]{1,0:T(8,128)(2,1)S(1)}) custom-call(f32[520,128]{1,0:T(8,128)S(1)} %get-tuple-element.43.own_ref, bf16[560,128]{1,0:T(8,128)(2,1)S(1)} %collective-permute-done.6.other_ref, bf16[2048,2048]{1,0:T(8,128)(2,1)S(1)} %bitcast.7), custom_call_target="tpu_custom_call" | custom-call | tf_op jit(solution)/shard_map/output/pallas_call | solution.py:549
  21.9 1.5 %collective-permute-start.7 = (bf16[16,2048]{1,0:T(8,128)(2,1)S(1)}, bf16[16,2048]{1,0:T(8,128)(2,1)S(1)}, u32[]{:S(2)}, u32[]{:S(2)}) collective-permute-start(bf16[16,2048]{1,0:T(8,128)(2,1)S(1)} %get-tuple-element.46), channel_id=1, source_target_pairs={{0,1},{1,0},{2,3},{3,2},{4,5},{5,4},{6,7},{7,6},{8,9},{9,8},{10,11... | collective-permute-start | bytes 196616 | tf_op jit(solution)/shard_map/ppermute | solution.py:560
  23.5 2.7 %collective-permute-done.7 = bf16[16,2048]{1,0:T(8,128)(2,1)S(1)} collective-permute-done((bf16[16,2048]{1,0:T(8,128)(2,1)S(1)}, bf16[16,2048]{1,0:T(8,128)(2,1)S(1)}, u32[]{:S(2)}, u32[]{:S(2)}) %collective-permute-start.7) | collective-permute-done | bytes 65568 | tf_op jit(solution)/shard_map/ppermute | solution.py:560
  26.2 0.6 %fusion = bf16[1,16,2048]{2,1,0:T(8,128)(2,1)} fusion(f32[16,2048]{1,0:T(8,128)S(1)} %get-tuple-element.45, bf16[16,2048]{1,0:T(8,128)(2,1)S(1)} %collective-permute-done.7), kind=kLoop, calls=%fused_computation.1 | loop fusion | flops 98304 | bytes 262144 | tf_op jit(solution)/shard_map/broadcast_in_dim | solution.py:561
  (2 shorter events, 0.0 us)
Async XLA Ops:
  0.0 8.3 %copy-start.4 = (s32[8,64]{1,0:T(8,128)S(1)}, s32[8,64]{1,0:T(8,128)}, u32[]{:S(2)}) copy-start(s32[8,64]{1,0:T(8,128)} %stretches_ref.1) | copy-start | bytes 6148
  0.0 8.3 %copy-start.5 = (s32[512]{0:T(512)S(1)}, s32[512]{0:T(512)}, u32[]{:S(2)}) copy-start(s32[512]{0:T(512)} %param.17) | copy-start | bytes 6148
  0.0 8.3 %copy-start.6 = (s32[8]{0:T(128)S(1)}, s32[8]{0:T(128)}, u32[]{:S(2)}) copy-start(s32[8]{0:T(128)} %counts_ref.1) | copy-start | bytes 100
  0.0 8.3 %copy-start.7 = (s32[1,32]{1,0:T(1,128)S(1)}, s32[1,32]{1,0:T(1,128)}, u32[]{:S(2)}) copy-start(s32[1,32]{1,0:T(1,128)} %positions_ref.1) | copy-start | bytes 388
  0.0 8.3 %copy-start.8 = (f32[1,128]{1,0:T(1,128)S(1)}, f32[1,128]{1,0:T(1,128)}, u32[]{:S(2)}) copy-start(f32[1,128]{1,0:T(1,128)} %constant.2.clone.freq_ref) | copy-start | bytes 1540
  0.0 12.7 %copy-start = (bf16[2048,2048]{1,0:T(8,128)(2,1)S(1)}, bf16[2048,2048]{1,0:T(8,128)(2,1)}, u32[]{:S(2)}) copy-start(bf16[2048,2048]{1,0:T(8,128)(2,1)} %wq_ref.1) | copy-start | bytes 25165828
  0.0 12.7 %copy-start.1 = (bf16[2048,512]{1,0:T(8,128)(2,1)S(1)}, bf16[2048,512]{1,0:T(8,128)(2,1)}, u32[]{:S(2)}) copy-start(bf16[2048,512]{1,0:T(8,128)(2,1)} %wk_ref.1) | copy-start | bytes 6291460
  0.0 12.7 %copy-start.2 = (bf16[2048,512]{1,0:T(8,128)(2,1)S(1)}, bf16[2048,512]{1,0:T(8,128)(2,1)}, u32[]{:S(2)}) copy-start(bf16[2048,512]{1,0:T(8,128)(2,1)} %wv_ref.1) | copy-start | bytes 6291460
  0.0 12.7 %copy-start.3 = (bf16[1,32,2048]{2,1,0:T(8,128)(2,1)S(1)}, bf16[1,32,2048]{2,1,0:T(8,128)(2,1)}, u32[]{:S(2)}) copy-start(bf16[1,32,2048]{2,1,0:T(8,128)(2,1)} %param.11) | copy-start | bytes 393220
  1.6 7.7 %collective-permute-start.3 = (bf16[128,512]{1,0:T(8,128)(2,1)S(1)}, bf16[128,512]{1,0:T(8,128)(2,1)S(1)}, u32[]{:S(2)}, u32[]{:S(2)}) collective-permute-start(bf16[128,512]{1,0:T(8,128)(2,1)S(1)} %get-tuple-element.32), channel_id=1, source_target_pairs={{0,2},{2,0},{1,3},{3,1},{4,6},{6,4},{5,7},{7,5},{8,10},{10,8},{9,1... | collective-permute-start | bytes 393224 | tf_op jit(solution)/shard_map/ppermute | solution.py:476
  2.1 15.4 %collective-permute-start = (bf16[64,512]{1,0:T(8,128)(2,1)S(1)}, bf16[64,512]{1,0:T(8,128)(2,1)S(1)}, u32[]{:S(2)}, u32[]{:S(2)}) collective-permute-start(bf16[64,512]{1,0:T(8,128)(2,1)S(1)} %get-tuple-element.26), channel_id=1, source_target_pairs={{0,16},{4,20},{8,24},{12,28},{16,0},{20,4},{24,8},{28,12},{1,17},{... | collective-permute-start | bytes 196616 | tf_op jit(solution)/shard_map/ppermute | solution.py:479
  5.8 11.7 %collective-permute-start.1 = (bf16[64,512]{1,0:T(8,128)(2,1)S(1)}, bf16[64,512]{1,0:T(8,128)(2,1)S(1)}, u32[]{:S(2)}, u32[]{:S(2)}) collective-permute-start(bf16[64,512]{1,0:T(8,128)(2,1)S(1)} %get-tuple-element.27), channel_id=1, source_target_pairs={{0,24},{4,28},{8,16},{12,20},{16,8},{20,12},{24,0},{28,4},{1,25},{... | collective-permute-start | bytes 196616 | tf_op jit(solution)/shard_map/ppermute | solution.py:479
  7.1 10.4 %collective-permute-start.2 = (bf16[64,512]{1,0:T(8,128)(2,1)S(1)}, bf16[64,512]{1,0:T(8,128)(2,1)S(1)}, u32[]{:S(2)}, u32[]{:S(2)}) collective-permute-start(bf16[64,512]{1,0:T(8,128)(2,1)S(1)} %get-tuple-element.28), channel_id=1, source_target_pairs={{0,12},{4,8},{8,4},{12,0},{16,28},{20,24},{24,20},{28,16},{1,13},{... | collective-permute-start | bytes 196616 | tf_op jit(solution)/shard_map/ppermute | solution.py:479
  9.3 8.5 %collective-permute-start.5 = (bf16[128,512]{1,0:T(8,128)(2,1)S(1)}, bf16[128,512]{1,0:T(8,128)(2,1)S(1)}, u32[]{:S(2)}, u32[]{:S(2)}) collective-permute-start(bf16[128,512]{1,0:T(8,128)(2,1)S(1)} %get-tuple-element.34), channel_id=1, source_target_pairs={{0,28},{2,22},{4,24},{6,18},{8,20},{10,30},{12,16},{14,26},{16,12}... | collective-permute-start | bytes 393224 | tf_op jit(solution)/shard_map/ppermute | solution.py:489
  12.3 6.1 %collective-permute-start.4 = (bf16[128,512]{1,0:T(8,128)(2,1)S(1)}, bf16[128,512]{1,0:T(8,128)(2,1)S(1)}, u32[]{:S(2)}, u32[]{:S(2)}) collective-permute-start(bf16[128,512]{1,0:T(8,128)(2,1)S(1)} %get-tuple-element.33.after_ref), channel_id=1, source_target_pairs={{0,8},{2,6},{4,12},{6,2},{8,0},{10,14},{12,4},{14,10},{16,24},{18,... | collective-permute-start | bytes 393224 | tf_op jit(solution)/shard_map/ppermute | solution.py:489
  12.7 7.6 %slice-start = ((s8[8388608]{0:T(1024)(128)(4,1)}), s8[4194304]{0:T(1024)(128)(4,1)S(1)}, s32[]{:S(2)}) async-start(s8[8388608]{0:T(1024)(128)(4,1)} %bitcast.6), calls=%async_computation | async-start | bytes 8388608
  12.7 7.6 %slice-start.1 = ((s8[8388608]{0:T(1024)(128)(4,1)}), s8[4194304]{0:T(1024)(128)(4,1)S(1)}, s32[]{:S(2)}) async-start(s8[8388608]{0:T(1024)(128)(4,1)} %bitcast.6), calls=%async_computation.1 | async-start | bytes 8388608
  18.9 1.4 %collective-permute-start.6 = (bf16[560,128]{1,0:T(8,128)(2,1)S(1)}, bf16[560,128]{1,0:T(8,128)(2,1)S(1)}, u32[]{:S(2)}, u32[]{:S(2)}) collective-permute-start(bf16[560,128]{1,0:T(8,128)(2,1)S(1)} %get-tuple-element.44), channel_id=1, source_target_pairs={{0,2},{2,0},{1,3},{3,1},{4,6},{6,4},{5,7},{7,5},{8,10},{10,8},{9,1... | collective-permute-start | bytes 430088 | tf_op jit(solution)/shard_map/ppermute | solution.py:545
  21.9 4.3 %collective-permute-start.7 = (bf16[16,2048]{1,0:T(8,128)(2,1)S(1)}, bf16[16,2048]{1,0:T(8,128)(2,1)S(1)}, u32[]{:S(2)}, u32[]{:S(2)}) collective-permute-start(bf16[16,2048]{1,0:T(8,128)(2,1)S(1)} %get-tuple-element.46), channel_id=1, source_target_pairs={{0,1},{1,0},{2,3},{3,2},{4,5},{5,4},{6,7},{7,6},{8,9},{9,8},{10,11... | collective-permute-start | bytes 196616 | tf_op jit(solution)/shard_map/ppermute | solution.py:560
